TPU v7x, 256 devices: a whole 4x4x8 slice. The times are simulated.
256 devices in a mesh: pipe: 16 (over x, z_hi), tensor: 16 (over y, z_lo, core).
Axes of the slice: x: 4, y: 4, z: 8 (z_hi: 4, z_lo: 2; z = z_hi * 2 + z_lo), core: 2. Of those that a mesh axis runs over, the one named last changes fastest.
Arguments:
- section_weights: bfloat16 [16, 2, 4096, 4096], P('pipe', None, 'tensor'), may hold values from -0.09375 to 0.09375
- context: bfloat16 [16, 2, 768, 4096], P('pipe', None, None, 'tensor'), may hold values from -3 to 3
- grad_out: bfloat16 [16, 2, 768, 4096], P('pipe', None, 'tensor'), may hold values from -3 to 3
Outputs:
- weight_grad: bfloat16 [16, 4096, 4096], P('pipe', 'tensor')
- input_grad: bfloat16 [16, 2, 768, 4096], P('pipe', None, None, 'tensor')
All inputs are finite; a program needn't handle non-finite values.
Results may differ from a plain program's by a relative error of at most 0.001.
Values may be sent and summed in bfloat16 or wider, within the bound.
No kernel may reach another device: no remote copies, remote signals or barrier semaphores. Data moves between devices by JAX's collectives and lax.ppermute only.
A program may use at most 128 MiB of HBM per device.

v0:
```python
import jax
import jax.numpy as jnp
from jax import lax
from jax.sharding import PartitionSpec as P


def from_behind(value, axis, by):
    count = lax.axis_size(axis)
    pairs = [(i, i + by) for i in range(count) if 0 <= i + by < count]
    return lax.ppermute(value, axis, pairs)


def shards(section_weights, context, grad_out):
    width_in = context.shape[3]
    width_out = grad_out.shape[3]
    owned = 2
    piece = lax.all_gather(grad_out, "tensor", axis=2, tiled=True)
    context_rows = context[0, :owned]
    weight_sum = jnp.einsum(
        "rtd,rto->rdo", context_rows, piece[0, :owned], preferred_element_type=jnp.float32
    )
    product = jnp.einsum(
        "rto,rdo->rtd", piece[0], section_weights[0], preferred_element_type=jnp.float32
    )
    back_rows = product
    weight_sum, back_rows = (weight_sum, back_rows)
    backward = back_rows.astype(jnp.bfloat16)
    from_next = from_behind(backward[0], "pipe", -1)
    from_prior = from_behind(backward[1], "pipe", 1)
    input_grad = jnp.stack([from_next, from_prior])[None]
    pieces = lax.axis_size("pipe")
    blocked = weight_sum[1].reshape(width_in, pieces, width_out // pieces)
    spread = lax.all_to_all(blocked, "pipe", split_axis=1, concat_axis=1, tiled=True)
    turned = spread[:, ::-1]
    partner = lax.all_to_all(turned, "pipe", split_axis=1, concat_axis=1, tiled=True).reshape(
        width_in, width_out
    )
    weight_grad = (weight_sum[0] + partner).astype(jnp.bfloat16)[None]
    return (weight_grad, input_grad)


def solution(mesh):
    placed = (
        P("pipe", None, "tensor", None),
        P("pipe", None, None, "tensor"),
        P("pipe", None, "tensor", None),
    )
    return jax.shard_map(
        shards,
        mesh=mesh,
        in_specs=placed,
        out_specs=(P("pipe", "tensor", None), P("pipe", None, None, "tensor")),
        check_vma=False,
    )
```

profile of v0, /device:TPU:58, one launch (start us, length us, event | category | flops | bytes accessed | tf_op | source)
XLA Modules:
  0.0 347.7 jit_solution(13366332358771188863)
XLA Ops:
  7.2 0.0 copy-start
  7.2 0.0 all-gather.2.cloned.1.call-start
  7.2 0.7 all-gather.2.cloned.1.call-update
  7.9 77.9 %all-gather.2.cloned.1.call-done = bf16[1,2,768,4096]{3,2,1,0:T(8,128)(2,1)} async-done(((bf16[1,2,48,4096]{3,2,1,0:T(8,128)(2,1)}), bf16[1,2,768,4096]{3,2,1,0:T(8,128)(2,1)}) %all-gather.2.cloned.1.call-update) | async-done | bytes 12582928 | tf_op jit(solution)/shard_map/all_gather | solution.py:17
  85.8 0.0 copy-done
  85.8 6.8 %fusion.2 = f32[2,256,4096]{2,1,0:T(8,128)S(1)} fusion(bf16[1,2,768,4096]{3,2,1,0:T(8,128)(2,1)} %all-gather.2.cloned.1.call-done, bf16[1,2,768,256]{3,2,1,0:T(8,128)(2,1)S(1)} %copy-done), kind=kOutput, calls=%fused_computation.2 | convolution fusion | flops 3221225472 | bytes 21757952 | tf_op jit(solution)/shard_map/rtd,rto->rdo/dot_general | solution.py:19
  92.6 0.0 copy-start.1
  92.6 0.4 slice.17
  93.1 2.8 copy-done.1
  95.8 1.7 copy.10
  97.5 2.4 copy.7
  100.0 104.5 %all_to_all.10 = f32[256,16,256]{2,0,1:T(8,128)} all-to-all(f32[256,16,256]{2,0,1:T(8,128)S(1)} %copy.7), channel_id=1, replica_groups=mesh['pipe'=16,'tensor'=16] {'pipe'}, dimensions={1} | all-to-all | bytes 8388608 | tf_op jit(solution)/shard_map/all_to_all | solution.py:33
  204.5 4.6 %rev.3 = f32[256,16,256]{2,0,1:T(8,128)} reverse(f32[256,16,256]{2,0,1:T(8,128)} %all_to_all.10), dimensions={1} | reverse | bytes 8388608 | tf_op jit(solution)/shard_map/rev | solution.py:34
  209.1 6.7 %all-to-all-start.1 = ((f32[256,16,256]{2,0,1:T(8,128)}), f32[256,16,256]{2,0,1:T(8,128)}, u32[]{:S(2)}, u32[]{:S(2)}) async-start(f32[256,16,256]{2,0,1:T(8,128)} %rev.3), calls=%async_computation.1 | async-start | bytes 8388608 | tf_op jit(solution)/shard_map/all_to_all | solution.py:35
  215.8 9.2 %fusion.6 = bf16[2,768,256]{2,1,0:T(8,128)(2,1)S(1)} fusion(bf16[1,2,256,4096]{3,2,1,0:T(8,128)(2,1)} %param.3, bf16[1,2,768,4096]{3,2,1,0:T(8,128)(2,1)} %all-gather.2.cloned.1.call-done), kind=kOutput, calls=%fused_computation.7 | convolution fusion | flops 3221618688 | bytes 17563648 | tf_op jit(solution)/shard_map/rto,rdo->rtd/dot_general | solution.py:22
  225.0 0.1 slice_bitcast_fusion.1
  225.1 5.5 %collective-permute-start = (bf16[768,256]{1,0:T(8,128)(2,1)S(1)}, bf16[768,256]{1,0:T(8,128)(2,1)S(1)}, u32[]{:S(2)}, u32[]{:S(2)}) collective-permute-start(bf16[768,256]{1,0:T(8,128)(2,1)S(1)} %get-tuple-element.2), channel_id=1, source_target_pairs={{16,0},{32,16},{48,32},{64,48},{80,64},{96,80},{112,96},{128,112},... | collective-permute-start | bytes 1179656 | tf_op jit(solution)/shard_map/ppermute | solution.py:10
  230.6 2.1 collective-permute-start.1
  232.7 90.4 %collective-permute-done = bf16[768,256]{1,0:T(8,128)(2,1)S(1)} collective-permute-done((bf16[768,256]{1,0:T(8,128)(2,1)S(1)}, bf16[768,256]{1,0:T(8,128)(2,1)S(1)}, u32[]{:S(2)}, u32[]{:S(2)}) %collective-permute-start) | collective-permute-done | bytes 393248 | tf_op jit(solution)/shard_map/ppermute | solution.py:10
  323.1 0.0 collective-permute-done.1
  323.1 0.9 maximum_bitcast_fusion
  324.0 0.0 all-to-all-done.1
  324.0 6.6 %copy.8 = f32[256,16,256]{2,1,0:T(8,128)} copy(f32[256,16,256]{2,0,1:T(8,128)} %all-to-all-done.1) | data formatting | bytes 8388608 | tf_op jit(solution)/shard_map/all_to_all | solution.py:35
  330.6 5.0 %reshape.8 = f32[1,256,4096]{2,1,0:T(8,128)} reshape(f32[256,16,256]{2,1,0:T(8,128)} %copy.8) | data formatting | bytes 8388608 | tf_op jit(solution)/shard_map/reshape | solution.py:35
  335.6 5.3 %fusion.4 = bf16[1,256,4096]{2,1,0:T(8,128)(2,1)} fusion(f32[1,256,4096]{2,1,0:T(8,128)} %reshape.8, f32[2,256,4096]{2,1,0:T(8,128)} %copy-done.1), kind=kLoop, calls=%fused_computation.5 | loop fusion | flops 2097152 | bytes 10485760 | tf_op jit(solution)/shard_map/convert_element_type | solution.py:38
Async XLA Ops:
  7.2 78.6 %copy-start = (bf16[1,2,768,256]{3,2,1,0:T(8,128)(2,1)S(1)}, bf16[1,2,768,256]{3,2,1,0:T(8,128)(2,1)}, u32[]{:S(2)}) copy-start(bf16[1,2,768,256]{3,2,1,0:T(8,128)(2,1)} %param.4) | copy-start | bytes 2359300
  7.2 78.6 %all-gather.2.cloned.1.call-start = ((), (), s32[]{:S(2)}) async-start(), calls=%async_computation.2 | async-start | bytes 13369344 | tf_op jit(solution)/shard_map/all_gather | solution.py:17
  92.6 3.2 copy-start.1
  209.1 114.9 %all-to-all-start.1 = ((f32[256,16,256]{2,0,1:T(8,128)}), f32[256,16,256]{2,0,1:T(8,128)}, u32[]{:S(2)}, u32[]{:S(2)}) async-start(f32[256,16,256]{2,0,1:T(8,128)} %rev.3), calls=%async_computation.1 | async-start | bytes 8388608 | tf_op jit(solution)/shard_map/all_to_all | solution.py:35
  225.1 98.0 %collective-permute-start = (bf16[768,256]{1,0:T(8,128)(2,1)S(1)}, bf16[768,256]{1,0:T(8,128)(2,1)S(1)}, u32[]{:S(2)}, u32[]{:S(2)}) collective-permute-start(bf16[768,256]{1,0:T(8,128)(2,1)S(1)} %get-tuple-element.2), channel_id=1, source_target_pairs={{16,0},{32,16},{48,32},{64,48},{80,64},{96,80},{112,96},{128,112},... | collective-permute-start | bytes 1179656 | tf_op jit(solution)/shard_map/ppermute | solution.py:10
  230.6 92.5 %collective-permute-start.1 = (bf16[768,256]{1,0:T(8,128)(2,1)S(1)}, bf16[768,256]{1,0:T(8,128)(2,1)S(1)}, u32[]{:S(2)}, u32[]{:S(2)}) collective-permute-start(bf16[768,256]{1,0:T(8,128)(2,1)S(1)} %get-tuple-element.3), channel_id=1, source_target_pairs={{0,16},{16,32},{32,48},{48,64},{64,80},{80,96},{96,112},{112,128},... | collective-permute-start | bytes 1179656 | tf_op jit(solution)/shard_map/ppermute | solution.py:10
Sparse Core Ops, SparseCore 0:
  9.8 75.9 all-gather.1
where the time goes:
time: 350 us; the launch traced here: 348 us
  waiting for transfers between devices  169 us (48%)
  blocking collectives  105 us (30%)
  local copies, waits for them, and re-layouts  23.5 us (7%)
  matrix products  16 us (5%)
  starting transfers between devices  14.4 us (4%)
  between operations  14.1 us (4%)
  other arithmetic  6.25 us (2%)
    all_to_all x1, blocking collectives, shards(): lax.all_to_all(blocked, 'pipe', split_axis=1, concat_axis=1, tiled=True)  105 us
    ppermute x2, waiting for transfers between devices, from_behind(): return lax.ppermute(value, axis, pairs)  90.4 us
    all_gather x1, waiting for transfers between devices, shards(): piece = lax.all_gather(grad_out, 'tensor', axis=2, tiled=True)  77.9 us
    dot_general x1, matrix products, shards(): jnp.einsum('rto,rdo->rtd', piece[0], section_weights[0], preferred_elemen...  9.21 us
    ppermute x2, starting transfers between devices, from_behind(): return lax.ppermute(value, axis, pairs)  7.57 us
  transfers between devices with their start and end apart: 4, of which 2 were waited for; matrix products, arithmetic and copies ran while one was open for 3% of the time, Pallas kernels for 0%

commit v1 on v0

v1 whole, which is shorter than its diff:
```python
import functools

import jax
import jax.numpy as jnp
from jax import lax
from jax.experimental import pallas as pl
from jax.experimental.pallas import tpu as pltpu
from jax.sharding import PartitionSpec as P

RING = 4
PLANES = 2
CORES = 2
KEYS = tuple(
    (dy, dz, dc) for dc in range(CORES) for dy in (0, -1, 1, 2) for dz in range(PLANES)
)


def place(y, plane, core):
    return (y * PLANES + plane) * CORES + core


def moved(value, step):
    pairs = []
    for y in range(RING):
        for plane in range(PLANES):
            for core in range(CORES):
                pairs.append((place(y, plane, core), place(*step(y, plane, core))))
    return lax.ppermute(value, "tensor", pairs)


def upward(value):
    return moved(value, lambda y, plane, core: ((y + 1) % RING, plane, core))


def downward(value):
    return moved(value, lambda y, plane, core: ((y - 1) % RING, plane, core))


def across(value):
    return moved(value, lambda y, plane, core: (y, 1 - plane, core))


def to_sibling(value):
    return moved(value, lambda y, plane, core: (y, plane, 1 - core))


def mirrored(value):
    count = lax.axis_size("pipe")
    return lax.ppermute(value, "pipe", [(i, count - 1 - i) for i in range(count)])


def from_behind(value, by):
    count = lax.axis_size("pipe")
    pairs = [(i, i + by) for i in range(count) if 0 <= i + by < count]
    return lax.ppermute(value, "pipe", pairs)


def gathered(own):
    held = {(0, 0): own, (0, 1): across(own)}
    for dz in range(PLANES):
        held[(-1, dz)] = upward(held[(0, dz)])
        held[(1, dz)] = downward(held[(0, dz)])
    held[(2, 0)] = upward(held[(-1, 0)])
    held[(2, 1)] = downward(held[(1, 1)])
    whole = {}
    for (dy, dz), value in held.items():
        whole[(dy, dz, 0)] = value
        whole[(dy, dz, 1)] = to_sibling(value)
    return [whole[key] for key in KEYS]


def block_of(t, key):
    dy, dz, dc = key
    core = t % CORES
    plane = (t // CORES) % PLANES
    y = t // (CORES * PLANES)
    if dc:
        core = 1 - core
    if dz:
        plane = 1 - plane
    return place((y + dy + RING) % RING, plane, core)


def loads(blocks, whole, sems):
    t = lax.axis_index("tensor")
    rows = blocks[0].shape[-2]
    copies = []
    for i, key in enumerate(KEYS):
        start = pl.multiple_of(block_of(t, key) * rows, rows)
        if len(whole.shape) == 3:
            target = whole.at[:, pl.ds(start, rows), :]
        else:
            target = whole.at[pl.ds(start, rows), :]
        copies.append(pltpu.make_async_copy(blocks[i], target, sems.at[i]))
    return copies


def first_kernel(*refs):
    n = len(KEYS)
    blocks = refs[:n]
    weights, context, back0, back1, total, whole, held, sems, wsem = refs[n:]
    copies = loads(blocks, whole, sems)
    wcopy = pltpu.make_async_copy(weights, held, wsem)
    wcopy.start()
    for copy in copies:
        copy.start()
    wcopy.wait()
    for copy in copies:
        copy.wait()
    tile = 256
    for r, out in enumerate((back0, back1)):
        @pl.loop(0, out.shape[0] // tile)
        def _(i, r=r, out=out):
            rows = pl.ds(pl.multiple_of(i * tile, tile), tile)
            out[rows, :] = lax.dot_general(
                whole[r, rows, :], held[r], (((1,), (1,)), ((), ())),
                preferred_element_type=jnp.float32,
            ).astype(out.dtype)
    wide = 512

    @pl.loop(0, total.shape[1] // wide)
    def _(i):
        cols = pl.ds(pl.multiple_of(i * wide, wide), wide)
        total[:, cols] = jnp.dot(
            context[...], whole[0, :, cols], preferred_element_type=jnp.float32
        )


def last_kernel(*refs):
    n = len(KEYS)
    blocks = refs[:n]
    context, total, out, whole, sems = refs[n:]
    copies = loads(blocks, whole, sems)
    for copy in copies:
        copy.start()
    for copy in copies:
        copy.wait()
    wide = 512

    @pl.loop(0, out.shape[1] // wide)
    def _(i):
        cols = pl.ds(pl.multiple_of(i * wide, wide), wide)
        out[:, cols] = (
            total[:, cols]
            + jnp.dot(context[...], whole[:, cols], preferred_element_type=jnp.float32)
        ).astype(out.dtype)


ANY = pl.BlockSpec(memory_space=pl.ANY)
VMEM = pl.BlockSpec(memory_space=pltpu.VMEM)


def shards(section_weights, context, grad_out):
    tokens, width_in = context.shape[2:]
    width_out = grad_out.shape[3]
    n = len(KEYS)
    both = grad_out[0]
    far = mirrored(both[1])
    far_context = mirrored(context[0, 1])
    near_blocks = gathered(both)
    far_blocks = gathered(far)
    params = pltpu.CompilerParams(vmem_limit_bytes=40 * 2**20)
    flops = 2 * tokens * width_in * width_out
    back0, back1, total = pl.pallas_call(
        first_kernel,
        out_shape=(
            jax.ShapeDtypeStruct((tokens, width_in), jnp.bfloat16),
            jax.ShapeDtypeStruct((tokens, width_in), jnp.bfloat16),
            jax.ShapeDtypeStruct((width_in, width_out), jnp.float32),
        ),
        in_specs=[ANY] * n + [ANY, VMEM],
        out_specs=(VMEM, VMEM, VMEM),
        scratch_shapes=[
            pltpu.VMEM((2, tokens, width_out), jnp.bfloat16),
            pltpu.VMEM((2, width_in, width_out), jnp.bfloat16),
            pltpu.SemaphoreType.DMA((n,)),
            pltpu.SemaphoreType.DMA,
        ],
        compiler_params=params,
        cost_estimate=pl.CostEstimate(
            flops=3 * flops, bytes_accessed=2 * (2 * tokens + 4 * width_in) * width_out,
            transcendentals=0,
        ),
    )(*near_blocks, section_weights[0], context[0, 0].T)
    weight_grad = pl.pallas_call(
        last_kernel,
        out_shape=jax.ShapeDtypeStruct((width_in, width_out), jnp.bfloat16),
        in_specs=[ANY] * n + [VMEM, VMEM],
        out_specs=VMEM,
        scratch_shapes=[
            pltpu.VMEM((tokens, width_out), jnp.bfloat16),
            pltpu.SemaphoreType.DMA((n,)),
        ],
        compiler_params=params,
        cost_estimate=pl.CostEstimate(
            flops=flops, bytes_accessed=2 * (tokens + 3 * width_in) * width_out,
            transcendentals=0,
        ),
    )(*far_blocks, far_context.T, total)
    from_next = from_behind(back0, -1)
    from_prior = from_behind(back1, 1)
    input_grad = jnp.stack([from_next, from_prior])[None]
    return (weight_grad[None], input_grad)


def solution(mesh):
    placed = (
        P("pipe", None, "tensor", None),
        P("pipe", None, None, "tensor"),
        P("pipe", None, "tensor", None),
    )
    return jax.shard_map(
        shards,
        mesh=mesh,
        in_specs=placed,
        out_specs=(P("pipe", "tensor", None), P("pipe", None, None, "tensor")),
        check_vma=False,
    )
```

time: 350 us -> 184 us (0.53)
  blocking collectives: 105 us -> 0 us
  waiting for transfers between devices: 169 us -> 106 us
  Pallas kernels: 0 us -> 22.1 us
  starting transfers between devices: 14.4 us -> 35 us
  matrix products: 16 us -> 0 us
  between operations: 14.1 us -> 0.79 us
  other arithmetic: 6.25 us -> 0.95 us
  local copies, waits for them, and re-layouts: 23.5 us -> 19 us
    all_to_all x1 -> x0, blocking collectives: 105 us -> none  [shards(): lax.all_to_all(blocked, 'pipe', split_axis=1, concat_axis=1, tiled=True)]
    all_gather x1 -> x0, waiting for transfers between devices: 77.9 us -> none  [shards(): piece = lax.all_gather(grad_out, 'tensor', axis=2, tiled=True)]
    ppermute x2 -> x34, starting transfers between devices: 7.57 us -> 35 us  [the longest x30 19.4 us: moved(): return lax.ppermute(value, 'tensor', pairs)]
    pallas_call x0 -> x2, Pallas kernels: none -> 22.1 us  [the longest x1 14.3 us: shards(): pl.pallas_call(first_kernel, out_shape=(jax.ShapeDtypeStruct((tokens, wid...]
    dot_general x2 -> x0, matrix products: 16 us -> none  [the longest x1 9.21 us: shards(): jnp.einsum('rto,rdo->rtd', piece[0], section_weights[0], preferred_elemen...]
    ppermute x2 -> x34, waiting for transfers between devices: 90.4 us -> 106 us  [the longest x30 64.5 us: moved(): return lax.ppermute(value, 'tensor', pairs)]
    unnamed x5 -> x32, local copies, waits for them, and re-layouts: 4.5 us -> 16 us
    all_to_all x1 -> x0, starting transfers between devices: 6.75 us -> none  [shards(): lax.all_to_all(turned, 'pipe', split_axis=1, concat_axis=1, tiled=True)]
  transfers between devices with their start and end apart: 4 -> 34, of which waited for: 2 -> 12; matrix products, arithmetic and copies ran while one was open for 3% -> 2% of each run, Pallas kernels for 0% -> 12%
where the time goes in v1:
time: 184 us; the launch traced here: 183 us
  waiting for transfers between devices  106 us (58%)
  starting transfers between devices  35 us (19%)
  Pallas kernels  22.1 us (12%)
  local copies, waits for them, and re-layouts  19 us (10%)
    ppermute x30, waiting for transfers between devices, moved(): return lax.ppermute(value, 'tensor', pairs)  64.5 us
    ppermute x2, waiting for transfers between devices, mirrored(): lax.ppermute(value, 'pipe', [(i, count - 1 - i) for i in range(count)])  28.4 us
    ppermute x30, starting transfers between devices, moved(): return lax.ppermute(value, 'tensor', pairs)  19.4 us
    unnamed x32, local copies, waits for them, and re-layouts  16 us
    pallas_call x1, Pallas kernels, shards(): pl.pallas_call(first_kernel, out_shape=(jax.ShapeDtypeStruct((tokens, wid...  14.3 us
    ppermute x2, waiting for transfers between devices, from_behind(): return lax.ppermute(value, 'pipe', pairs)  12.6 us
    ppermute x2, starting transfers between devices, from_behind(): return lax.ppermute(value, 'pipe', pairs)  9.01 us
    pallas_call x1, Pallas kernels, shards(): pl.pallas_call(last_kernel, out_shape=jax.ShapeDtypeStruct((width_in, wid...  7.75 us
  transfers between devices with their start and end apart: 34, of which 12 were waited for; matrix products, arithmetic and copies ran while one was open for 2% of the time, Pallas kernels for 12%

profile of v1, /device:TPU:58, one launch (start us, length us, event | category | flops | bytes accessed | tf_op | source)
XLA Modules:
  0.0 183.2 jit_solution(10098237233175808545)
XLA Ops:
  0.6 1.0 slice_bitcast_fusion
  1.7 6.4 %collective-permute-start = (bf16[48,4096]{1,0:T(8,128)(2,1)S(1)}, bf16[48,4096]{1,0:T(8,128)(2,1)S(1)}, u32[]{:S(2)}, u32[]{:S(2)}) collective-permute-start(bf16[48,4096]{1,0:T(8,128)(2,1)S(1)} %slice_bitcast_fusion), channel_id=1, source_target_pairs={{0,240},{16,224},{32,208},{48,192},{64,176},{80,160},{96,144},{112... | collective-permute-start | bytes 1179656 | tf_op jit(solution)/shard_map/ppermute | solution.py:49
  8.1 1.0 collective-permute-start.17
  9.1 0.2 collective-permute-start.18
  9.3 1.8 collective-permute-start.20
  11.1 1.9 %fusion = (bf16[1,1,768,256]{3,2,1,0:T(8,128)(2,1)}, bf16[1,1,768,256]{3,2,1,0:T(8,128)(2,1)S(1)}) fusion(bf16[1,2,768,256]{3,2,1,0:T(8,128)(2,1)} %param.4), kind=kLoop, calls=%fused_computation.2 | loop fusion | bytes 1572864 | tf_op jit(solution)/shard_map/slice | solution.py:184
  13.0 0.2 copy.7
  13.2 0.2 collective-permute-start.16
  13.4 12.8 %collective-permute-done.refs_0_ = bf16[48,4096]{1,0:T(8,128)(2,1)S(1)} collective-permute-done((bf16[48,4096]{1,0:T(8,128)(2,1)S(1)}, bf16[48,4096]{1,0:T(8,128)(2,1)S(1)}, u32[]{:S(2)}, u32[]{:S(2)}) %collective-permute-start) | collective-permute-done | bytes 393248 | tf_op jit(solution)/shard_map/ppermute | solution.py:49
  26.2 15.5 %collective-permute-done.16 = bf16[768,256]{0,1:T(8,128)(2,1)S(1)} collective-permute-done((bf16[768,256]{0,1:T(8,128)(2,1)S(1)}, bf16[768,256]{0,1:T(8,128)(2,1)S(1)}, u32[]{:S(2)}, u32[]{:S(2)}) %collective-permute-start.16) | collective-permute-done | bytes 393248 | tf_op jit(solution)/shard_map/ppermute | solution.py:49
  41.8 1.7 collective-permute-start.1
  43.5 0.2 collective-permute-done.17.refs_1_
  43.7 0.2 collective-permute-start.2
  43.9 1.8 collective-permute-start.4
  45.7 0.0 collective-permute-done.20.refs_4_
  45.7 0.0 collective-permute-start.8
  45.7 6.3 %collective-permute-done.1.refs_1_ = bf16[48,4096]{1,0:T(8,128)(2,1)S(1)} collective-permute-done((bf16[48,4096]{1,0:T(8,128)(2,1)S(1)}, bf16[48,4096]{1,0:T(8,128)(2,1)S(1)}, u32[]{:S(2)}, u32[]{:S(2)}) %collective-permute-start.1) | collective-permute-done | bytes 393248 | tf_op jit(solution)/shard_map/ppermute | solution.py:28
  52.1 0.7 collective-permute-start.5
  52.8 0.0 collective-permute-done.24.refs_8_
  52.8 0.9 copy-done.7
  53.7 2.5 %collective-permute-start.3 = (bf16[48,4096]{1,0:T(8,128)(2,1)S(1)}, bf16[48,4096]{1,0:T(8,128)(2,1)S(1)}, u32[]{:S(2)}, u32[]{:S(2)}) collective-permute-start(bf16[48,4096]{1,0:T(8,128)(2,1)S(1)} %collective-permute-done.1.refs_1_), channel_id=1, source_target_pairs={{0,4},{1,5},{2,6},{3,7},{4,8},{5,9},{6,10},{7,11},{8,12},{9,13},{1... | collective-permute-start | bytes 1179656 | tf_op jit(solution)/shard_map/ppermute | solution.py:28
  56.2 3.2 %collective-permute-start.19 = (bf16[2,48,4096]{2,1,0:T(8,128)(2,1)}, bf16[2,48,4096]{2,1,0:T(8,128)(2,1)}, u32[]{:S(2)}, u32[]{:S(2)}) collective-permute-start(bf16[2,48,4096]{2,1,0:T(8,128)(2,1)} %collective-permute-done.17.refs_1_), channel_id=1, source_target_pairs={{0,4},{1,5},{2,6},{3,7},{4,8},{5,9},{6,10},{7,11},{8,12},{9,13},{1... | collective-permute-start | bytes 2359304 | tf_op jit(solution)/shard_map/ppermute | solution.py:28
  59.4 0.1 collective-permute-start.6
  59.5 5.8 %collective-permute-done.5.refs_5_ = bf16[48,4096]{1,0:T(8,128)(2,1)S(1)} collective-permute-done((bf16[48,4096]{1,0:T(8,128)(2,1)S(1)}, bf16[48,4096]{1,0:T(8,128)(2,1)S(1)}, u32[]{:S(2)}, u32[]{:S(2)}) %collective-permute-start.5) | collective-permute-done | bytes 393248 | tf_op jit(solution)/shard_map/ppermute | solution.py:28
  65.3 0.4 collective-permute-done.3.refs_3_
  65.8 0.1 collective-permute-start.10
  65.9 22.2 %collective-permute-done.6.refs_6_ = bf16[48,4096]{1,0:T(8,128)(2,1)S(1)} collective-permute-done((bf16[48,4096]{1,0:T(8,128)(2,1)S(1)}, bf16[48,4096]{1,0:T(8,128)(2,1)S(1)}, u32[]{:S(2)}, u32[]{:S(2)}) %collective-permute-start.6) | collective-permute-done | bytes 393248 | tf_op jit(solution)/shard_map/ppermute | solution.py:28
  88.1 3.7 %collective-permute-start.22 = (bf16[2,48,4096]{2,1,0:T(8,128)(2,1)}, bf16[2,48,4096]{2,1,0:T(8,128)(2,1)}, u32[]{:S(2)}, u32[]{:S(2)}) collective-permute-start(bf16[2,48,4096]{2,1,0:T(8,128)(2,1)} %collective-permute-done.18.refs_2_), channel_id=1, source_target_pairs={{0,4},{1,5},{2,6},{3,7},{4,8},{5,9},{6,10},{7,11},{8,12},{9,13},{1... | collective-permute-start | bytes 2359304 | tf_op jit(solution)/shard_map/ppermute | solution.py:28
  91.8 0.7 copy-done.1
  92.5 0.0 collective-permute-start.25
  92.5 0.0 collective-permute-done.10.refs_10_
  92.6 0.8 copy-done.3
  93.3 0.5 collective-permute-start.26
  93.8 0.1 collective-permute-start.28
  94.0 12.3 %collective-permute-done.22.refs_6_ = bf16[2,48,4096]{2,1,0:T(8,128)(2,1)} collective-permute-done((bf16[2,48,4096]{2,1,0:T(8,128)(2,1)}, bf16[2,48,4096]{2,1,0:T(8,128)(2,1)}, u32[]{:S(2)}, u32[]{:S(2)}) %collective-permute-start.22) | collective-permute-done | bytes 786464 | tf_op jit(solution)/shard_map/ppermute | solution.py:28
  106.2 0.0 collective-permute-start.29
  106.2 0.0 collective-permute-done.25.refs_9_
  106.2 0.9 copy-done.9
  107.1 0.5 collective-permute-start.27
  107.6 0.0 collective-permute-done.26.refs_10_
  107.6 0.9 copy-done.11
  108.5 0.0 collective-permute-start.30
  108.5 6.3 %collective-permute-done.23.refs_7_ = bf16[2,48,4096]{2,1,0:T(8,128)(2,1)} collective-permute-done((bf16[2,48,4096]{2,1,0:T(8,128)(2,1)}, bf16[2,48,4096]{2,1,0:T(8,128)(2,1)}, u32[]{:S(2)}, u32[]{:S(2)}) %collective-permute-start.23) | collective-permute-done | bytes 786464 | tf_op jit(solution)/shard_map/ppermute | solution.py:28
  114.8 0.9 copy-done.13
  115.7 1.9 %copy.8 = bf16[1,1,768,256]{2,3,1,0:T(8,128)(2,1)} copy(bf16[1,1,768,256]{3,2,1,0:T(8,128)(2,1)} %get-tuple-element.8) | data formatting | bytes 786432
  117.6 10.9 %collective-permute-done.7.refs_7_ = bf16[48,4096]{1,0:T(8,128)(2,1)} collective-permute-done((bf16[48,4096]{1,0:T(8,128)(2,1)S(1)}, bf16[48,4096]{1,0:T(8,128)(2,1)}, u32[]{:S(2)}, u32[]{:S(2)}) %collective-permute-start.7) | collective-permute-done | bytes 393248 | tf_op jit(solution)/shard_map/ppermute | solution.py:28
  128.6 0.5 collective-permute-start.13
  129.1 0.1 collective-permute-start.11
  129.2 0.4 collective-permute-start.14
  129.6 0.1 collective-permute-start.15
  129.7 1.0 copy-done.5
  130.7 1.1 copy-done.6
  131.8 1.1 copy-done.8
  133.0 1.1 copy-done.10
  134.1 1.1 copy-done.12
  135.2 1.1 copy-done.14
  136.4 14.3 %shard_map.50 = (bf16[768,256]{1,0:T(8,128)(2,1)S(1)}, bf16[768,256]{1,0:T(8,128)(2,1)S(1)}, f32[256,4096]{1,0:T(8,128)}) custom-call(bf16[2,48,4096]{2,1,0:T(8,128)(2,1)S(1)} %bitcast.20, bf16[2,48,4096]{2,1,0:T(8,128)(2,1)} %collective-permute-done.17.refs_1_, bf16[2,48,4096]{2,1,0:T(8,128)(2,1)} %collective-permute-done.18.refs_2_, ...), custom_call_target="tpu_custom_call" | custom-call | flops 4831838208 | bytes 20971520 | tf_op jit(solution)/shard_map/pallas_call | solution.py:164
  150.7 7.1 %collective-permute-start.32 = (bf16[768,256]{1,0:T(8,128)(2,1)S(1)}, bf16[768,256]{1,0:T(8,128)(2,1)S(1)}, u32[]{:S(2)}, u32[]{:S(2)}) collective-permute-start(bf16[768,256]{1,0:T(8,128)(2,1)S(1)} %get-tuple-element.6), channel_id=1, source_target_pairs={{16,0},{32,16},{48,32},{64,48},{80,64},{96,80},{112,96},{128,112},... | collective-permute-start | bytes 1179656 | tf_op jit(solution)/shard_map/ppermute | solution.py:55
  157.8 1.9 %collective-permute-start.33 = (bf16[768,256]{1,0:T(8,128)(2,1)S(1)}, bf16[768,256]{1,0:T(8,128)(2,1)S(1)}, u32[]{:S(2)}, u32[]{:S(2)}) collective-permute-start(bf16[768,256]{1,0:T(8,128)(2,1)S(1)} %get-tuple-element.7), channel_id=1, source_target_pairs={{0,16},{16,32},{32,48},{48,64},{64,80},{80,96},{96,112},{112,128},... | collective-permute-start | bytes 1179656 | tf_op jit(solution)/shard_map/ppermute | solution.py:55
  159.8 2.2 %copy-done = f32[256,4096]{1,0:T(8,128)S(1)} copy-done((f32[256,4096]{1,0:T(8,128)S(1)}, f32[256,4096]{1,0:T(8,128)}, u32[]{:S(2)}) %copy-start) | copy-done | bytes 4194328
  162.0 7.7 %shard_map.51 = bf16[256,4096]{1,0:T(8,128)(2,1)} custom-call(bf16[48,4096]{1,0:T(8,128)(2,1)S(1)} %collective-permute-done.refs_0_, bf16[48,4096]{1,0:T(8,128)(2,1)S(1)} %collective-permute-done.1.refs_1_, bf16[48,4096]{1,0:T(8,128)(2,1)S(1)} %collective-permute-done.2.refs_2_, bf16[48,4096]{1,0:T(8,128)(2,1)S(1)} %collective-permute-done.3.refs_3_, ...), custom_call_target="tpu_custom_call" | custom-call | flops 1610612736 | bytes 12582912 | tf_op jit(solution)/shard_map/pallas_call | solution.py:185
  169.7 4.6 %collective-permute-done.32 = bf16[768,256]{1,0:T(8,128)(2,1)S(1)} collective-permute-done((bf16[768,256]{1,0:T(8,128)(2,1)S(1)}, bf16[768,256]{1,0:T(8,128)(2,1)S(1)}, u32[]{:S(2)}, u32[]{:S(2)}) %collective-permute-start.32) | collective-permute-done | bytes 393248 | tf_op jit(solution)/shard_map/ppermute | solution.py:55
  174.3 8.0 %collective-permute-done.33 = bf16[768,256]{1,0:T(8,128)(2,1)S(1)} collective-permute-done((bf16[768,256]{1,0:T(8,128)(2,1)S(1)}, bf16[768,256]{1,0:T(8,128)(2,1)S(1)}, u32[]{:S(2)}, u32[]{:S(2)}) %collective-permute-start.33) | collective-permute-done | bytes 393248 | tf_op jit(solution)/shard_map/ppermute | solution.py:55
  182.3 0.9 maximum_bitcast_fusion
  (41 shorter events, 0.1 us)
Async XLA Ops:
  1.7 24.6 %collective-permute-start = (bf16[48,4096]{1,0:T(8,128)(2,1)S(1)}, bf16[48,4096]{1,0:T(8,128)(2,1)S(1)}, u32[]{:S(2)}, u32[]{:S(2)}) collective-permute-start(bf16[48,4096]{1,0:T(8,128)(2,1)S(1)} %slice_bitcast_fusion), channel_id=1, source_target_pairs={{0,240},{16,224},{32,208},{48,192},{64,176},{80,160},{96,144},{112... | collective-permute-start | bytes 1179656 | tf_op jit(solution)/shard_map/ppermute | solution.py:49
  8.1 35.6 %collective-permute-start.17 = (bf16[2,48,4096]{2,1,0:T(8,128)(2,1)}, bf16[2,48,4096]{2,1,0:T(8,128)(2,1)}, u32[]{:S(2)}, u32[]{:S(2)}) collective-permute-start(bf16[2,48,4096]{2,1,0:T(8,128)(2,1)} %bitcast.16), channel_id=1, source_target_pairs={{0,2},{1,3},{2,0},{3,1},{4,6},{5,7},{6,4},{7,5},{8,10},{9,11},{10,... | collective-permute-start | bytes 2359304 | tf_op jit(solution)/shard_map/ppermute | solution.py:28
  9.1 34.8 %collective-permute-start.18 = (bf16[2,48,4096]{2,1,0:T(8,128)(2,1)}, bf16[2,48,4096]{2,1,0:T(8,128)(2,1)}, u32[]{:S(2)}, u32[]{:S(2)}) collective-permute-start(bf16[2,48,4096]{2,1,0:T(8,128)(2,1)} %bitcast.17), channel_id=1, source_target_pairs={{0,4},{1,5},{2,6},{3,7},{4,8},{5,9},{6,10},{7,11},{8,12},{9,13},{1... | collective-permute-start | bytes 2359304 | tf_op jit(solution)/shard_map/ppermute | solution.py:28
  9.3 36.4 %collective-permute-start.20 = (bf16[2,48,4096]{2,1,0:T(8,128)(2,1)}, bf16[2,48,4096]{2,1,0:T(8,128)(2,1)}, u32[]{:S(2)}, u32[]{:S(2)}) collective-permute-start(bf16[2,48,4096]{2,1,0:T(8,128)(2,1)} %bitcast.18), channel_id=1, source_target_pairs={{0,12},{1,13},{2,14},{3,15},{4,0},{5,1},{6,2},{7,3},{8,4},{9,5},{1... | collective-permute-start | bytes 2359304 | tf_op jit(solution)/shard_map/ppermute | solution.py:28
  13.2 28.6 %collective-permute-start.16 = (bf16[768,256]{0,1:T(8,128)(2,1)S(1)}, bf16[768,256]{0,1:T(8,128)(2,1)S(1)}, u32[]{:S(2)}, u32[]{:S(2)}) collective-permute-start(bf16[768,256]{0,1:T(8,128)(2,1)S(1)} %bitcast.22), channel_id=1, source_target_pairs={{0,240},{16,224},{32,208},{48,192},{64,176},{80,160},{96,144},{112... | collective-permute-start | bytes 1179656 | tf_op jit(solution)/shard_map/ppermute | solution.py:49
  26.2 26.6 %collective-permute-start.24 = (bf16[2,48,4096]{2,1,0:T(8,128)(2,1)}, bf16[2,48,4096]{2,1,0:T(8,128)(2,1)S(1)}, u32[]{:S(2)}, u32[]{:S(2)}) collective-permute-start(bf16[2,48,4096]{2,1,0:T(8,128)(2,1)} %bitcast.19), channel_id=1, source_target_pairs={{0,1},{1,0},{2,3},{3,2},{4,5},{5,4},{6,7},{7,6},{8,9},{9,8},{10,11... | collective-permute-start | bytes 2359304 | tf_op jit(solution)/shard_map/ppermute | solution.py:28
  41.8 10.3 %collective-permute-start.1 = (bf16[48,4096]{1,0:T(8,128)(2,1)S(1)}, bf16[48,4096]{1,0:T(8,128)(2,1)S(1)}, u32[]{:S(2)}, u32[]{:S(2)}) collective-permute-start(bf16[48,4096]{1,0:T(8,128)(2,1)S(1)} %collective-permute-done.refs_0_), channel_id=1, source_target_pairs={{0,2},{1,3},{2,0},{3,1},{4,6},{5,7},{6,4},{7,5},{8,10},{9,11},{10,... | collective-permute-start | bytes 1179656 | tf_op jit(solution)/shard_map/ppermute | solution.py:28
  43.7 12.5 %collective-permute-start.2 = (bf16[48,4096]{1,0:T(8,128)(2,1)S(1)}, bf16[48,4096]{1,0:T(8,128)(2,1)S(1)}, u32[]{:S(2)}, u32[]{:S(2)}) collective-permute-start(bf16[48,4096]{1,0:T(8,128)(2,1)S(1)} %collective-permute-done.refs_0_), channel_id=1, source_target_pairs={{0,4},{1,5},{2,6},{3,7},{4,8},{5,9},{6,10},{7,11},{8,12},{9,13},{1... | collective-permute-start | bytes 1179656 | tf_op jit(solution)/shard_map/ppermute | solution.py:28
  43.9 12.3 %collective-permute-start.4 = (bf16[48,4096]{1,0:T(8,128)(2,1)S(1)}, bf16[48,4096]{1,0:T(8,128)(2,1)S(1)}, u32[]{:S(2)}, u32[]{:S(2)}) collective-permute-start(bf16[48,4096]{1,0:T(8,128)(2,1)S(1)} %collective-permute-done.refs_0_), channel_id=1, source_target_pairs={{0,12},{1,13},{2,14},{3,15},{4,0},{5,1},{6,2},{7,3},{8,4},{9,5},{1... | collective-permute-start | bytes 1179656 | tf_op jit(solution)/shard_map/ppermute | solution.py:28
  45.7 13.7 %collective-permute-start.8 = (bf16[48,4096]{1,0:T(8,128)(2,1)S(1)}, bf16[48,4096]{1,0:T(8,128)(2,1)S(1)}, u32[]{:S(2)}, u32[]{:S(2)}) collective-permute-start(bf16[48,4096]{1,0:T(8,128)(2,1)S(1)} %collective-permute-done.refs_0_), channel_id=1, source_target_pairs={{0,1},{1,0},{2,3},{3,2},{4,5},{5,4},{6,7},{7,6},{8,9},{9,8},{10,11... | collective-permute-start | bytes 1179656 | tf_op jit(solution)/shard_map/ppermute | solution.py:28
  52.1 13.3 %collective-permute-start.5 = (bf16[48,4096]{1,0:T(8,128)(2,1)S(1)}, bf16[48,4096]{1,0:T(8,128)(2,1)S(1)}, u32[]{:S(2)}, u32[]{:S(2)}) collective-permute-start(bf16[48,4096]{1,0:T(8,128)(2,1)S(1)} %collective-permute-done.1.refs_1_), channel_id=1, source_target_pairs={{0,12},{1,13},{2,14},{3,15},{4,0},{5,1},{6,2},{7,3},{8,4},{9,5},{1... | collective-permute-start | bytes 1179656 | tf_op jit(solution)/shard_map/ppermute | solution.py:28
  52.8 0.9 copy-start.7
  53.7 12.1 %collective-permute-start.3 = (bf16[48,4096]{1,0:T(8,128)(2,1)S(1)}, bf16[48,4096]{1,0:T(8,128)(2,1)S(1)}, u32[]{:S(2)}, u32[]{:S(2)}) collective-permute-start(bf16[48,4096]{1,0:T(8,128)(2,1)S(1)} %collective-permute-done.1.refs_1_), channel_id=1, source_target_pairs={{0,4},{1,5},{2,6},{3,7},{4,8},{5,9},{6,10},{7,11},{8,12},{9,13},{1... | collective-permute-start | bytes 1179656 | tf_op jit(solution)/shard_map/ppermute | solution.py:28
  56.2 37.6 %collective-permute-start.21 = (bf16[2,48,4096]{2,1,0:T(8,128)(2,1)}, bf16[2,48,4096]{2,1,0:T(8,128)(2,1)}, u32[]{:S(2)}, u32[]{:S(2)}) collective-permute-start(bf16[2,48,4096]{2,1,0:T(8,128)(2,1)} %collective-permute-done.17.refs_1_), channel_id=1, source_target_pairs={{0,12},{1,13},{2,14},{3,15},{4,0},{5,1},{6,2},{7,3},{8,4},{9,5},{1... | collective-permute-start | bytes 2359304 | tf_op jit(solution)/shard_map/ppermute | solution.py:28
  56.2 37.6 %collective-permute-start.19 = (bf16[2,48,4096]{2,1,0:T(8,128)(2,1)}, bf16[2,48,4096]{2,1,0:T(8,128)(2,1)}, u32[]{:S(2)}, u32[]{:S(2)}) collective-permute-start(bf16[2,48,4096]{2,1,0:T(8,128)(2,1)} %collective-permute-done.17.refs_1_), channel_id=1, source_target_pairs={{0,4},{1,5},{2,6},{3,7},{4,8},{5,9},{6,10},{7,11},{8,12},{9,13},{1... | collective-permute-start | bytes 2359304 | tf_op jit(solution)/shard_map/ppermute | solution.py:28
  59.4 28.7 %collective-permute-start.6 = (bf16[48,4096]{1,0:T(8,128)(2,1)S(1)}, bf16[48,4096]{1,0:T(8,128)(2,1)S(1)}, u32[]{:S(2)}, u32[]{:S(2)}) collective-permute-start(bf16[48,4096]{1,0:T(8,128)(2,1)S(1)} %collective-permute-done.2.refs_2_), channel_id=1, source_target_pairs={{0,4},{1,5},{2,6},{3,7},{4,8},{5,9},{6,10},{7,11},{8,12},{9,13},{1... | collective-permute-start | bytes 1179656 | tf_op jit(solution)/shard_map/ppermute | solution.py:28
  65.3 26.5 %collective-permute-start.9 = (bf16[48,4096]{1,0:T(8,128)(2,1)S(1)}, bf16[48,4096]{1,0:T(8,128)(2,1)S(1)}, u32[]{:S(2)}, u32[]{:S(2)}) collective-permute-start(bf16[48,4096]{1,0:T(8,128)(2,1)S(1)} %collective-permute-done.1.refs_1_), channel_id=1, source_target_pairs={{0,1},{1,0},{2,3},{3,2},{4,5},{5,4},{6,7},{7,6},{8,9},{9,8},{10,11... | collective-permute-start | bytes 1179656 | tf_op jit(solution)/shard_map/ppermute | solution.py:28
  65.8 26.8 %collective-permute-start.10 = (bf16[48,4096]{1,0:T(8,128)(2,1)S(1)}, bf16[48,4096]{1,0:T(8,128)(2,1)S(1)}, u32[]{:S(2)}, u32[]{:S(2)}) collective-permute-start(bf16[48,4096]{1,0:T(8,128)(2,1)S(1)} %collective-permute-done.2.refs_2_), channel_id=1, source_target_pairs={{0,1},{1,0},{2,3},{3,2},{4,5},{5,4},{6,7},{7,6},{8,9},{9,8},{10,11... | collective-permute-start | bytes 1179656 | tf_op jit(solution)/shard_map/ppermute | solution.py:28
  88.1 18.1 %collective-permute-start.22 = (bf16[2,48,4096]{2,1,0:T(8,128)(2,1)}, bf16[2,48,4096]{2,1,0:T(8,128)(2,1)}, u32[]{:S(2)}, u32[]{:S(2)}) collective-permute-start(bf16[2,48,4096]{2,1,0:T(8,128)(2,1)} %collective-permute-done.18.refs_2_), channel_id=1, source_target_pairs={{0,4},{1,5},{2,6},{3,7},{4,8},{5,9},{6,10},{7,11},{8,12},{9,13},{1... | collective-permute-start | bytes 2359304 | tf_op jit(solution)/shard_map/ppermute | solution.py:28
  91.8 0.7 copy-start.1
  92.5 13.7 %collective-permute-start.25 = (bf16[2,48,4096]{2,1,0:T(8,128)(2,1)}, bf16[2,48,4096]{2,1,0:T(8,128)(2,1)S(1)}, u32[]{:S(2)}, u32[]{:S(2)}) collective-permute-start(bf16[2,48,4096]{2,1,0:T(8,128)(2,1)} %collective-permute-done.17.refs_1_), channel_id=1, source_target_pairs={{0,1},{1,0},{2,3},{3,2},{4,5},{5,4},{6,7},{7,6},{8,9},{9,8},{10,11... | collective-permute-start | bytes 2359304 | tf_op jit(solution)/shard_map/ppermute | solution.py:28
  92.5 0.8 copy-start.3
  93.3 14.3 %collective-permute-start.26 = (bf16[2,48,4096]{2,1,0:T(8,128)(2,1)}, bf16[2,48,4096]{2,1,0:T(8,128)(2,1)S(1)}, u32[]{:S(2)}, u32[]{:S(2)}) collective-permute-start(bf16[2,48,4096]{2,1,0:T(8,128)(2,1)} %collective-permute-done.18.refs_2_), channel_id=1, source_target_pairs={{0,1},{1,0},{2,3},{3,2},{4,5},{5,4},{6,7},{7,6},{8,9},{9,8},{10,11... | collective-permute-start | bytes 2359304 | tf_op jit(solution)/shard_map/ppermute | solution.py:28
  93.8 21.0 %collective-permute-start.23 = (bf16[2,48,4096]{2,1,0:T(8,128)(2,1)}, bf16[2,48,4096]{2,1,0:T(8,128)(2,1)}, u32[]{:S(2)}, u32[]{:S(2)}) collective-permute-start(bf16[2,48,4096]{2,1,0:T(8,128)(2,1)} %collective-permute-done.21.refs_5_), channel_id=1, source_target_pairs={{0,12},{1,13},{2,14},{3,15},{4,0},{5,1},{6,2},{7,3},{8,4},{9,5},{1... | collective-permute-start | bytes 2359304 | tf_op jit(solution)/shard_map/ppermute | solution.py:28
  93.8 21.0 %collective-permute-start.28 = (bf16[2,48,4096]{2,1,0:T(8,128)(2,1)}, bf16[2,48,4096]{2,1,0:T(8,128)(2,1)S(1)}, u32[]{:S(2)}, u32[]{:S(2)}) collective-permute-start(bf16[2,48,4096]{2,1,0:T(8,128)(2,1)} %collective-permute-done.20.refs_4_), channel_id=1, source_target_pairs={{0,1},{1,0},{2,3},{3,2},{4,5},{5,4},{6,7},{7,6},{8,9},{9,8},{10,11... | collective-permute-start | bytes 2359304 | tf_op jit(solution)/shard_map/ppermute | solution.py:28
  106.2 22.3 %collective-permute-start.29 = (bf16[2,48,4096]{2,1,0:T(8,128)(2,1)}, bf16[2,48,4096]{2,1,0:T(8,128)(2,1)}, u32[]{:S(2)}, u32[]{:S(2)}) collective-permute-start(bf16[2,48,4096]{2,1,0:T(8,128)(2,1)} %collective-permute-done.21.refs_5_), channel_id=1, source_target_pairs={{0,1},{1,0},{2,3},{3,2},{4,5},{5,4},{6,7},{7,6},{8,9},{9,8},{10,11... | collective-permute-start | bytes 2359304 | tf_op jit(solution)/shard_map/ppermute | solution.py:28
  106.2 0.9 copy-start.9
  107.1 22.0 %collective-permute-start.27 = (bf16[2,48,4096]{2,1,0:T(8,128)(2,1)}, bf16[2,48,4096]{2,1,0:T(8,128)(2,1)}, u32[]{:S(2)}, u32[]{:S(2)}) collective-permute-start(bf16[2,48,4096]{2,1,0:T(8,128)(2,1)} %collective-permute-done.19.refs_3_), channel_id=1, source_target_pairs={{0,1},{1,0},{2,3},{3,2},{4,5},{5,4},{6,7},{7,6},{8,9},{9,8},{10,11... | collective-permute-start | bytes 2359304 | tf_op jit(solution)/shard_map/ppermute | solution.py:28
  107.6 0.9 copy-start.11
  108.5 20.6 %collective-permute-start.30 = (bf16[2,48,4096]{2,1,0:T(8,128)(2,1)}, bf16[2,48,4096]{2,1,0:T(8,128)(2,1)}, u32[]{:S(2)}, u32[]{:S(2)}) collective-permute-start(bf16[2,48,4096]{2,1,0:T(8,128)(2,1)} %collective-permute-done.22.refs_6_), channel_id=1, source_target_pairs={{0,1},{1,0},{2,3},{3,2},{4,5},{5,4},{6,7},{7,6},{8,9},{9,8},{10,11... | collective-permute-start | bytes 2359304 | tf_op jit(solution)/shard_map/ppermute | solution.py:28
  114.8 14.8 %collective-permute-start.31 = (bf16[2,48,4096]{2,1,0:T(8,128)(2,1)}, bf16[2,48,4096]{2,1,0:T(8,128)(2,1)}, u32[]{:S(2)}, u32[]{:S(2)}) collective-permute-start(bf16[2,48,4096]{2,1,0:T(8,128)(2,1)} %collective-permute-done.23.refs_7_), channel_id=1, source_target_pairs={{0,1},{1,0},{2,3},{3,2},{4,5},{5,4},{6,7},{7,6},{8,9},{9,8},{10,11... | collective-permute-start | bytes 2359304 | tf_op jit(solution)/shard_map/ppermute | solution.py:28
  114.8 0.9 copy-start.13
  115.7 12.8 %collective-permute-start.7 = (bf16[48,4096]{1,0:T(8,128)(2,1)S(1)}, bf16[48,4096]{1,0:T(8,128)(2,1)}, u32[]{:S(2)}, u32[]{:S(2)}) collective-permute-start(bf16[48,4096]{1,0:T(8,128)(2,1)S(1)} %collective-permute-done.5.refs_5_), channel_id=1, source_target_pairs={{0,12},{1,13},{2,14},{3,15},{4,0},{5,1},{6,2},{7,3},{8,4},{9,5},{1... | collective-permute-start | bytes 1179656 | tf_op jit(solution)/shard_map/ppermute | solution.py:28
  128.6 22.1 %collective-permute-start.12 = (bf16[48,4096]{1,0:T(8,128)(2,1)S(1)}, bf16[48,4096]{1,0:T(8,128)(2,1)S(1)}, u32[]{:S(2)}, u32[]{:S(2)}) collective-permute-start(bf16[48,4096]{1,0:T(8,128)(2,1)S(1)} %collective-permute-done.4.refs_4_), channel_id=1, source_target_pairs={{0,1},{1,0},{2,3},{3,2},{4,5},{5,4},{6,7},{7,6},{8,9},{9,8},{10,11... | collective-permute-start | bytes 1179656 | tf_op jit(solution)/shard_map/ppermute | solution.py:28
  128.6 29.2 %collective-permute-start.13 = (bf16[48,4096]{1,0:T(8,128)(2,1)S(1)}, bf16[48,4096]{1,0:T(8,128)(2,1)S(1)}, u32[]{:S(2)}, u32[]{:S(2)}) collective-permute-start(bf16[48,4096]{1,0:T(8,128)(2,1)S(1)} %collective-permute-done.5.refs_5_), channel_id=1, source_target_pairs={{0,1},{1,0},{2,3},{3,2},{4,5},{5,4},{6,7},{7,6},{8,9},{9,8},{10,11... | collective-permute-start | bytes 1179656 | tf_op jit(solution)/shard_map/ppermute | solution.py:28
  129.1 30.6 %collective-permute-start.11 = (bf16[48,4096]{1,0:T(8,128)(2,1)S(1)}, bf16[48,4096]{1,0:T(8,128)(2,1)S(1)}, u32[]{:S(2)}, u32[]{:S(2)}) collective-permute-start(bf16[48,4096]{1,0:T(8,128)(2,1)S(1)} %collective-permute-done.3.refs_3_), channel_id=1, source_target_pairs={{0,1},{1,0},{2,3},{3,2},{4,5},{5,4},{6,7},{7,6},{8,9},{9,8},{10,11... | collective-permute-start | bytes 1179656 | tf_op jit(solution)/shard_map/ppermute | solution.py:28
  129.2 30.6 %collective-permute-start.14 = (bf16[48,4096]{1,0:T(8,128)(2,1)S(1)}, bf16[48,4096]{1,0:T(8,128)(2,1)S(1)}, u32[]{:S(2)}, u32[]{:S(2)}) collective-permute-start(bf16[48,4096]{1,0:T(8,128)(2,1)S(1)} %collective-permute-done.6.refs_6_), channel_id=1, source_target_pairs={{0,1},{1,0},{2,3},{3,2},{4,5},{5,4},{6,7},{7,6},{8,9},{9,8},{10,11... | collective-permute-start | bytes 1179656 | tf_op jit(solution)/shard_map/ppermute | solution.py:28
  129.6 30.1 %collective-permute-start.15 = (bf16[48,4096]{1,0:T(8,128)(2,1)}, bf16[48,4096]{1,0:T(8,128)(2,1)S(1)}, u32[]{:S(2)}, u32[]{:S(2)}) collective-permute-start(bf16[48,4096]{1,0:T(8,128)(2,1)} %collective-permute-done.7.refs_7_), channel_id=1, source_target_pairs={{0,1},{1,0},{2,3},{3,2},{4,5},{5,4},{6,7},{7,6},{8,9},{9,8},{10,11... | collective-permute-start | bytes 1179656 | tf_op jit(solution)/shard_map/ppermute | solution.py:28
  129.7 1.0 copy-start.5
  130.7 1.1 copy-start.6
  131.8 1.1 copy-start.8
  133.0 1.1 copy-start.10
  134.1 1.1 copy-start.12
  135.2 1.1 copy-start.14
  136.4 23.4 %copy-start.2 = (bf16[48,4096]{1,0:T(8,128)(2,1)S(1)}, bf16[48,4096]{1,0:T(8,128)(2,1)}, u32[]{:S(2)}) copy-start(bf16[48,4096]{1,0:T(8,128)(2,1)} %copy-done.1) | copy-start | bytes 1179652
  136.4 23.4 %copy-start.4 = (bf16[48,4096]{1,0:T(8,128)(2,1)S(1)}, bf16[48,4096]{1,0:T(8,128)(2,1)}, u32[]{:S(2)}) copy-start(bf16[48,4096]{1,0:T(8,128)(2,1)} %copy-done.3) | copy-start | bytes 1179652
  150.7 23.6 %collective-permute-start.32 = (bf16[768,256]{1,0:T(8,128)(2,1)S(1)}, bf16[768,256]{1,0:T(8,128)(2,1)S(1)}, u32[]{:S(2)}, u32[]{:S(2)}) collective-permute-start(bf16[768,256]{1,0:T(8,128)(2,1)S(1)} %get-tuple-element.6), channel_id=1, source_target_pairs={{16,0},{32,16},{48,32},{64,48},{80,64},{96,80},{112,96},{128,112},... | collective-permute-start | bytes 1179656 | tf_op jit(solution)/shard_map/ppermute | solution.py:55
  157.8 24.5 %collective-permute-start.33 = (bf16[768,256]{1,0:T(8,128)(2,1)S(1)}, bf16[768,256]{1,0:T(8,128)(2,1)S(1)}, u32[]{:S(2)}, u32[]{:S(2)}) collective-permute-start(bf16[768,256]{1,0:T(8,128)(2,1)S(1)} %get-tuple-element.7), channel_id=1, source_target_pairs={{0,16},{16,32},{32,48},{48,64},{64,80},{80,96},{96,112},{112,128},... | collective-permute-start | bytes 1179656 | tf_op jit(solution)/shard_map/ppermute | solution.py:55
  159.8 2.2 %copy-start = (f32[256,4096]{1,0:T(8,128)S(1)}, f32[256,4096]{1,0:T(8,128)}, u32[]{:S(2)}) copy-start(f32[256,4096]{1,0:T(8,128)} %get-tuple-element.5.refs_17_) | copy-start | bytes 12582916

commit v2 on v0

v2 whole, which is shorter than its diff:
```python
import jax
import jax.numpy as jnp
from jax import lax
from jax.experimental import pallas as pl
from jax.experimental.pallas import tpu as pltpu
from jax.sharding import PartitionSpec as P

RING = 4
PLANES = 2
CORES = 2
HOPS = range(RING)
NEAR = tuple((hop, dz, 0) for dz in range(PLANES) for hop in HOPS)
EARLY = tuple((hop, dz, 0) for dz in range(PLANES) for hop in (0, 1))
LATE = tuple((hop, dz, dc) for hop in (2, 3) for dz in range(PLANES) for dc in range(CORES))
ANY = pl.BlockSpec(memory_space=pl.ANY)
VMEM = pl.BlockSpec(memory_space=pltpu.VMEM)


def place(y, plane, core):
    return (y * PLANES + plane) * CORES + core


def moved(value, step):
    pairs = []
    for y in range(RING):
        for plane in range(PLANES):
            for core in range(CORES):
                pairs.append((place(y, plane, core), place(*step(y, plane, core))))
    return lax.ppermute(value, "tensor", pairs)


def around(value):
    return moved(value, lambda y, plane, core: ((y + 1 - 2 * core) % RING, plane, core))


def across(value):
    return moved(value, lambda y, plane, core: (y, 1 - plane, core))


def to_sibling(value):
    return moved(value, lambda y, plane, core: (y, plane, 1 - core))


def mirrored(value):
    count = lax.axis_size("pipe")
    return lax.ppermute(value, "pipe", [(i, count - 1 - i) for i in range(count)])


def from_behind(value, by, other):
    count, group = lax.axis_size("pipe"), lax.axis_size("tensor")
    pairs = []
    for i in range(count):
        if 0 <= i + by < count:
            for t in range(group):
                target = t + 1 - 2 * (t % CORES) if other else t
                pairs.append((i * group + t, (i + by) * group + target))
    return lax.ppermute(value, ("pipe", "tensor"), pairs)


def after(value, *earlier):
    return lax.optimization_barrier((value, *earlier))[0]


def origin(key):
    t = lax.axis_index("tensor")
    hop, dz, dc = key
    core = t % CORES
    plane = (t // CORES) % PLANES
    y = t // (CORES * PLANES)
    if dc:
        core = 1 - core
    if dz:
        plane = 1 - plane
    y = (y + RING - hop + 2 * hop * core) % RING
    return y, plane, core


def back_kernel(*refs):
    n = len(NEAR)
    blocks = refs[:n], refs[n : 2 * n]
    own_w, sib_w, own0, own1, sib0, sib1, whole, held, bsems, wsems = refs[2 * n :]
    rows = blocks[0][0].shape[0]
    copies = []
    for r in range(2):
        copies.append(pltpu.make_async_copy(own_w.at[r], held.at[r, 0], wsems.at[r, 0]))
        copies.append(pltpu.make_async_copy(sib_w.at[r], held.at[r, 1], wsems.at[r, 1]))
    for i, key in enumerate(NEAR):
        y, plane, _ = origin(key)
        start = pl.multiple_of((y * PLANES + plane) * rows, rows)
        for r in range(2):
            copies.append(
                pltpu.make_async_copy(
                    blocks[r][i], whole.at[r, pl.ds(start, rows), :], bsems.at[r, i]
                )
            )
    for copy in copies:
        copy.start()
    for copy in copies:
        copy.wait()
    for r, outs in enumerate(((own0, sib0), (own1, sib1))):
        for which, out in enumerate(outs):
            out[...] = lax.dot_general(
                whole[r], held[r, which], (((1,), (1,)), ((), ())),
                preferred_element_type=jnp.float32,
            ).astype(out.dtype)


def sum_kernel(*refs):
    n, m = len(NEAR), len(EARLY)
    near, far = refs[:n], refs[n : n + m]
    near_own, near_sib, far_own, far_sib, own, sib, whole, upright, flat, bsems, csems = refs[n + m :]
    rows = far[0].shape[0]
    width = near_own.shape[1]
    copies = []
    for i, block in enumerate(near + far):
        copies.append(
            pltpu.make_async_copy(block, whole.at[pl.ds(i * rows, rows), :], bsems.at[i])
        )
    for j, (a, b) in enumerate(((near_own, far_own), (near_sib, far_sib))):
        for i, key in enumerate(NEAR + EARLY):
            start = pl.multiple_of(place(*origin(key)) * rows, rows)
            source = a if i < n else b
            copies.append(
                pltpu.make_async_copy(
                    source.at[pl.ds(start, rows), :],
                    upright.at[j, pl.ds(i * rows, rows), :],
                    csems.at[j, i],
                )
            )
    for copy in copies:
        copy.start()
    for copy in copies:
        copy.wait()
    wide = 512
    for j, out in ((1, sib), (0, own)):
        flat[...] = upright[j].T

        @pl.loop(0, out.shape[1] // wide)
        def _(i, out=out):
            cols = pl.ds(pl.multiple_of(i * wide, wide), wide)
            out[:, cols] = jnp.dot(
                flat[...], whole[:, cols], preferred_element_type=jnp.float32
            )


def last_kernel(*refs):
    n = len(LATE)
    blocks = refs[:n]
    context, mine, theirs, out, whole, upright, flat, bsems, csems = refs[n:]
    rows = blocks[0].shape[0]
    copies = []
    for i, key in enumerate(LATE):
        start = pl.multiple_of(place(*origin(key)) * rows, rows)
        copies.append(
            pltpu.make_async_copy(
                context.at[pl.ds(start, rows), :],
                upright.at[pl.ds(i * rows, rows), :],
                csems.at[i],
            )
        )
        copies.append(
            pltpu.make_async_copy(blocks[i], whole.at[pl.ds(i * rows, rows), :], bsems.at[i])
        )
    for copy in copies:
        copy.start()
    for copy in copies:
        copy.wait()
    flat[...] = upright[...].T
    wide = 512

    @pl.loop(0, out.shape[1] // wide)
    def _(i):
        cols = pl.ds(pl.multiple_of(i * wide, wide), wide)
        out[:, cols] = (
            mine[:, cols]
            + theirs[:, cols]
            + jnp.dot(flat[...], whole[:, cols], preferred_element_type=jnp.float32)
        ).astype(out.dtype)


def interleaved(same, other):
    core = lax.axis_index("tensor") % CORES
    a = same.reshape(RING * PLANES, -1, same.shape[1])
    b = other.reshape(RING * PLANES, -1, same.shape[1])
    even = jnp.where(core == 0, a, b)
    odd = jnp.where(core == 0, b, a)
    return jnp.stack([even, odd], axis=1).reshape(-1, same.shape[1])


def shards(section_weights, context, grad_out):
    width_in = context.shape[3]
    rows, width_out = grad_out.shape[2:]
    own_w = section_weights[0]
    near_own = context[0, 0]
    held = {("A", 0, 0): grad_out[0, 0], ("B", 0, 0): grad_out[0, 1]}
    held["M", 0, 0] = mirrored(held["B", 0, 0])
    for name in "AB":
        held[name, 0, 1] = across(held[name, 0, 0])
    sib_w = to_sibling(own_w)
    near_sib = to_sibling(near_own)
    far_own = mirrored(context[0, 1])
    order = [(name, hop, dz) for dz in range(PLANES) for hop in HOPS[1:] for name in "AB"]
    order += [("M", hop, dz) for hop in HOPS[1:] for dz in range(PLANES)]
    waits = {
        ("B", 3, 0): ("A", 0, 1),
        ("A", 1, 1): ("B", 0, 1),
        ("A", 2, 1): ("M", 0, 0),
        ("B", 3, 1): ("M", 0, 1),
    }
    for i, key in enumerate(order):
        name, hop, dz = key
        earlier = [held[order[i - 2]]] if i > 1 else []
        if key in waits:
            earlier.append(held[waits[key]])
        if key == ("M", 1, 0):
            earlier.append(far_own)
        held[key] = around(after(held[name, hop - 1, dz], *earlier))
        if key == ("A", 2, 1):
            held["M", 0, 1] = across(held["M", 0, 0])
        if key == ("M", 1, 0):
            far_sib = to_sibling(far_own)

    half = RING * PLANES * rows
    back_shape = jax.ShapeDtypeStruct((half, width_in), jnp.bfloat16)
    own0, own1, sib0, sib1 = pl.pallas_call(
        back_kernel,
        out_shape=(back_shape,) * 4,
        in_specs=[ANY] * (2 * len(NEAR) + 2),
        out_specs=(VMEM,) * 4,
        scratch_shapes=[
            pltpu.VMEM((2, half, width_out), jnp.bfloat16),
            pltpu.VMEM((2, 2, width_in, width_out), jnp.bfloat16),
            pltpu.SemaphoreType.DMA((2, len(NEAR))),
            pltpu.SemaphoreType.DMA((2, 2)),
        ],
        compiler_params=pltpu.CompilerParams(vmem_limit_bytes=24 * 2**20),
        cost_estimate=pl.CostEstimate(
            flops=8 * half * width_in * width_out,
            bytes_accessed=4 * (half + 2 * width_in) * width_out,
            transcendentals=0,
        ),
    )(*(held[name, *key[:2]] for name in "AB" for key in NEAR), own_w, sib_w)

    sum_shape = jax.ShapeDtypeStruct((width_in, width_out), jnp.float32)
    count = len(NEAR) + len(EARLY)
    mine, for_sibling = pl.pallas_call(
        sum_kernel,
        out_shape=(sum_shape,) * 2,
        in_specs=[ANY] * (count + 4),
        out_specs=(VMEM,) * 2,
        scratch_shapes=[
            pltpu.VMEM((count * rows, width_out), jnp.bfloat16),
            pltpu.VMEM((2, count * rows, width_in), jnp.bfloat16),
            pltpu.VMEM((width_in, count * rows), jnp.bfloat16),
            pltpu.SemaphoreType.DMA((count,)),
            pltpu.SemaphoreType.DMA((2, count)),
        ],
        compiler_params=pltpu.CompilerParams(vmem_limit_bytes=24 * 2**20),
        cost_estimate=pl.CostEstimate(
            flops=4 * count * rows * width_in * width_out,
            bytes_accessed=(2 * count * rows + 8 * width_in) * width_out,
            transcendentals=0,
        ),
    )(
        *(held["A", *key[:2]] for key in NEAR),
        *(held["M", *key[:2]] for key in EARLY),
        near_own, near_sib, far_own, after(far_sib, own0),
    )
    theirs = to_sibling(for_sibling)

    late = []
    for key in LATE:
        value = held["M", *key[:2]]
        late.append(to_sibling(value) if key[2] else value)
    count = len(LATE)
    weight_grad = pl.pallas_call(
        last_kernel,
        out_shape=jax.ShapeDtypeStruct((width_in, width_out), jnp.bfloat16),
        in_specs=[ANY] * (count + 1) + [VMEM, VMEM],
        out_specs=VMEM,
        scratch_shapes=[
            pltpu.VMEM((count * rows, width_out), jnp.bfloat16),
            pltpu.VMEM((count * rows, width_in), jnp.bfloat16),
            pltpu.VMEM((width_in, count * rows), jnp.bfloat16),
            pltpu.SemaphoreType.DMA((count,)),
            pltpu.SemaphoreType.DMA((count,)),
        ],
        compiler_params=pltpu.CompilerParams(vmem_limit_bytes=24 * 2**20),
        cost_estimate=pl.CostEstimate(
            flops=2 * count * rows * width_in * width_out,
            bytes_accessed=(2 * count * rows + 10 * width_in) * width_out,
            transcendentals=0,
        ),
    )(*late, far_own, mine, theirs)

    from_next = interleaved(from_behind(own0, -1, False), from_behind(sib0, -1, True))
    from_prior = interleaved(from_behind(own1, 1, False), from_behind(sib1, 1, True))
    input_grad = jnp.stack([from_next, from_prior])[None]
    return (weight_grad[None], input_grad)


def solution(mesh):
    placed = (
        P("pipe", None, "tensor", None),
        P("pipe", None, None, "tensor"),
        P("pipe", None, "tensor", None),
    )
    return jax.shard_map(
        shards,
        mesh=mesh,
        in_specs=placed,
        out_specs=(P("pipe", "tensor", None), P("pipe", None, None, "tensor")),
        check_vma=False,
    )
```

time: 350 us -> 160 us (0.46)
  the two profiles are of different devices: /device:TPU:58 before, /device:TPU:27 now
where the time goes in v2:
time: 160 us; the launch traced here: 159 us
  starting transfers between devices  62 us (39%)
  waiting for transfers between devices  61.9 us (39%)
  Pallas kernels  26.9 us (17%)
  local copies, waits for them, and re-layouts  6.61 us (4%)
    ppermute x29, waiting for transfers between devices, moved(): return lax.ppermute(value, 'tensor', pairs)  32.4 us
    ppermute x29, starting transfers between devices, moved(): return lax.ppermute(value, 'tensor', pairs)  31.5 us
    ppermute x4, starting transfers between devices, from_behind(): return lax.ppermute(value, ('pipe', 'tensor'), pairs)  19.3 us
    ppermute x2, waiting for transfers between devices, mirrored(): lax.ppermute(value, 'pipe', [(i, count - 1 - i) for i in range(count)])  17.8 us
    ppermute x4, waiting for transfers between devices, from_behind(): return lax.ppermute(value, ('pipe', 'tensor'), pairs)  11.7 us
    pallas_call x1, Pallas kernels, shards(): pl.pallas_call(sum_kernel, out_shape=(sum_shape,) * 2, in_specs=[ANY] * (...  11.4 us
    ppermute x2, starting transfers between devices, mirrored(): lax.ppermute(value, 'pipe', [(i, count - 1 - i) for i in range(count)])  11.2 us
    pallas_call x1, Pallas kernels, shards(): pl.pallas_call(last_kernel, out_shape=jax.ShapeDtypeStruct((width_in, wid...  8.03 us
  transfers between devices with their start and end apart: 35, of which 16 were waited for; matrix products, arithmetic and copies ran while one was open for 2% of the time, Pallas kernels for 5%

profile of v2, /device:TPU:27, one launch (start us, length us, event | category | flops | bytes accessed | tf_op | source)
XLA Modules:
  0.0 159.5 jit_solution(16123514292538125411)
XLA Ops:
  0.6 0.8 collective-permute-start.29
  1.4 1.2 slice_bitcast_fusion.2
  2.6 0.5 collective-permute-start.2
  3.1 0.2 collective-permute-start.14
  3.3 7.2 %collective-permute-done.2.refs_1_ = bf16[48,4096]{1,0:T(8,128)(2,1)S(1)} collective-permute-done((bf16[48,4096]{1,0:T(8,128)(2,1)S(1)}, bf16[48,4096]{1,0:T(8,128)(2,1)S(1)}, u32[]{:S(2)}, u32[]{:S(2)}) %collective-permute-start.2) | collective-permute-done | bytes 393248 | tf_op jit(solution)/shard_map/ppermute | solution.py:29
  10.5 1.6 %collective-permute-start.1 = (bf16[48,4096]{1,0:T(8,128)(2,1)S(1)}, bf16[48,4096]{1,0:T(8,128)(2,1)S(1)}, u32[]{:S(2)}, u32[]{:S(2)}) collective-permute-start(bf16[48,4096]{1,0:T(8,128)(2,1)S(1)} %get-tuple-element.50.refs_0_), channel_id=1, source_target_pairs={{0,2},{1,3},{2,0},{3,1},{4,6},{5,7},{6,4},{7,5},{8,10},{9,11},{10,... | collective-permute-start | bytes 1179656 | tf_op jit(solution)/shard_map/ppermute | solution.py:29
  12.1 2.6 %collective-permute-done.14.refs_9_ = bf16[48,4096]{1,0:T(8,128)(2,1)S(1)} collective-permute-done((bf16[48,4096]{1,0:T(8,128)(2,1)S(1)}, bf16[48,4096]{1,0:T(8,128)(2,1)S(1)}, u32[]{:S(2)}, u32[]{:S(2)}) %collective-permute-start.14) | collective-permute-done | bytes 393248 | tf_op jit(solution)/shard_map/ppermute | solution.py:29
  14.7 1.6 %collective-permute-start.5 = (bf16[48,4096]{1,0:T(8,128)(2,1)S(1)}, bf16[48,4096]{1,0:T(8,128)(2,1)S(1)}, u32[]{:S(2)}, u32[]{:S(2)}) collective-permute-start(bf16[48,4096]{1,0:T(8,128)(2,1)S(1)} %get-tuple-element.51.refs_8_), channel_id=1, source_target_pairs={{0,2},{1,3},{2,0},{3,1},{4,6},{5,7},{6,4},{7,5},{8,10},{9,11},{10,... | collective-permute-start | bytes 1179656 | tf_op jit(solution)/shard_map/ppermute | solution.py:29
  16.3 2.6 %collective-permute-done.3.refs_2_ = bf16[48,4096]{1,0:T(8,128)(2,1)S(1)} collective-permute-done((bf16[48,4096]{1,0:T(8,128)(2,1)S(1)}, bf16[48,4096]{1,0:T(8,128)(2,1)S(1)}, u32[]{:S(2)}, u32[]{:S(2)}) %collective-permute-start.3) | collective-permute-done | bytes 393248 | tf_op jit(solution)/shard_map/ppermute | solution.py:29
  18.9 1.1 collective-permute-done.1.refs_4_
  20.1 3.1 %collective-permute-done.15.refs_10_ = bf16[48,4096]{1,0:T(8,128)(2,1)S(1)} collective-permute-done((bf16[48,4096]{1,0:T(8,128)(2,1)S(1)}, bf16[48,4096]{1,0:T(8,128)(2,1)S(1)}, u32[]{:S(2)}, u32[]{:S(2)}) %collective-permute-start.15) | collective-permute-done | bytes 393248 | tf_op jit(solution)/shard_map/ppermute | solution.py:29
  23.1 6.9 %collective-permute-start = (bf16[48,4096]{1,0:T(8,128)(2,1)S(1)}, bf16[48,4096]{1,0:T(8,128)(2,1)S(1)}, u32[]{:S(2)}, u32[]{:S(2)}) collective-permute-start(bf16[48,4096]{1,0:T(8,128)(2,1)S(1)} %get-tuple-element.51.refs_8_), channel_id=1, source_target_pairs={{0,240},{16,224},{32,208},{48,192},{64,176},{80,160},{96,144},{112... | collective-permute-start | bytes 1179656 | tf_op jit(solution)/shard_map/ppermute | solution.py:46
  30.1 0.0 collective-permute-done.5.refs_12_
  30.1 0.0 collective-permute-done.4.refs_3_
  30.1 0.0 collective-permute-start.6
  30.1 1.5 collective-permute-done.16.refs_11_
  31.5 0.5 collective-permute-start.17
  32.1 14.7 %collective-permute-done.refs_8_ = bf16[48,4096]{1,0:T(8,128)(2,1)S(1)} collective-permute-done((bf16[48,4096]{1,0:T(8,128)(2,1)S(1)}, bf16[48,4096]{1,0:T(8,128)(2,1)S(1)}, u32[]{:S(2)}, u32[]{:S(2)}) %collective-permute-start) | collective-permute-done | bytes 393248 | tf_op jit(solution)/shard_map/ppermute | solution.py:46
  46.8 0.0 collective-permute-done.6.refs_5_
  46.8 0.0 collective-permute-start.7
  46.8 0.0 collective-permute-start.13
  46.8 3.0 %collective-permute-start.18 = (bf16[48,4096]{1,0:T(8,128)(2,1)S(1)}, bf16[48,4096]{1,0:T(8,128)(2,1)S(1)}, u32[]{:S(2)}, u32[]{:S(2)}) collective-permute-start(bf16[48,4096]{1,0:T(8,128)(2,1)S(1)} %collective-permute-done.17.refs_13_), channel_id=1, source_target_pairs={{0,4},{1,13},{2,6},{3,15},{4,8},{5,1},{6,10},{7,3},{8,12},{9,5},{1... | collective-permute-start | bytes 1179656 | tf_op jit(solution)/shard_map/ppermute | solution.py:29
  49.8 1.2 slice_bitcast_fusion
  51.0 4.3 %collective-permute-start.9 = (bf16[768,256]{1,0:T(8,128)(2,1)S(1)}, bf16[768,256]{1,0:T(8,128)(2,1)S(1)}, u32[]{:S(2)}, u32[]{:S(2)}) collective-permute-start(bf16[768,256]{1,0:T(8,128)(2,1)S(1)} %get-tuple-element.49), channel_id=1, source_target_pairs={{0,240},{16,224},{32,208},{48,192},{64,176},{80,160},{96,144},{112... | collective-permute-start | bytes 1179656 | tf_op jit(solution)/shard_map/ppermute | solution.py:46
  55.3 0.0 collective-permute-done.7.refs_6_
  55.3 1.9 %collective-permute-start.8 = (bf16[48,4096]{1,0:T(8,128)(2,1)S(1)}, bf16[48,4096]{1,0:T(8,128)(2,1)S(1)}, u32[]{:S(2)}, u32[]{:S(2)}) collective-permute-start(bf16[48,4096]{1,0:T(8,128)(2,1)S(1)} %collective-permute-done.7.refs_6_), channel_id=1, source_target_pairs={{0,4},{1,13},{2,6},{3,15},{4,8},{5,1},{6,10},{7,3},{8,12},{9,5},{1... | collective-permute-start | bytes 1179656 | tf_op jit(solution)/shard_map/ppermute | solution.py:29
  57.2 0.0 collective-permute-done.13.refs_10_
  57.2 2.0 %collective-permute-done.18.refs_14_ = bf16[48,4096]{1,0:T(8,128)(2,1)S(1)} collective-permute-done((bf16[48,4096]{1,0:T(8,128)(2,1)S(1)}, bf16[48,4096]{1,0:T(8,128)(2,1)S(1)}, u32[]{:S(2)}, u32[]{:S(2)}) %collective-permute-start.18) | collective-permute-done | bytes 393248 | tf_op jit(solution)/shard_map/ppermute | solution.py:29
  59.2 0.0 collective-permute-start.19
  59.2 8.8 %collective-permute-start.27 = (bf16[768,256]{1,0:T(8,128)(2,1)S(1)}, bf16[768,256]{1,0:T(8,128)(2,1)S(1)}, u32[]{:S(2)}, u32[]{:S(2)}) collective-permute-start(bf16[768,256]{1,0:T(8,128)(2,1)S(1)} %get-tuple-element.48.refs_12_), channel_id=1, source_target_pairs={{0,1},{1,0},{2,3},{3,2},{4,5},{5,4},{6,7},{7,6},{8,9},{9,8},{10,11... | collective-permute-start | bytes 1179656 | tf_op jit(solution)/shard_map/ppermute | solution.py:29
  68.1 3.1 %collective-permute-done.9.refs_14_.refs_8_ = bf16[768,256]{1,0:T(8,128)(2,1)S(1)} collective-permute-done((bf16[768,256]{1,0:T(8,128)(2,1)S(1)}, bf16[768,256]{1,0:T(8,128)(2,1)S(1)}, u32[]{:S(2)}, u32[]{:S(2)}) %collective-permute-start.9) | collective-permute-done | bytes 393248 | tf_op jit(solution)/shard_map/ppermute | solution.py:46
  71.2 1.9 %collective-permute-start.28 = (bf16[768,256]{1,0:T(8,128)(2,1)S(1)}, bf16[768,256]{1,0:T(8,128)(2,1)S(1)}, u32[]{:S(2)}, u32[]{:S(2)}) collective-permute-start(bf16[768,256]{1,0:T(8,128)(2,1)S(1)} %collective-permute-done.9.refs_14_.refs_8_), channel_id=1, source_target_pairs={{0,1},{1,0},{2,3},{3,2},{4,5},{5,4},{6,7},{7,6},{8,9},{9,8},{10,11... | collective-permute-start | bytes 1179656 | tf_op jit(solution)/shard_map/ppermute | solution.py:29
  73.1 1.9 %collective-permute-start.10 = (bf16[48,4096]{1,0:T(8,128)(2,1)S(1)}, bf16[48,4096]{1,0:T(8,128)(2,1)S(1)}, u32[]{:S(2)}, u32[]{:S(2)}) collective-permute-start(bf16[48,4096]{1,0:T(8,128)(2,1)S(1)} %collective-permute-done.refs_8_), channel_id=1, source_target_pairs={{0,4},{1,13},{2,6},{3,15},{4,8},{5,1},{6,10},{7,3},{8,12},{9,5},{1... | collective-permute-start | bytes 1179656 | tf_op jit(solution)/shard_map/ppermute | solution.py:29
  74.9 0.1 collective-permute-start.20
  75.1 2.2 %copy-done = bf16[1,2,256,4096]{3,2,1,0:T(8,128)(2,1)S(1)} copy-done((bf16[1,2,256,4096]{3,2,1,0:T(8,128)(2,1)S(1)}, bf16[1,2,256,4096]{3,2,1,0:T(8,128)(2,1)}, u32[]{:S(2)}) %copy-start) | copy-done | bytes 4194328
  77.3 7.5 %shard_map.50 = (bf16[384,256]{1,0:T(8,128)(2,1)S(1)}, bf16[384,256]{1,0:T(8,128)(2,1)S(1)}, bf16[384,256]{1,0:T(8,128)(2,1)S(1)}, bf16[384,256]{1,0:T(8,128)(2,1)S(1)}) custom-call(bf16[48,4096]{1,0:T(8,128)(2,1)S(1)} %get-tuple-element.50.refs_0_, bf16[48,4096]{1,0:T(8,128)(2,1)S(1)} %collective-permute-done.2.refs_1_, ...), custom_call_target="tpu_custom_call" | custom-call | flops 3221225472 | bytes 14680064 | tf_op jit(solution)/shard_map/pallas_call | solution.py:225
  84.8 0.0 collective-permute-done.27.refs_13_
  84.8 0.0 collective-permute-done.10.refs_9_
  84.8 0.3 collective-permute-done.20.refs_11_
  85.1 11.4 %shard_map.51 = (f32[256,4096]{1,0:T(8,128)S(1)}, f32[256,4096]{1,0:T(8,128)}) custom-call(bf16[48,4096]{1,0:T(8,128)(2,1)S(1)} %get-tuple-element.50.refs_0_, bf16[48,4096]{1,0:T(8,128)(2,1)S(1)} %collective-permute-done.2.refs_1_, bf16[48,4096]{1,0:T(8,128)(2,1)S(1)} %collective-permute-done.3.refs_2_, ...), custom_call_target="tpu_custom_call" | custom-call | flops 2415919104 | bytes 13107200 | tf_op jit(solution)/shard_map/pallas_call | solution.py:246
  96.5 2.0 %copy-done.1 = f32[256,4096]{1,0:T(8,128)} copy-done((f32[256,4096]{1,0:T(8,128)}, f32[256,4096]{1,0:T(8,128)S(1)}, u32[]{:S(2)}) %copy-start.1) | copy-done | bytes 4194328
  98.5 1.7 %collective-permute-start.30 = (f32[256,4096]{1,0:T(8,128)}, f32[256,4096]{1,0:T(8,128)}, u32[]{:S(2)}, u32[]{:S(2)}) collective-permute-start(f32[256,4096]{1,0:T(8,128)} %get-tuple-element.44), channel_id=1, source_target_pairs={{0,1},{1,0},{2,3},{3,2},{4,5},{5,4},{6,7},{7,6},{8,9},{9,8},{10,11... | collective-permute-start | bytes 12582920 | tf_op jit(solution)/shard_map/ppermute | solution.py:29
  100.2 0.1 collective-permute-start.11
  100.4 0.1 collective-permute-start.21
  100.5 7.6 %collective-permute-done.11.refs_0_ = bf16[48,4096]{1,0:T(8,128)(2,1)S(1)} collective-permute-done((bf16[48,4096]{1,0:T(8,128)(2,1)S(1)}, bf16[48,4096]{1,0:T(8,128)(2,1)S(1)}, u32[]{:S(2)}, u32[]{:S(2)}) %collective-permute-start.11) | collective-permute-done | bytes 393248 | tf_op jit(solution)/shard_map/ppermute | solution.py:29
  108.1 0.0 collective-permute-start.23
  108.1 4.2 %collective-permute-done.21.refs_2_ = bf16[48,4096]{1,0:T(8,128)(2,1)S(1)} collective-permute-done((bf16[48,4096]{1,0:T(8,128)(2,1)S(1)}, bf16[48,4096]{1,0:T(8,128)(2,1)S(1)}, u32[]{:S(2)}, u32[]{:S(2)}) %collective-permute-start.21) | collective-permute-done | bytes 393248 | tf_op jit(solution)/shard_map/ppermute | solution.py:29
  112.3 0.0 collective-permute-start.25
  112.3 7.8 %collective-permute-start.31 = (bf16[384,256]{1,0:T(8,128)(2,1)S(1)}, bf16[384,256]{1,0:T(8,128)(2,1)S(1)}, u32[]{:S(2)}, u32[]{:S(2)}) collective-permute-start(bf16[384,256]{1,0:T(8,128)(2,1)S(1)} %get-tuple-element.41), channel_id=1, source_target_pairs={{16,0},{17,1},{18,2},{19,3},{20,4},{21,5},{22,6},{23,7},{24,8},{25... | collective-permute-start | bytes 589832 | tf_op jit(solution)/shard_map/ppermute | solution.py:57
  120.1 5.1 %collective-permute-start.32 = (bf16[384,256]{1,0:T(8,128)(2,1)S(1)}, bf16[384,256]{1,0:T(8,128)(2,1)S(1)}, u32[]{:S(2)}, u32[]{:S(2)}) collective-permute-start(bf16[384,256]{1,0:T(8,128)(2,1)S(1)} %get-tuple-element.45), channel_id=1, source_target_pairs={{16,1},{17,0},{18,3},{19,2},{20,5},{21,4},{22,7},{23,6},{24,9},{25... | collective-permute-start | bytes 589832 | tf_op jit(solution)/shard_map/ppermute | solution.py:57
  125.2 0.0 collective-permute-done.23.refs_4_
  125.2 4.5 %collective-permute-start.33 = (bf16[384,256]{1,0:T(8,128)(2,1)S(1)}, bf16[384,256]{1,0:T(8,128)(2,1)S(1)}, u32[]{:S(2)}, u32[]{:S(2)}) collective-permute-start(bf16[384,256]{1,0:T(8,128)(2,1)S(1)} %get-tuple-element.46), channel_id=1, source_target_pairs={{0,16},{1,17},{2,18},{3,19},{4,20},{5,21},{6,22},{7,23},{8,24},{9,... | collective-permute-start | bytes 589832 | tf_op jit(solution)/shard_map/ppermute | solution.py:57
  129.8 1.9 %collective-permute-start.34 = (bf16[384,256]{1,0:T(8,128)(2,1)S(1)}, bf16[384,256]{1,0:T(8,128)(2,1)S(1)}, u32[]{:S(2)}, u32[]{:S(2)}) collective-permute-start(bf16[384,256]{1,0:T(8,128)(2,1)S(1)} %get-tuple-element.47), channel_id=1, source_target_pairs={{0,17},{1,16},{2,19},{3,18},{4,21},{5,20},{6,23},{7,22},{8,25},{9,... | collective-permute-start | bytes 589832 | tf_op jit(solution)/shard_map/ppermute | solution.py:57
  131.7 0.5 collective-permute-start.12
  132.2 1.6 %collective-permute-done.32 = bf16[384,256]{1,0:T(8,128)(2,1)S(1)} collective-permute-done((bf16[384,256]{1,0:T(8,128)(2,1)S(1)}, bf16[384,256]{1,0:T(8,128)(2,1)S(1)}, u32[]{:S(2)}, u32[]{:S(2)}) %collective-permute-start.32) | collective-permute-done | bytes 196640 | tf_op jit(solution)/shard_map/ppermute | solution.py:57
  133.8 1.8 %collective-permute-start.22 = (bf16[48,4096]{1,0:T(8,128)(2,1)S(1)}, bf16[48,4096]{1,0:T(8,128)(2,1)S(1)}, u32[]{:S(2)}, u32[]{:S(2)}) collective-permute-start(bf16[48,4096]{1,0:T(8,128)(2,1)S(1)} %collective-permute-done.21.refs_2_), channel_id=1, source_target_pairs={{0,1},{1,0},{2,3},{3,2},{4,5},{5,4},{6,7},{7,6},{8,9},{9,8},{10,11... | collective-permute-start | bytes 1179656 | tf_op jit(solution)/shard_map/ppermute | solution.py:29
  135.6 5.2 %collective-permute-done.33 = bf16[384,256]{1,0:T(8,128)(2,1)S(1)} collective-permute-done((bf16[384,256]{1,0:T(8,128)(2,1)S(1)}, bf16[384,256]{1,0:T(8,128)(2,1)S(1)}, u32[]{:S(2)}, u32[]{:S(2)}) %collective-permute-start.33) | collective-permute-done | bytes 196640 | tf_op jit(solution)/shard_map/ppermute | solution.py:57
  140.8 3.8 %collective-permute-start.24 = (bf16[48,4096]{1,0:T(8,128)(2,1)S(1)}, bf16[48,4096]{1,0:T(8,128)(2,1)S(1)}, u32[]{:S(2)}, u32[]{:S(2)}) collective-permute-start(bf16[48,4096]{1,0:T(8,128)(2,1)S(1)} %collective-permute-done.23.refs_4_), channel_id=1, source_target_pairs={{0,1},{1,0},{2,3},{3,2},{4,5},{5,4},{6,7},{7,6},{8,9},{9,8},{10,11... | collective-permute-start | bytes 1179656 | tf_op jit(solution)/shard_map/ppermute | solution.py:29
  144.7 4.8 %collective-permute-done.34 = bf16[384,256]{1,0:T(8,128)(2,1)S(1)} collective-permute-done((bf16[384,256]{1,0:T(8,128)(2,1)S(1)}, bf16[384,256]{1,0:T(8,128)(2,1)S(1)}, u32[]{:S(2)}, u32[]{:S(2)}) %collective-permute-start.34) | collective-permute-done | bytes 196640 | tf_op jit(solution)/shard_map/ppermute | solution.py:57
  149.5 0.4 collective-permute-start.26
  149.9 0.1 broadcast_select_fusion.1
  150.1 0.9 maximum_bitcast_fusion
  151.1 0.2 collective-permute-done.26.refs_7_
  151.3 8.0 %shard_map.52 = bf16[256,4096]{1,0:T(8,128)(2,1)} custom-call(bf16[48,4096]{1,0:T(8,128)(2,1)S(1)} %collective-permute-done.11.refs_0_, bf16[48,4096]{1,0:T(8,128)(2,1)S(1)} %collective-permute-done.12.refs_1_, bf16[48,4096]{1,0:T(8,128)(2,1)S(1)} %collective-permute-done.21.refs_2_, bf16[48,4096]{1,0:T(8,128)(2,1)S(1)} %collective-permute-done.22.refs_3_, ...), custom_call_target="tpu_custom_call" | custom-call | flops 805306368 | bytes 13631488 | tf_op jit(solution)/shard_map/pallas_call | solution.py:276
  (23 shorter events, 0.2 us)
Async XLA Ops:
  0.6 74.5 %collective-permute-start.29 = (bf16[2,256,4096]{2,1,0:T(8,128)(2,1)}, bf16[2,256,4096]{2,1,0:T(8,128)(2,1)S(1)}, u32[]{:S(2)}, u32[]{:S(2)}) collective-permute-start(bf16[2,256,4096]{2,1,0:T(8,128)(2,1)} %bitcast.18), channel_id=1, source_target_pairs={{0,1},{1,0},{2,3},{3,2},{4,5},{5,4},{6,7},{7,6},{8,9},{9,8},{10,11... | collective-permute-start | bytes 12582920 | tf_op jit(solution)/shard_map/ppermute | solution.py:29
  2.6 7.9 %collective-permute-start.2 = (bf16[48,4096]{1,0:T(8,128)(2,1)S(1)}, bf16[48,4096]{1,0:T(8,128)(2,1)S(1)}, u32[]{:S(2)}, u32[]{:S(2)}) collective-permute-start(bf16[48,4096]{1,0:T(8,128)(2,1)S(1)} %get-tuple-element.50.refs_0_), channel_id=1, source_target_pairs={{0,4},{1,13},{2,6},{3,15},{4,8},{5,1},{6,10},{7,3},{8,12},{9,5},{1... | collective-permute-start | bytes 1179656 | tf_op jit(solution)/shard_map/ppermute | solution.py:29
  3.1 11.6 %collective-permute-start.14 = (bf16[48,4096]{1,0:T(8,128)(2,1)S(1)}, bf16[48,4096]{1,0:T(8,128)(2,1)S(1)}, u32[]{:S(2)}, u32[]{:S(2)}) collective-permute-start(bf16[48,4096]{1,0:T(8,128)(2,1)S(1)} %get-tuple-element.51.refs_8_), channel_id=1, source_target_pairs={{0,4},{1,13},{2,6},{3,15},{4,8},{5,1},{6,10},{7,3},{8,12},{9,5},{1... | collective-permute-start | bytes 1179656 | tf_op jit(solution)/shard_map/ppermute | solution.py:29
  10.5 8.4 %collective-permute-start.3 = (bf16[48,4096]{1,0:T(8,128)(2,1)S(1)}, bf16[48,4096]{1,0:T(8,128)(2,1)S(1)}, u32[]{:S(2)}, u32[]{:S(2)}) collective-permute-start(bf16[48,4096]{1,0:T(8,128)(2,1)S(1)} %collective-permute-done.2.refs_1_), channel_id=1, source_target_pairs={{0,4},{1,13},{2,6},{3,15},{4,8},{5,1},{6,10},{7,3},{8,12},{9,5},{1... | collective-permute-start | bytes 1179656 | tf_op jit(solution)/shard_map/ppermute | solution.py:29
  10.5 9.6 %collective-permute-start.1 = (bf16[48,4096]{1,0:T(8,128)(2,1)S(1)}, bf16[48,4096]{1,0:T(8,128)(2,1)S(1)}, u32[]{:S(2)}, u32[]{:S(2)}) collective-permute-start(bf16[48,4096]{1,0:T(8,128)(2,1)S(1)} %get-tuple-element.50.refs_0_), channel_id=1, source_target_pairs={{0,2},{1,3},{2,0},{3,1},{4,6},{5,7},{6,4},{7,5},{8,10},{9,11},{10,... | collective-permute-start | bytes 1179656 | tf_op jit(solution)/shard_map/ppermute | solution.py:29
  14.7 8.4 %collective-permute-start.15 = (bf16[48,4096]{1,0:T(8,128)(2,1)S(1)}, bf16[48,4096]{1,0:T(8,128)(2,1)S(1)}, u32[]{:S(2)}, u32[]{:S(2)}) collective-permute-start(bf16[48,4096]{1,0:T(8,128)(2,1)S(1)} %collective-permute-done.14.refs_9_), channel_id=1, source_target_pairs={{0,4},{1,13},{2,6},{3,15},{4,8},{5,1},{6,10},{7,3},{8,12},{9,5},{1... | collective-permute-start | bytes 1179656 | tf_op jit(solution)/shard_map/ppermute | solution.py:29
  14.7 15.4 %collective-permute-start.5 = (bf16[48,4096]{1,0:T(8,128)(2,1)S(1)}, bf16[48,4096]{1,0:T(8,128)(2,1)S(1)}, u32[]{:S(2)}, u32[]{:S(2)}) collective-permute-start(bf16[48,4096]{1,0:T(8,128)(2,1)S(1)} %get-tuple-element.51.refs_8_), channel_id=1, source_target_pairs={{0,2},{1,3},{2,0},{3,1},{4,6},{5,7},{6,4},{7,5},{8,10},{9,11},{10,... | collective-permute-start | bytes 1179656 | tf_op jit(solution)/shard_map/ppermute | solution.py:29
  18.9 11.2 %collective-permute-start.4 = (bf16[48,4096]{1,0:T(8,128)(2,1)S(1)}, bf16[48,4096]{1,0:T(8,128)(2,1)S(1)}, u32[]{:S(2)}, u32[]{:S(2)}) collective-permute-start(bf16[48,4096]{1,0:T(8,128)(2,1)S(1)} %collective-permute-done.3.refs_2_), channel_id=1, source_target_pairs={{0,4},{1,13},{2,6},{3,15},{4,8},{5,1},{6,10},{7,3},{8,12},{9,5},{1... | collective-permute-start | bytes 1179656 | tf_op jit(solution)/shard_map/ppermute | solution.py:29
  23.1 8.4 %collective-permute-start.16 = (bf16[48,4096]{1,0:T(8,128)(2,1)S(1)}, bf16[48,4096]{1,0:T(8,128)(2,1)S(1)}, u32[]{:S(2)}, u32[]{:S(2)}) collective-permute-start(bf16[48,4096]{1,0:T(8,128)(2,1)S(1)} %collective-permute-done.15.refs_10_), channel_id=1, source_target_pairs={{0,4},{1,13},{2,6},{3,15},{4,8},{5,1},{6,10},{7,3},{8,12},{9,5},{1... | collective-permute-start | bytes 1179656 | tf_op jit(solution)/shard_map/ppermute | solution.py:29
  23.1 23.7 %collective-permute-start = (bf16[48,4096]{1,0:T(8,128)(2,1)S(1)}, bf16[48,4096]{1,0:T(8,128)(2,1)S(1)}, u32[]{:S(2)}, u32[]{:S(2)}) collective-permute-start(bf16[48,4096]{1,0:T(8,128)(2,1)S(1)} %get-tuple-element.51.refs_8_), channel_id=1, source_target_pairs={{0,240},{16,224},{32,208},{48,192},{64,176},{80,160},{96,144},{112... | collective-permute-start | bytes 1179656 | tf_op jit(solution)/shard_map/ppermute | solution.py:46
  30.1 16.7 %collective-permute-start.6 = (bf16[48,4096]{1,0:T(8,128)(2,1)S(1)}, bf16[48,4096]{1,0:T(8,128)(2,1)S(1)}, u32[]{:S(2)}, u32[]{:S(2)}) collective-permute-start(bf16[48,4096]{1,0:T(8,128)(2,1)S(1)} %collective-permute-done.1.refs_4_), channel_id=1, source_target_pairs={{0,4},{1,13},{2,6},{3,15},{4,8},{5,1},{6,10},{7,3},{8,12},{9,5},{1... | collective-permute-start | bytes 1179656 | tf_op jit(solution)/shard_map/ppermute | solution.py:29
  31.5 15.3 %collective-permute-start.17 = (bf16[48,4096]{1,0:T(8,128)(2,1)S(1)}, bf16[48,4096]{1,0:T(8,128)(2,1)S(1)}, u32[]{:S(2)}, u32[]{:S(2)}) collective-permute-start(bf16[48,4096]{1,0:T(8,128)(2,1)S(1)} %collective-permute-done.5.refs_12_), channel_id=1, source_target_pairs={{0,4},{1,13},{2,6},{3,15},{4,8},{5,1},{6,10},{7,3},{8,12},{9,5},{1... | collective-permute-start | bytes 1179656 | tf_op jit(solution)/shard_map/ppermute | solution.py:29
  46.8 8.5 %collective-permute-start.7 = (bf16[48,4096]{1,0:T(8,128)(2,1)S(1)}, bf16[48,4096]{1,0:T(8,128)(2,1)S(1)}, u32[]{:S(2)}, u32[]{:S(2)}) collective-permute-start(bf16[48,4096]{1,0:T(8,128)(2,1)S(1)} %collective-permute-done.6.refs_5_), channel_id=1, source_target_pairs={{0,4},{1,13},{2,6},{3,15},{4,8},{5,1},{6,10},{7,3},{8,12},{9,5},{1... | collective-permute-start | bytes 1179656 | tf_op jit(solution)/shard_map/ppermute | solution.py:29
  46.8 10.4 %collective-permute-start.13 = (bf16[48,4096]{1,0:T(8,128)(2,1)S(1)}, bf16[48,4096]{1,0:T(8,128)(2,1)S(1)}, u32[]{:S(2)}, u32[]{:S(2)}) collective-permute-start(bf16[48,4096]{1,0:T(8,128)(2,1)S(1)} %collective-permute-done.refs_8_), channel_id=1, source_target_pairs={{0,2},{1,3},{2,0},{3,1},{4,6},{5,7},{6,4},{7,5},{8,10},{9,11},{10,... | collective-permute-start | bytes 1179656 | tf_op jit(solution)/shard_map/ppermute | solution.py:29
  46.8 12.4 %collective-permute-start.18 = (bf16[48,4096]{1,0:T(8,128)(2,1)S(1)}, bf16[48,4096]{1,0:T(8,128)(2,1)S(1)}, u32[]{:S(2)}, u32[]{:S(2)}) collective-permute-start(bf16[48,4096]{1,0:T(8,128)(2,1)S(1)} %collective-permute-done.17.refs_13_), channel_id=1, source_target_pairs={{0,4},{1,13},{2,6},{3,15},{4,8},{5,1},{6,10},{7,3},{8,12},{9,5},{1... | collective-permute-start | bytes 1179656 | tf_op jit(solution)/shard_map/ppermute | solution.py:29
  51.0 20.1 %collective-permute-start.9 = (bf16[768,256]{1,0:T(8,128)(2,1)S(1)}, bf16[768,256]{1,0:T(8,128)(2,1)S(1)}, u32[]{:S(2)}, u32[]{:S(2)}) collective-permute-start(bf16[768,256]{1,0:T(8,128)(2,1)S(1)} %get-tuple-element.49), channel_id=1, source_target_pairs={{0,240},{16,224},{32,208},{48,192},{64,176},{80,160},{96,144},{112... | collective-permute-start | bytes 1179656 | tf_op jit(solution)/shard_map/ppermute | solution.py:46
  55.3 17.8 %collective-permute-start.8 = (bf16[48,4096]{1,0:T(8,128)(2,1)S(1)}, bf16[48,4096]{1,0:T(8,128)(2,1)S(1)}, u32[]{:S(2)}, u32[]{:S(2)}) collective-permute-start(bf16[48,4096]{1,0:T(8,128)(2,1)S(1)} %collective-permute-done.7.refs_6_), channel_id=1, source_target_pairs={{0,4},{1,13},{2,6},{3,15},{4,8},{5,1},{6,10},{7,3},{8,12},{9,5},{1... | collective-permute-start | bytes 1179656 | tf_op jit(solution)/shard_map/ppermute | solution.py:29
  59.2 15.7 %collective-permute-start.19 = (bf16[48,4096]{1,0:T(8,128)(2,1)S(1)}, bf16[48,4096]{1,0:T(8,128)(2,1)S(1)}, u32[]{:S(2)}, u32[]{:S(2)}) collective-permute-start(bf16[48,4096]{1,0:T(8,128)(2,1)S(1)} %collective-permute-done.18.refs_14_), channel_id=1, source_target_pairs={{0,4},{1,13},{2,6},{3,15},{4,8},{5,1},{6,10},{7,3},{8,12},{9,5},{1... | collective-permute-start | bytes 1179656 | tf_op jit(solution)/shard_map/ppermute | solution.py:29
  59.2 25.5 %collective-permute-start.27 = (bf16[768,256]{1,0:T(8,128)(2,1)S(1)}, bf16[768,256]{1,0:T(8,128)(2,1)S(1)}, u32[]{:S(2)}, u32[]{:S(2)}) collective-permute-start(bf16[768,256]{1,0:T(8,128)(2,1)S(1)} %get-tuple-element.48.refs_12_), channel_id=1, source_target_pairs={{0,1},{1,0},{2,3},{3,2},{4,5},{5,4},{6,7},{7,6},{8,9},{9,8},{10,11... | collective-permute-start | bytes 1179656 | tf_op jit(solution)/shard_map/ppermute | solution.py:29
  71.2 13.6 %collective-permute-start.28 = (bf16[768,256]{1,0:T(8,128)(2,1)S(1)}, bf16[768,256]{1,0:T(8,128)(2,1)S(1)}, u32[]{:S(2)}, u32[]{:S(2)}) collective-permute-start(bf16[768,256]{1,0:T(8,128)(2,1)S(1)} %collective-permute-done.9.refs_14_.refs_8_), channel_id=1, source_target_pairs={{0,1},{1,0},{2,3},{3,2},{4,5},{5,4},{6,7},{7,6},{8,9},{9,8},{10,11... | collective-permute-start | bytes 1179656 | tf_op jit(solution)/shard_map/ppermute | solution.py:29
  73.1 11.7 %collective-permute-start.10 = (bf16[48,4096]{1,0:T(8,128)(2,1)S(1)}, bf16[48,4096]{1,0:T(8,128)(2,1)S(1)}, u32[]{:S(2)}, u32[]{:S(2)}) collective-permute-start(bf16[48,4096]{1,0:T(8,128)(2,1)S(1)} %collective-permute-done.refs_8_), channel_id=1, source_target_pairs={{0,4},{1,13},{2,6},{3,15},{4,8},{5,1},{6,10},{7,3},{8,12},{9,5},{1... | collective-permute-start | bytes 1179656 | tf_op jit(solution)/shard_map/ppermute | solution.py:29
  74.9 10.2 %collective-permute-start.20 = (bf16[48,4096]{1,0:T(8,128)(2,1)S(1)}, bf16[48,4096]{1,0:T(8,128)(2,1)S(1)}, u32[]{:S(2)}, u32[]{:S(2)}) collective-permute-start(bf16[48,4096]{1,0:T(8,128)(2,1)S(1)} %collective-permute-done.13.refs_10_), channel_id=1, source_target_pairs={{0,4},{1,13},{2,6},{3,15},{4,8},{5,1},{6,10},{7,3},{8,12},{9,5},{1... | collective-permute-start | bytes 1179656 | tf_op jit(solution)/shard_map/ppermute | solution.py:29
  75.1 2.2 %copy-start = (bf16[1,2,256,4096]{3,2,1,0:T(8,128)(2,1)S(1)}, bf16[1,2,256,4096]{3,2,1,0:T(8,128)(2,1)}, u32[]{:S(2)}) copy-start(bf16[1,2,256,4096]{3,2,1,0:T(8,128)(2,1)} %param.3) | copy-start | bytes 12582916
  96.5 2.0 %copy-start.1 = (f32[256,4096]{1,0:T(8,128)}, f32[256,4096]{1,0:T(8,128)S(1)}, u32[]{:S(2)}) copy-start(f32[256,4096]{1,0:T(8,128)S(1)} %get-tuple-element.43.refs_9_) | copy-start | bytes 12582916
  98.5 52.7 %collective-permute-start.30 = (f32[256,4096]{1,0:T(8,128)}, f32[256,4096]{1,0:T(8,128)}, u32[]{:S(2)}, u32[]{:S(2)}) collective-permute-start(f32[256,4096]{1,0:T(8,128)} %get-tuple-element.44), channel_id=1, source_target_pairs={{0,1},{1,0},{2,3},{3,2},{4,5},{5,4},{6,7},{7,6},{8,9},{9,8},{10,11... | collective-permute-start | bytes 12582920 | tf_op jit(solution)/shard_map/ppermute | solution.py:29
  100.2 7.8 %collective-permute-start.11 = (bf16[48,4096]{1,0:T(8,128)(2,1)S(1)}, bf16[48,4096]{1,0:T(8,128)(2,1)S(1)}, u32[]{:S(2)}, u32[]{:S(2)}) collective-permute-start(bf16[48,4096]{1,0:T(8,128)(2,1)S(1)} %collective-permute-done.10.refs_9_), channel_id=1, source_target_pairs={{0,4},{1,13},{2,6},{3,15},{4,8},{5,1},{6,10},{7,3},{8,12},{9,5},{1... | collective-permute-start | bytes 1179656 | tf_op jit(solution)/shard_map/ppermute | solution.py:29
  100.4 11.9 %collective-permute-start.21 = (bf16[48,4096]{1,0:T(8,128)(2,1)S(1)}, bf16[48,4096]{1,0:T(8,128)(2,1)S(1)}, u32[]{:S(2)}, u32[]{:S(2)}) collective-permute-start(bf16[48,4096]{1,0:T(8,128)(2,1)S(1)} %collective-permute-done.20.refs_11_), channel_id=1, source_target_pairs={{0,4},{1,13},{2,6},{3,15},{4,8},{5,1},{6,10},{7,3},{8,12},{9,5},{1... | collective-permute-start | bytes 1179656 | tf_op jit(solution)/shard_map/ppermute | solution.py:29
  108.1 17.1 %collective-permute-start.23 = (bf16[48,4096]{1,0:T(8,128)(2,1)S(1)}, bf16[48,4096]{1,0:T(8,128)(2,1)S(1)}, u32[]{:S(2)}, u32[]{:S(2)}) collective-permute-start(bf16[48,4096]{1,0:T(8,128)(2,1)S(1)} %collective-permute-done.11.refs_0_), channel_id=1, source_target_pairs={{0,4},{1,13},{2,6},{3,15},{4,8},{5,1},{6,10},{7,3},{8,12},{9,5},{1... | collective-permute-start | bytes 1179656 | tf_op jit(solution)/shard_map/ppermute | solution.py:29
  112.3 17.5 %collective-permute-start.25 = (bf16[48,4096]{1,0:T(8,128)(2,1)S(1)}, bf16[48,4096]{1,0:T(8,128)(2,1)S(1)}, u32[]{:S(2)}, u32[]{:S(2)}) collective-permute-start(bf16[48,4096]{1,0:T(8,128)(2,1)S(1)} %collective-permute-done.21.refs_2_), channel_id=1, source_target_pairs={{0,4},{1,13},{2,6},{3,15},{4,8},{5,1},{6,10},{7,3},{8,12},{9,5},{1... | collective-permute-start | bytes 1179656 | tf_op jit(solution)/shard_map/ppermute | solution.py:29
  112.3 19.4 %collective-permute-start.31 = (bf16[384,256]{1,0:T(8,128)(2,1)S(1)}, bf16[384,256]{1,0:T(8,128)(2,1)S(1)}, u32[]{:S(2)}, u32[]{:S(2)}) collective-permute-start(bf16[384,256]{1,0:T(8,128)(2,1)S(1)} %get-tuple-element.41), channel_id=1, source_target_pairs={{16,0},{17,1},{18,2},{19,3},{20,4},{21,5},{22,6},{23,7},{24,8},{25... | collective-permute-start | bytes 589832 | tf_op jit(solution)/shard_map/ppermute | solution.py:57
  120.1 13.7 %collective-permute-start.32 = (bf16[384,256]{1,0:T(8,128)(2,1)S(1)}, bf16[384,256]{1,0:T(8,128)(2,1)S(1)}, u32[]{:S(2)}, u32[]{:S(2)}) collective-permute-start(bf16[384,256]{1,0:T(8,128)(2,1)S(1)} %get-tuple-element.45), channel_id=1, source_target_pairs={{16,1},{17,0},{18,3},{19,2},{20,5},{21,4},{22,7},{23,6},{24,9},{25... | collective-permute-start | bytes 589832 | tf_op jit(solution)/shard_map/ppermute | solution.py:57
  125.2 15.6 %collective-permute-start.33 = (bf16[384,256]{1,0:T(8,128)(2,1)S(1)}, bf16[384,256]{1,0:T(8,128)(2,1)S(1)}, u32[]{:S(2)}, u32[]{:S(2)}) collective-permute-start(bf16[384,256]{1,0:T(8,128)(2,1)S(1)} %get-tuple-element.46), channel_id=1, source_target_pairs={{0,16},{1,17},{2,18},{3,19},{4,20},{5,21},{6,22},{7,23},{8,24},{9,... | collective-permute-start | bytes 589832 | tf_op jit(solution)/shard_map/ppermute | solution.py:57
  129.8 19.8 %collective-permute-start.34 = (bf16[384,256]{1,0:T(8,128)(2,1)S(1)}, bf16[384,256]{1,0:T(8,128)(2,1)S(1)}, u32[]{:S(2)}, u32[]{:S(2)}) collective-permute-start(bf16[384,256]{1,0:T(8,128)(2,1)S(1)} %get-tuple-element.47), channel_id=1, source_target_pairs={{0,17},{1,16},{2,19},{3,18},{4,21},{5,20},{6,23},{7,22},{8,25},{9,... | collective-permute-start | bytes 589832 | tf_op jit(solution)/shard_map/ppermute | solution.py:57
  131.7 19.6 %copy-start.2 = (f32[256,4096]{1,0:T(8,128)S(1)}, f32[256,4096]{1,0:T(8,128)}, u32[]{:S(2)}) copy-start(f32[256,4096]{1,0:T(8,128)} %copy-done.1) | copy-start | bytes 12582916
  131.7 19.4 %collective-permute-start.12 = (bf16[48,4096]{1,0:T(8,128)(2,1)S(1)}, bf16[48,4096]{1,0:T(8,128)(2,1)S(1)}, u32[]{:S(2)}, u32[]{:S(2)}) collective-permute-start(bf16[48,4096]{1,0:T(8,128)(2,1)S(1)} %collective-permute-done.11.refs_0_), channel_id=1, source_target_pairs={{0,1},{1,0},{2,3},{3,2},{4,5},{5,4},{6,7},{7,6},{8,9},{9,8},{10,11... | collective-permute-start | bytes 1179656 | tf_op jit(solution)/shard_map/ppermute | solution.py:29
  133.8 17.3 %collective-permute-start.22 = (bf16[48,4096]{1,0:T(8,128)(2,1)S(1)}, bf16[48,4096]{1,0:T(8,128)(2,1)S(1)}, u32[]{:S(2)}, u32[]{:S(2)}) collective-permute-start(bf16[48,4096]{1,0:T(8,128)(2,1)S(1)} %collective-permute-done.21.refs_2_), channel_id=1, source_target_pairs={{0,1},{1,0},{2,3},{3,2},{4,5},{5,4},{6,7},{7,6},{8,9},{9,8},{10,11... | collective-permute-start | bytes 1179656 | tf_op jit(solution)/shard_map/ppermute | solution.py:29
  140.8 10.3 %collective-permute-start.24 = (bf16[48,4096]{1,0:T(8,128)(2,1)S(1)}, bf16[48,4096]{1,0:T(8,128)(2,1)S(1)}, u32[]{:S(2)}, u32[]{:S(2)}) collective-permute-start(bf16[48,4096]{1,0:T(8,128)(2,1)S(1)} %collective-permute-done.23.refs_4_), channel_id=1, source_target_pairs={{0,1},{1,0},{2,3},{3,2},{4,5},{5,4},{6,7},{7,6},{8,9},{9,8},{10,11... | collective-permute-start | bytes 1179656 | tf_op jit(solution)/shard_map/ppermute | solution.py:29
  149.5 1.7 %collective-permute-start.26 = (bf16[48,4096]{1,0:T(8,128)(2,1)S(1)}, bf16[48,4096]{1,0:T(8,128)(2,1)S(1)}, u32[]{:S(2)}, u32[]{:S(2)}) collective-permute-start(bf16[48,4096]{1,0:T(8,128)(2,1)S(1)} %collective-permute-done.25.refs_6_), channel_id=1, source_target_pairs={{0,1},{1,0},{2,3},{3,2},{4,5},{5,4},{6,7},{7,6},{8,9},{9,8},{10,11... | collective-permute-start | bytes 1179656 | tf_op jit(solution)/shard_map/ppermute | solution.py:29

commit v3 on v0

v3 whole, which is shorter than its diff:
```python
import functools

import jax
import jax.numpy as jnp
from jax import lax
from jax.experimental import pallas as pl
from jax.experimental.pallas import tpu as pltpu
from jax.sharding import PartitionSpec as P

RING = 4
PLANES = 2
CORES = 2
ANY = pl.BlockSpec(memory_space=pl.ANY)
VMEM = pl.BlockSpec(memory_space=pltpu.VMEM)
HBM = pl.BlockSpec(memory_space=pltpu.HBM)
NEAR = tuple((dy, dz, dc) for dz in range(PLANES) for dy in (0, -1, 1, 2) for dc in range(CORES))
LATE = tuple((2, dz, dc) for dz in range(PLANES) for dc in range(CORES))
EARLY = tuple(key for key in NEAR if key not in LATE)


def place(y, plane, core):
    return (y * PLANES + plane) * CORES + core


def moved(value, step):
    pairs = []
    for y in range(RING):
        for plane in range(PLANES):
            for core in range(CORES):
                pairs.append((place(y, plane, core), place(*step(y, plane, core))))
    return lax.ppermute(value, "tensor", pairs)


def upward(value):
    return moved(value, lambda y, plane, core: ((y + 1) % RING, plane, core))


def downward(value):
    return moved(value, lambda y, plane, core: ((y - 1) % RING, plane, core))


def across(value):
    return moved(value, lambda y, plane, core: (y, 1 - plane, core))


def to_sibling(value):
    return moved(value, lambda y, plane, core: (y, plane, 1 - core))


def mirrored(value):
    count = lax.axis_size("pipe")
    return lax.ppermute(value, "pipe", [(i, count - 1 - i) for i in range(count)])


def from_behind(value, by):
    count = lax.axis_size("pipe")
    pairs = [(i, i + by) for i in range(count) if 0 <= i + by < count]
    return lax.ppermute(value, "pipe", pairs)


def after(value, *earlier):
    return lax.optimization_barrier((value, *earlier))[0]


def first_row(key, rows):
    t = lax.axis_index("tensor")
    dy, dz, dc = key
    core = t % CORES
    plane = (t // CORES) % PLANES
    y = (t // (CORES * PLANES) + dy + RING) % RING
    block = place(y, 1 - plane if dz else plane, 1 - core if dc else core)
    return pl.multiple_of(block * rows, rows)


def run(copies):
    for copy in copies:
        copy.start()
    for copy in copies:
        copy.wait()


def back_kernel(*refs):
    n = len(NEAR)
    blocks = refs[:n]
    weights, first, second, whole, held, bsems, wsems = refs[n:]
    rows = blocks[0].shape[1]
    copies = [pltpu.make_async_copy(weights.at[r], held.at[r], wsems.at[r]) for r in range(2)]
    for i, key in enumerate(NEAR):
        target = whole.at[:, pl.ds(first_row(key, rows), rows), :]
        copies.append(pltpu.make_async_copy(blocks[i], target, bsems.at[i]))
    run(copies)
    tile = 384
    for r, out in enumerate((first, second)):
        for i in range(out.shape[0] // tile):
            span = slice(i * tile, (i + 1) * tile)
            out[span, :] = lax.dot_general(
                whole[r, span, :], held[r], (((1,), (1,)), ((), ())),
                preferred_element_type=jnp.float32,
            ).astype(out.dtype)


def sum_kernel(keys, late_keys, more, *refs):
    n = len(keys)
    blocks, context, rest = refs[:n], refs[n], refs[n + 1 :]
    if more:
        before, *rest = rest
    if late_keys:
        total, late, *rest = rest
    else:
        total, *rest = rest
    whole, upright, flat, bsems, csems = rest
    rows = whole.shape[0] // n
    copies = []
    for i, block in enumerate(blocks):
        source = block.at[0] if len(block.shape) == 3 else block
        copies.append(
            pltpu.make_async_copy(source, whole.at[pl.ds(i * rows, rows), :], bsems.at[i])
        )
    for i, key in enumerate(keys + late_keys):
        source = context.at[pl.ds(first_row(key, rows), rows), :]
        target = upright.at[pl.ds(i * rows, rows), :]
        copies.append(pltpu.make_async_copy(source, target, csems.at[i]))
    run(copies)
    count = n * rows
    flat[...] = upright[pl.ds(0, count), :].T
    if late_keys:
        late[...] = upright[pl.ds(count, len(late_keys) * rows), :].T
    wide = 512

    @pl.loop(0, total.shape[1] // wide)
    def _(i):
        cols = pl.ds(pl.multiple_of(i * wide, wide), wide)
        product = jnp.dot(flat[...], whole[:, cols], preferred_element_type=jnp.float32)
        total[:, cols] = before[:, cols] + product if more else product


def last_kernel(*refs):
    n = len(LATE)
    context, total, out, whole = refs[n:]
    rows = refs[0].shape[0]
    for i, block in enumerate(refs[:n]):
        whole[pl.ds(i * rows, rows), :] = block[...]
    out[...] = (
        total[...] + jnp.dot(context[...], whole[...], preferred_element_type=jnp.float32)
    ).astype(out.dtype)


def shards(section_weights, context, grad_out):
    tokens, width_in = context.shape[2:]
    rows, width_out = grad_out.shape[2:]
    flops = 2 * tokens * width_in * width_out

    near = {(0, 0, 0): grad_out[0]}
    far = {}

    def send(held, move, begin, end, *earlier):
        key = (*end, int(move is to_sibling))
        held[key] = move(after(held[(*begin, 0)], *earlier))
        return held[key]

    def share(held, *spots):
        for spot in spots:
            held[(*spot, 1)] = to_sibling(held[(*spot, 0)])
        return [held[(*spot, 1)] for spot in spots]

    step = [
        send(near, upward, (0, 0), (-1, 0)),
        send(near, downward, (0, 0), (1, 0)),
        send(near, across, (0, 0), (0, 1)),
    ]
    far[0, 0, 0] = mirrored(after(grad_out[0, 1], *step))
    up_context = context[0, 1]
    step.append(up_context)
    step = [
        send(near, upward, (-1, 0), (2, 0), *step),
        send(near, downward, (0, 1), (1, 1), *step),
        far[0, 0, 0],
        *share(near, (0, 0), (-1, 0), (1, 0), (0, 1)),
    ]
    far_context = mirrored(after(up_context, *step))
    step = [
        send(near, upward, (0, 1), (-1, 1), *step),
        send(near, downward, (1, 1), (2, 1), *step),
        send(far, across, (0, 0), (0, 1), *step),
        far_context,
    ]
    for spot in ((2, 0), (1, 1)):
        send(near, to_sibling, spot, spot, far[0, 1, 0])
    for spot in ((-1, 1), (2, 1)):
        send(near, to_sibling, spot, spot, *step)
    send(far, upward, (0, 0), (-1, 0), *step)
    send(far, downward, (0, 0), (1, 0), *step)

    back_shape = jax.ShapeDtypeStruct((tokens, width_in), jnp.bfloat16)
    back = pl.pallas_call(
        back_kernel,
        out_shape=(back_shape,) * 2,
        in_specs=[HBM] + [ANY] * (len(NEAR) - 1) + [HBM],
        out_specs=(VMEM,) * 2,
        scratch_shapes=[
            pltpu.VMEM((2, tokens, width_out), jnp.bfloat16),
            pltpu.VMEM((2, width_in, width_out), jnp.bfloat16),
            pltpu.SemaphoreType.DMA((len(NEAR),)),
            pltpu.SemaphoreType.DMA((2,)),
        ],
        compiler_params=pltpu.CompilerParams(vmem_limit_bytes=20 * 2**20),
        cost_estimate=pl.CostEstimate(
            flops=2 * flops, bytes_accessed=4 * (tokens + width_in) * width_out, transcendentals=0
        ),
    )(*(near[key] for key in NEAR), section_weights[0])
    from_next = from_behind(back[0], -1)
    from_prior = from_behind(back[1], 1)
    input_grad = jnp.stack([from_next, from_prior])[None]

    send(far, upward, (0, 1), (-1, 1), back[0])
    send(far, downward, (0, 1), (1, 1), back[0])
    send(far, upward, (-1, 0), (2, 0), back[0])

    def summed(keys, blocks, held, total, late):
        count = len(keys)
        everything = keys + late
        sizes = count * rows, len(late) * rows
        shapes = [jax.ShapeDtypeStruct((width_in, width_out), jnp.float32)]
        if late:
            shapes.append(jax.ShapeDtypeStruct((width_in, sizes[1]), jnp.bfloat16))
        return pl.pallas_call(
            functools.partial(sum_kernel, keys, late, total is not None),
            out_shape=tuple(shapes),
            in_specs=[ANY] * count + [ANY] + [VMEM] * (total is not None),
            out_specs=(VMEM,) * len(shapes),
            scratch_shapes=[
                pltpu.VMEM((sizes[0], width_out), jnp.bfloat16),
                pltpu.VMEM((sum(sizes), width_in), jnp.bfloat16),
                pltpu.VMEM((width_in, sizes[0]), jnp.bfloat16),
                pltpu.SemaphoreType.DMA((count,)),
                pltpu.SemaphoreType.DMA((len(everything),)),
            ],
            compiler_params=pltpu.CompilerParams(vmem_limit_bytes=18 * 2**20),
            cost_estimate=pl.CostEstimate(
                flops=2 * sizes[0] * width_in * width_out,
                bytes_accessed=(2 * sizes[0] + 6 * width_in) * width_out,
                transcendentals=0,
            ),
        )(*blocks, held, *([] if total is None else [total]))

    (total,) = summed(NEAR, [near[key] for key in NEAR], after(context[0, 0], *back), None, ())
    send(far, downward, (1, 1), (2, 1), total)
    for spot in ((0, 0), (0, 1), (-1, 0), (1, 0)):
        send(far, to_sibling, spot, spot, total)
    share(far, (-1, 1), (1, 1), (2, 0))
    send(far, to_sibling, (2, 1), (2, 1), from_next, from_prior)
    total, late_context = summed(EARLY, [far[key] for key in EARLY], far_context, total, LATE)
    late = len(LATE) * rows

    wide = 1024
    columns = pl.BlockSpec((width_in, wide), lambda i: (0, i))
    weight_grad = pl.pallas_call(
        last_kernel,
        out_shape=jax.ShapeDtypeStruct((width_in, width_out), jnp.bfloat16),
        grid=(width_out // wide,),
        in_specs=[pl.BlockSpec((rows, wide), lambda i: (0, i))] * len(LATE)
        + [pl.BlockSpec((width_in, late), lambda i: (0, 0)), columns],
        out_specs=columns,
        scratch_shapes=[pltpu.VMEM((late, wide), jnp.bfloat16)],
        compiler_params=pltpu.CompilerParams(vmem_limit_bytes=12 * 2**20),
        cost_estimate=pl.CostEstimate(
            flops=flops // 4, bytes_accessed=(2 * late + 6 * width_in) * width_out,
            transcendentals=0,
        ),
    )(*(far[key] for key in LATE), late_context, total)
    return (weight_grad[None], input_grad)


def solution(mesh):
    placed = (
        P("pipe", None, "tensor", None),
        P("pipe", None, None, "tensor"),
        P("pipe", None, "tensor", None),
    )
    return jax.shard_map(
        shards,
        mesh=mesh,
        in_specs=placed,
        out_specs=(P("pipe", "tensor", None), P("pipe", None, None, "tensor")),
        check_vma=False,
    )
```

time: 350 us -> 143 us (0.41)
  the two profiles are of different devices: /device:TPU:58 before, /device:TPU:1 now
where the time goes in v3:
time: 143 us; the launch traced here: 142 us
  waiting for transfers between devices  57.1 us (40%)
  starting transfers between devices  56.5 us (40%)
  Pallas kernels  21.4 us (15%)
  local copies, waits for them, and re-layouts  5.51 us (4%)
    ppermute x30, starting transfers between devices, moved(): return lax.ppermute(value, 'tensor', pairs)  39.2 us
    ppermute x30, waiting for transfers between devices, moved(): return lax.ppermute(value, 'tensor', pairs)  32.9 us
    ppermute x2, waiting for transfers between devices, mirrored(): lax.ppermute(value, 'pipe', [(i, count - 1 - i) for i in range(count)])  14.5 us
    pallas_call x2, Pallas kernels, summed(): pl.pallas_call(functools.partial(sum_kernel, keys, late, total is not Non...  13.8 us
    ppermute x2, waiting for transfers between devices, from_behind(): return lax.ppermute(value, 'pipe', pairs)  9.7 us
    ppermute x2, starting transfers between devices, mirrored(): lax.ppermute(value, 'pipe', [(i, count - 1 - i) for i in range(count)])  8.89 us
    ppermute x2, starting transfers between devices, from_behind(): return lax.ppermute(value, 'pipe', pairs)  8.43 us
    pallas_call x1, Pallas kernels, shards(): pl.pallas_call(back_kernel, out_shape=(back_shape,) * 2, in_specs=[HBM] +...  4.8 us
  transfers between devices with their start and end apart: 34, of which 12 were waited for; matrix products, arithmetic and copies ran while one was open for 2% of the time, Pallas kernels for 13%

profile of v3, /device:TPU:1, one launch (start us, length us, event | category | flops | bytes accessed | tf_op | source)
XLA Modules:
  0.0 142.3 jit_solution(13458257417570482869)
XLA Ops:
  0.6 2.6 %collective-permute-start.2 = (bf16[2,48,4096]{2,1,0:T(8,128)(2,1)}, bf16[2,48,4096]{2,1,0:T(8,128)(2,1)S(1)}, u32[]{:S(2)}, u32[]{:S(2)}) collective-permute-start(bf16[2,48,4096]{2,1,0:T(8,128)(2,1)} %bitcast.13), channel_id=1, source_target_pairs={{0,2},{1,3},{2,0},{3,1},{4,6},{5,7},{6,4},{7,5},{8,10},{9,11},{10,... | collective-permute-start | bytes 2359304 | tf_op jit(solution)/shard_map/ppermute | solution.py:31
  3.2 2.7 %collective-permute-start.1 = (bf16[2,48,4096]{2,1,0:T(8,128)(2,1)}, bf16[2,48,4096]{2,1,0:T(8,128)(2,1)S(1)}, u32[]{:S(2)}, u32[]{:S(2)}) collective-permute-start(bf16[2,48,4096]{2,1,0:T(8,128)(2,1)} %bitcast.14), channel_id=1, source_target_pairs={{0,12},{1,13},{2,14},{3,15},{4,0},{5,1},{6,2},{7,3},{8,4},{9,5},{1... | collective-permute-start | bytes 2359304 | tf_op jit(solution)/shard_map/ppermute | solution.py:31
  5.9 0.0 collective-permute-start
  5.9 1.2 collective-permute-start.6
  7.2 1.0 slice_bitcast_fusion.2
  8.2 11.5 %collective-permute-done.2.refs_8_ = bf16[2,48,4096]{2,1,0:T(8,128)(2,1)S(1)} collective-permute-done((bf16[2,48,4096]{2,1,0:T(8,128)(2,1)}, bf16[2,48,4096]{2,1,0:T(8,128)(2,1)S(1)}, u32[]{:S(2)}, u32[]{:S(2)}) %collective-permute-start.2) | collective-permute-done | bytes 786464 | tf_op jit(solution)/shard_map/ppermute | solution.py:31
  19.7 2.4 %collective-permute-done.1.refs_4_ = bf16[2,48,4096]{2,1,0:T(8,128)(2,1)S(1)} collective-permute-done((bf16[2,48,4096]{2,1,0:T(8,128)(2,1)}, bf16[2,48,4096]{2,1,0:T(8,128)(2,1)S(1)}, u32[]{:S(2)}, u32[]{:S(2)}) %collective-permute-start.1) | collective-permute-done | bytes 786464 | tf_op jit(solution)/shard_map/ppermute | solution.py:31
  22.1 3.0 %collective-permute-done.refs_2_ = bf16[2,48,4096]{2,1,0:T(8,128)(2,1)S(1)} collective-permute-done((bf16[2,48,4096]{2,1,0:T(8,128)(2,1)}, bf16[2,48,4096]{2,1,0:T(8,128)(2,1)S(1)}, u32[]{:S(2)}, u32[]{:S(2)}) %collective-permute-start) | collective-permute-done | bytes 786464 | tf_op jit(solution)/shard_map/ppermute | solution.py:31
  25.1 7.3 %collective-permute-start.3 = (bf16[48,4096]{1,0:T(8,128)(2,1)S(1)}, bf16[48,4096]{1,0:T(8,128)(2,1)S(1)}, u32[]{:S(2)}, u32[]{:S(2)}) collective-permute-start(bf16[48,4096]{1,0:T(8,128)(2,1)S(1)} %slice_bitcast_fusion.2), channel_id=1, source_target_pairs={{0,240},{16,224},{32,208},{48,192},{64,176},{80,160},{96,144},{112... | collective-permute-start | bytes 1179656 | tf_op jit(solution)/shard_map/ppermute | solution.py:52
  32.5 1.2 slice_bitcast_fusion
  33.6 0.1 collective-permute-start.4
  33.7 2.5 %collective-permute-start.9 = (bf16[2,48,4096]{2,1,0:T(8,128)(2,1)S(1)}, bf16[2,48,4096]{2,1,0:T(8,128)(2,1)S(1)}, u32[]{:S(2)}, u32[]{:S(2)}) collective-permute-start(bf16[2,48,4096]{2,1,0:T(8,128)(2,1)S(1)} %collective-permute-done.2.refs_8_), channel_id=1, source_target_pairs={{0,1},{1,0},{2,3},{3,2},{4,5},{5,4},{6,7},{7,6},{8,9},{9,8},{10,11... | collective-permute-start | bytes 2359304 | tf_op jit(solution)/shard_map/ppermute | solution.py:31
  36.2 0.1 collective-permute-start.8
  36.3 0.0 collective-permute-done.6.refs_1_
  36.3 2.8 %collective-permute-start.5 = (bf16[2,48,4096]{2,1,0:T(8,128)(2,1)S(1)}, bf16[2,48,4096]{2,1,0:T(8,128)(2,1)S(1)}, u32[]{:S(2)}, u32[]{:S(2)}) collective-permute-start(bf16[2,48,4096]{2,1,0:T(8,128)(2,1)S(1)} %collective-permute-done.2.refs_8_), channel_id=1, source_target_pairs={{0,12},{1,13},{2,14},{3,15},{4,0},{5,1},{6,2},{7,3},{8,4},{9,5},{1... | collective-permute-start | bytes 2359304 | tf_op jit(solution)/shard_map/ppermute | solution.py:31
  39.1 10.1 %collective-permute-done.3.refs_0_ = bf16[48,4096]{1,0:T(8,128)(2,1)S(1)} collective-permute-done((bf16[48,4096]{1,0:T(8,128)(2,1)S(1)}, bf16[48,4096]{1,0:T(8,128)(2,1)S(1)}, u32[]{:S(2)}, u32[]{:S(2)}) %collective-permute-start.3) | collective-permute-done | bytes 393248 | tf_op jit(solution)/shard_map/ppermute | solution.py:52
  49.2 1.0 collective-permute-start.7
  50.2 0.0 collective-permute-done.8.refs_5_
  50.2 1.3 collective-permute-done.4.refs_6_
  51.5 4.0 %collective-permute-done.5.refs_12_ = bf16[2,48,4096]{2,1,0:T(8,128)(2,1)S(1)} collective-permute-done((bf16[2,48,4096]{2,1,0:T(8,128)(2,1)S(1)}, bf16[2,48,4096]{2,1,0:T(8,128)(2,1)S(1)}, u32[]{:S(2)}, u32[]{:S(2)}) %collective-permute-start.5) | collective-permute-done | bytes 786464 | tf_op jit(solution)/shard_map/ppermute | solution.py:31
  55.5 0.0 collective-permute-done.7.refs_3_
  55.5 0.0 collective-permute-start.10
  55.5 3.4 %collective-permute-start.11 = (bf16[2,48,4096]{2,1,0:T(8,128)(2,1)S(1)}, bf16[2,48,4096]{2,1,0:T(8,128)(2,1)S(1)}, u32[]{:S(2)}, u32[]{:S(2)}) collective-permute-start(bf16[2,48,4096]{2,1,0:T(8,128)(2,1)S(1)} %collective-permute-done.5.refs_12_), channel_id=1, source_target_pairs={{0,12},{1,13},{2,14},{3,15},{4,0},{5,1},{6,2},{7,3},{8,4},{9,5},{1... | collective-permute-start | bytes 2359304 | tf_op jit(solution)/shard_map/ppermute | solution.py:31
  58.9 0.7 collective-permute-start.12
  59.6 1.6 %collective-permute-start.13 = (bf16[768,256]{1,0:T(8,128)(2,1)S(1)}, bf16[768,256]{1,0:T(8,128)(2,1)S(1)}, u32[]{:S(2)}, u32[]{:S(2)}) collective-permute-start(bf16[768,256]{1,0:T(8,128)(2,1)S(1)} %get-tuple-element.33), channel_id=1, source_target_pairs={{0,240},{16,224},{32,208},{48,192},{64,176},{80,160},{96,144},{112... | collective-permute-start | bytes 1179656 | tf_op jit(solution)/shard_map/ppermute | solution.py:52
  61.2 10.0 %collective-permute-done.12.refs_6_ = bf16[48,4096]{1,0:T(8,128)(2,1)S(1)} collective-permute-done((bf16[48,4096]{1,0:T(8,128)(2,1)S(1)}, bf16[48,4096]{1,0:T(8,128)(2,1)S(1)}, u32[]{:S(2)}, u32[]{:S(2)}) %collective-permute-start.12) | collective-permute-done | bytes 393248 | tf_op jit(solution)/shard_map/ppermute | solution.py:31
  71.2 2.6 %collective-permute-start.15 = (bf16[2,48,4096]{2,1,0:T(8,128)(2,1)S(1)}, bf16[2,48,4096]{2,1,0:T(8,128)(2,1)S(1)}, u32[]{:S(2)}, u32[]{:S(2)}) collective-permute-start(bf16[2,48,4096]{2,1,0:T(8,128)(2,1)S(1)} %collective-permute-done.4.refs_6_), channel_id=1, source_target_pairs={{0,1},{1,0},{2,3},{3,2},{4,5},{5,4},{6,7},{7,6},{8,9},{9,8},{10,11... | collective-permute-start | bytes 2359304 | tf_op jit(solution)/shard_map/ppermute | solution.py:31
  73.8 0.0 collective-permute-start.17
  73.8 4.4 %collective-permute-done.13.refs_12_ = bf16[768,256]{1,0:T(8,128)(2,1)S(1)} collective-permute-done((bf16[768,256]{1,0:T(8,128)(2,1)S(1)}, bf16[768,256]{1,0:T(8,128)(2,1)S(1)}, u32[]{:S(2)}, u32[]{:S(2)}) %collective-permute-start.13) | collective-permute-done | bytes 393248 | tf_op jit(solution)/shard_map/ppermute | solution.py:52
  78.2 0.0 collective-permute-done.10.refs_10_
  78.2 0.0 collective-permute-done.11.refs_14_
  78.2 1.6 %collective-permute-start.16 = (bf16[2,48,4096]{2,1,0:T(8,128)(2,1)S(1)}, bf16[2,48,4096]{2,1,0:T(8,128)(2,1)S(1)}, u32[]{:S(2)}, u32[]{:S(2)}) collective-permute-start(bf16[2,48,4096]{2,1,0:T(8,128)(2,1)S(1)} %collective-permute-done.10.refs_10_), channel_id=1, source_target_pairs={{0,1},{1,0},{2,3},{3,2},{4,5},{5,4},{6,7},{7,6},{8,9},{9,8},{10,11... | collective-permute-start | bytes 2359304 | tf_op jit(solution)/shard_map/ppermute | solution.py:31
  79.8 0.1 collective-permute-start.18
  79.9 0.0 collective-permute-start.14
  79.9 0.0 collective-permute-done.15.refs_7_
  79.9 2.7 %collective-permute-start.28 = (bf16[48,4096]{1,0:T(8,128)(2,1)S(1)}, bf16[48,4096]{1,0:T(8,128)(2,1)S(1)}, u32[]{:S(2)}, u32[]{:S(2)}) collective-permute-start(bf16[48,4096]{1,0:T(8,128)(2,1)S(1)} %collective-permute-done.3.refs_0_), channel_id=1, source_target_pairs={{0,12},{1,13},{2,14},{3,15},{4,0},{5,1},{6,2},{7,3},{8,4},{9,5},{1... | collective-permute-start | bytes 1179656 | tf_op jit(solution)/shard_map/ppermute | solution.py:31
  82.6 0.0 collective-permute-done.17.refs_13_
  82.6 0.0 collective-permute-done.16.refs_11_
  82.6 0.3 collective-permute-done.18.refs_15_
  82.9 1.1 copy-done
  84.0 2.2 %copy-done.2 = bf16[1,2,256,4096]{3,2,1,0:T(8,128)(2,1)S(1)} copy-done((bf16[1,2,256,4096]{3,2,1,0:T(8,128)(2,1)S(1)}, bf16[1,2,256,4096]{3,2,1,0:T(8,128)(2,1)}, u32[]{:S(2)}) %copy-start.2) | copy-done | bytes 4194328
  86.2 4.8 %shard_map.50 = (bf16[768,256]{1,0:T(8,128)(2,1)S(1)}, bf16[768,256]{1,0:T(8,128)(2,1)S(1)}) custom-call(bf16[2,48,4096]{2,1,0:T(8,128)(2,1)S(1)} %bitcast.17, bf16[2,48,4096]{2,1,0:T(8,128)(2,1)S(1)} %collective-permute-done.6.refs_1_, bf16[2,48,4096]{2,1,0:T(8,128)(2,1)S(1)} %collective-permute-done.refs_2_, ...), custom_call_target="tpu_custom_call" | custom-call | flops 3221225472 | bytes 16777216 | tf_op jit(solution)/shard_map/pallas_call | solution.py:195
  91.0 0.1 collective-permute-start.31
  91.1 2.7 %collective-permute-start.21 = (bf16[48,4096]{1,0:T(8,128)(2,1)S(1)}, bf16[48,4096]{1,0:T(8,128)(2,1)S(1)}, u32[]{:S(2)}, u32[]{:S(2)}) collective-permute-start(bf16[48,4096]{1,0:T(8,128)(2,1)S(1)} %collective-permute-done.12.refs_6_), channel_id=1, source_target_pairs={{0,12},{1,13},{2,14},{3,15},{4,0},{5,1},{6,2},{7,3},{8,4},{9,5},{1... | collective-permute-start | bytes 1179656 | tf_op jit(solution)/shard_map/ppermute | solution.py:31
  93.8 7.4 %shard_map.51.refs_13_ = f32[256,4096]{1,0:T(8,128)S(1)} custom-call(bf16[2,48,4096]{2,1,0:T(8,128)(2,1)S(1)} %bitcast.18, bf16[2,48,4096]{2,1,0:T(8,128)(2,1)S(1)} %collective-permute-done.6.refs_1_, bf16[2,48,4096]{2,1,0:T(8,128)(2,1)S(1)} %collective-permute-done.refs_2_, bf16[2,48,4096]{2,1,0:T(8,128)(2,1)S(1)} %collective-permute-done.7.refs_3_, ...), custom_call_target="tpu_custom_call" | custom-call | flops 1610612736 | bytes 12582912 | tf_op jit(solution)/shard_map/pallas_call | solution.py:226
  101.1 1.4 collective-permute-start.26
  102.5 0.0 collective-permute-done.21.refs_10_
  102.5 7.1 %collective-permute-start.24 = (bf16[768,256]{1,0:T(8,128)(2,1)S(1)}, bf16[768,256]{1,0:T(8,128)(2,1)S(1)}, u32[]{:S(2)}, u32[]{:S(2)}) collective-permute-start(bf16[768,256]{1,0:T(8,128)(2,1)S(1)} %get-tuple-element.42), channel_id=1, source_target_pairs={{0,16},{16,32},{32,48},{48,64},{64,80},{80,96},{96,112},{112,128},... | collective-permute-start | bytes 1179656 | tf_op jit(solution)/shard_map/ppermute | solution.py:58
  109.6 0.0 collective-permute-done.28.refs_4_
  109.7 1.3 collective-permute-start.23
  111.0 3.0 %collective-permute-start.22 = (bf16[48,4096]{1,0:T(8,128)(2,1)S(1)}, bf16[48,4096]{1,0:T(8,128)(2,1)S(1)}, u32[]{:S(2)}, u32[]{:S(2)}) collective-permute-start(bf16[48,4096]{1,0:T(8,128)(2,1)S(1)} %collective-permute-done.21.refs_10_), channel_id=1, source_target_pairs={{0,12},{1,13},{2,14},{3,15},{4,0},{5,1},{6,2},{7,3},{8,4},{9,5},{1... | collective-permute-start | bytes 1179656 | tf_op jit(solution)/shard_map/ppermute | solution.py:31
  114.0 1.7 %collective-permute-start.27 = (bf16[48,4096]{1,0:T(8,128)(2,1)S(1)}, bf16[48,4096]{1,0:T(8,128)(2,1)S(1)}, u32[]{:S(2)}, u32[]{:S(2)}) collective-permute-start(bf16[48,4096]{1,0:T(8,128)(2,1)S(1)} %collective-permute-done.14.refs_2_), channel_id=1, source_target_pairs={{0,1},{1,0},{2,3},{3,2},{4,5},{5,4},{6,7},{7,6},{8,9},{9,8},{10,11... | collective-permute-start | bytes 1179656 | tf_op jit(solution)/shard_map/ppermute | solution.py:31
  115.6 0.1 collective-permute-start.29
  115.7 6.8 %collective-permute-done.24 = bf16[768,256]{1,0:T(8,128)(2,1)S(1)} collective-permute-done((bf16[768,256]{1,0:T(8,128)(2,1)S(1)}, bf16[768,256]{1,0:T(8,128)(2,1)S(1)}, u32[]{:S(2)}, u32[]{:S(2)}) %collective-permute-start.24) | collective-permute-done | bytes 393248 | tf_op jit(solution)/shard_map/ppermute | solution.py:58
  122.5 5.0 %collective-permute-start.30 = (bf16[48,4096]{1,0:T(8,128)(2,1)S(1)}, bf16[48,4096]{1,0:T(8,128)(2,1)S(1)}, u32[]{:S(2)}, u32[]{:S(2)}) collective-permute-start(bf16[48,4096]{1,0:T(8,128)(2,1)S(1)} %collective-permute-done.12.refs_6_), channel_id=1, source_target_pairs={{0,1},{1,0},{2,3},{3,2},{4,5},{5,4},{6,7},{7,6},{8,9},{9,8},{10,11... | collective-permute-start | bytes 1179656 | tf_op jit(solution)/shard_map/ppermute | solution.py:31
  127.4 2.9 %collective-permute-done.23 = bf16[768,256]{1,0:T(8,128)(2,1)S(1)} collective-permute-done((bf16[768,256]{1,0:T(8,128)(2,1)S(1)}, bf16[768,256]{1,0:T(8,128)(2,1)S(1)}, u32[]{:S(2)}, u32[]{:S(2)}) %collective-permute-start.23) | collective-permute-done | bytes 393248 | tf_op jit(solution)/shard_map/ppermute | solution.py:58
  130.4 0.7 collective-permute-start.32
  131.1 0.0 collective-permute-start.33
  131.1 0.5 collective-permute-start.20
  131.6 0.1 collective-permute-start.25
  131.7 0.9 maximum_bitcast_fusion
  132.6 0.3 collective-permute-done.33.refs_11_
  133.0 6.4 %shard_map.52 = (f32[256,4096]{1,0:T(8,128)S(1)}, bf16[256,192]{1,0:T(8,128)(2,1)S(1)}) custom-call(bf16[48,4096]{1,0:T(8,128)(2,1)S(1)} %collective-permute-done.3.refs_0_, bf16[48,4096]{1,0:T(8,128)(2,1)S(1)} %collective-permute-done.26.refs_1_, bf16[48,4096]{1,0:T(8,128)(2,1)S(1)} %collective-permute-done.14.refs_2_, ...), custom_call_target="tpu_custom_call" | custom-call | flops 1207959552 | bytes 11010048 | tf_op jit(solution)/shard_map/pallas_call | solution.py:226
  139.4 2.8 %shard_map.53 = bf16[256,4096]{1,0:T(8,128)(2,1)} custom-call(bf16[48,4096]{1,0:T(8,128)(2,1)S(1)} %collective-permute-done.19.refs_0_, bf16[48,4096]{1,0:T(8,128)(2,1)S(1)} %collective-permute-done.20.refs_1_, bf16[48,4096]{1,0:T(8,128)(2,1)S(1)} %collective-permute-done.22.refs_2_, bf16[48,4096]{1,0:T(8,128)(2,1)S(1)} %collective-permute-done.25.refs_3_, ...), custom_call_target="tpu_custom_call" | custom-call | flops 402653184 | bytes 7864320 | tf_op jit(solution)/shard_map/pallas_call | solution.py:257
  (17 shorter events, 0.0 us)
Async XLA Ops:
  0.6 19.1 %collective-permute-start.2 = (bf16[2,48,4096]{2,1,0:T(8,128)(2,1)}, bf16[2,48,4096]{2,1,0:T(8,128)(2,1)S(1)}, u32[]{:S(2)}, u32[]{:S(2)}) collective-permute-start(bf16[2,48,4096]{2,1,0:T(8,128)(2,1)} %bitcast.13), channel_id=1, source_target_pairs={{0,2},{1,3},{2,0},{3,1},{4,6},{5,7},{6,4},{7,5},{8,10},{9,11},{10,... | collective-permute-start | bytes 2359304 | tf_op jit(solution)/shard_map/ppermute | solution.py:31
  3.2 18.9 %collective-permute-start.1 = (bf16[2,48,4096]{2,1,0:T(8,128)(2,1)}, bf16[2,48,4096]{2,1,0:T(8,128)(2,1)S(1)}, u32[]{:S(2)}, u32[]{:S(2)}) collective-permute-start(bf16[2,48,4096]{2,1,0:T(8,128)(2,1)} %bitcast.14), channel_id=1, source_target_pairs={{0,12},{1,13},{2,14},{3,15},{4,0},{5,1},{6,2},{7,3},{8,4},{9,5},{1... | collective-permute-start | bytes 2359304 | tf_op jit(solution)/shard_map/ppermute | solution.py:31
  5.9 19.2 %collective-permute-start = (bf16[2,48,4096]{2,1,0:T(8,128)(2,1)}, bf16[2,48,4096]{2,1,0:T(8,128)(2,1)S(1)}, u32[]{:S(2)}, u32[]{:S(2)}) collective-permute-start(bf16[2,48,4096]{2,1,0:T(8,128)(2,1)} %bitcast.15), channel_id=1, source_target_pairs={{0,4},{1,5},{2,6},{3,7},{4,8},{5,9},{6,10},{7,11},{8,12},{9,13},{1... | collective-permute-start | bytes 2359304 | tf_op jit(solution)/shard_map/ppermute | solution.py:31
  5.9 30.4 %collective-permute-start.6 = (bf16[2,48,4096]{2,1,0:T(8,128)(2,1)}, bf16[2,48,4096]{2,1,0:T(8,128)(2,1)S(1)}, u32[]{:S(2)}, u32[]{:S(2)}) collective-permute-start(bf16[2,48,4096]{2,1,0:T(8,128)(2,1)} %bitcast.16), channel_id=1, source_target_pairs={{0,1},{1,0},{2,3},{3,2},{4,5},{5,4},{6,7},{7,6},{8,9},{9,8},{10,11... | collective-permute-start | bytes 2359304 | tf_op jit(solution)/shard_map/ppermute | solution.py:31
  25.1 24.1 %collective-permute-start.3 = (bf16[48,4096]{1,0:T(8,128)(2,1)S(1)}, bf16[48,4096]{1,0:T(8,128)(2,1)S(1)}, u32[]{:S(2)}, u32[]{:S(2)}) collective-permute-start(bf16[48,4096]{1,0:T(8,128)(2,1)S(1)} %slice_bitcast_fusion.2), channel_id=1, source_target_pairs={{0,240},{16,224},{32,208},{48,192},{64,176},{80,160},{96,144},{112... | collective-permute-start | bytes 1179656 | tf_op jit(solution)/shard_map/ppermute | solution.py:52
  33.6 17.9 %collective-permute-start.4 = (bf16[2,48,4096]{2,1,0:T(8,128)(2,1)S(1)}, bf16[2,48,4096]{2,1,0:T(8,128)(2,1)S(1)}, u32[]{:S(2)}, u32[]{:S(2)}) collective-permute-start(bf16[2,48,4096]{2,1,0:T(8,128)(2,1)S(1)} %collective-permute-done.refs_2_), channel_id=1, source_target_pairs={{0,4},{1,5},{2,6},{3,7},{4,8},{5,9},{6,10},{7,11},{8,12},{9,13},{1... | collective-permute-start | bytes 2359304 | tf_op jit(solution)/shard_map/ppermute | solution.py:31
  33.7 16.5 %collective-permute-start.9 = (bf16[2,48,4096]{2,1,0:T(8,128)(2,1)S(1)}, bf16[2,48,4096]{2,1,0:T(8,128)(2,1)S(1)}, u32[]{:S(2)}, u32[]{:S(2)}) collective-permute-start(bf16[2,48,4096]{2,1,0:T(8,128)(2,1)S(1)} %collective-permute-done.2.refs_8_), channel_id=1, source_target_pairs={{0,1},{1,0},{2,3},{3,2},{4,5},{5,4},{6,7},{7,6},{8,9},{9,8},{10,11... | collective-permute-start | bytes 2359304 | tf_op jit(solution)/shard_map/ppermute | solution.py:31
  36.2 14.0 %collective-permute-start.8 = (bf16[2,48,4096]{2,1,0:T(8,128)(2,1)S(1)}, bf16[2,48,4096]{2,1,0:T(8,128)(2,1)S(1)}, u32[]{:S(2)}, u32[]{:S(2)}) collective-permute-start(bf16[2,48,4096]{2,1,0:T(8,128)(2,1)S(1)} %collective-permute-done.1.refs_4_), channel_id=1, source_target_pairs={{0,1},{1,0},{2,3},{3,2},{4,5},{5,4},{6,7},{7,6},{8,9},{9,8},{10,11... | collective-permute-start | bytes 2359304 | tf_op jit(solution)/shard_map/ppermute | solution.py:31
  36.3 19.2 %collective-permute-start.5 = (bf16[2,48,4096]{2,1,0:T(8,128)(2,1)S(1)}, bf16[2,48,4096]{2,1,0:T(8,128)(2,1)S(1)}, u32[]{:S(2)}, u32[]{:S(2)}) collective-permute-start(bf16[2,48,4096]{2,1,0:T(8,128)(2,1)S(1)} %collective-permute-done.2.refs_8_), channel_id=1, source_target_pairs={{0,12},{1,13},{2,14},{3,15},{4,0},{5,1},{6,2},{7,3},{8,4},{9,5},{1... | collective-permute-start | bytes 2359304 | tf_op jit(solution)/shard_map/ppermute | solution.py:31
  49.2 6.3 %collective-permute-start.7 = (bf16[2,48,4096]{2,1,0:T(8,128)(2,1)S(1)}, bf16[2,48,4096]{2,1,0:T(8,128)(2,1)S(1)}, u32[]{:S(2)}, u32[]{:S(2)}) collective-permute-start(bf16[2,48,4096]{2,1,0:T(8,128)(2,1)S(1)} %collective-permute-done.refs_2_), channel_id=1, source_target_pairs={{0,1},{1,0},{2,3},{3,2},{4,5},{5,4},{6,7},{7,6},{8,9},{9,8},{10,11... | collective-permute-start | bytes 2359304 | tf_op jit(solution)/shard_map/ppermute | solution.py:31
  55.5 22.7 %collective-permute-start.10 = (bf16[2,48,4096]{2,1,0:T(8,128)(2,1)S(1)}, bf16[2,48,4096]{2,1,0:T(8,128)(2,1)S(1)}, u32[]{:S(2)}, u32[]{:S(2)}) collective-permute-start(bf16[2,48,4096]{2,1,0:T(8,128)(2,1)S(1)} %collective-permute-done.2.refs_8_), channel_id=1, source_target_pairs={{0,4},{1,5},{2,6},{3,7},{4,8},{5,9},{6,10},{7,11},{8,12},{9,13},{1... | collective-permute-start | bytes 2359304 | tf_op jit(solution)/shard_map/ppermute | solution.py:31
  55.5 22.7 %collective-permute-start.11 = (bf16[2,48,4096]{2,1,0:T(8,128)(2,1)S(1)}, bf16[2,48,4096]{2,1,0:T(8,128)(2,1)S(1)}, u32[]{:S(2)}, u32[]{:S(2)}) collective-permute-start(bf16[2,48,4096]{2,1,0:T(8,128)(2,1)S(1)} %collective-permute-done.5.refs_12_), channel_id=1, source_target_pairs={{0,12},{1,13},{2,14},{3,15},{4,0},{5,1},{6,2},{7,3},{8,4},{9,5},{1... | collective-permute-start | bytes 2359304 | tf_op jit(solution)/shard_map/ppermute | solution.py:31
  58.9 12.3 %collective-permute-start.12 = (bf16[48,4096]{1,0:T(8,128)(2,1)S(1)}, bf16[48,4096]{1,0:T(8,128)(2,1)S(1)}, u32[]{:S(2)}, u32[]{:S(2)}) collective-permute-start(bf16[48,4096]{1,0:T(8,128)(2,1)S(1)} %collective-permute-done.3.refs_0_), channel_id=1, source_target_pairs={{0,2},{1,3},{2,0},{3,1},{4,6},{5,7},{6,4},{7,5},{8,10},{9,11},{10,... | collective-permute-start | bytes 1179656 | tf_op jit(solution)/shard_map/ppermute | solution.py:31
  59.6 18.6 %collective-permute-start.13 = (bf16[768,256]{1,0:T(8,128)(2,1)S(1)}, bf16[768,256]{1,0:T(8,128)(2,1)S(1)}, u32[]{:S(2)}, u32[]{:S(2)}) collective-permute-start(bf16[768,256]{1,0:T(8,128)(2,1)S(1)} %get-tuple-element.33), channel_id=1, source_target_pairs={{0,240},{16,224},{32,208},{48,192},{64,176},{80,160},{96,144},{112... | collective-permute-start | bytes 1179656 | tf_op jit(solution)/shard_map/ppermute | solution.py:52
  71.2 8.7 %collective-permute-start.15 = (bf16[2,48,4096]{2,1,0:T(8,128)(2,1)S(1)}, bf16[2,48,4096]{2,1,0:T(8,128)(2,1)S(1)}, u32[]{:S(2)}, u32[]{:S(2)}) collective-permute-start(bf16[2,48,4096]{2,1,0:T(8,128)(2,1)S(1)} %collective-permute-done.4.refs_6_), channel_id=1, source_target_pairs={{0,1},{1,0},{2,3},{3,2},{4,5},{5,4},{6,7},{7,6},{8,9},{9,8},{10,11... | collective-permute-start | bytes 2359304 | tf_op jit(solution)/shard_map/ppermute | solution.py:31
  73.8 8.8 %collective-permute-start.17 = (bf16[2,48,4096]{2,1,0:T(8,128)(2,1)S(1)}, bf16[2,48,4096]{2,1,0:T(8,128)(2,1)S(1)}, u32[]{:S(2)}, u32[]{:S(2)}) collective-permute-start(bf16[2,48,4096]{2,1,0:T(8,128)(2,1)S(1)} %collective-permute-done.5.refs_12_), channel_id=1, source_target_pairs={{0,1},{1,0},{2,3},{3,2},{4,5},{5,4},{6,7},{7,6},{8,9},{9,8},{10,11... | collective-permute-start | bytes 2359304 | tf_op jit(solution)/shard_map/ppermute | solution.py:31
  78.2 4.4 %collective-permute-start.16 = (bf16[2,48,4096]{2,1,0:T(8,128)(2,1)S(1)}, bf16[2,48,4096]{2,1,0:T(8,128)(2,1)S(1)}, u32[]{:S(2)}, u32[]{:S(2)}) collective-permute-start(bf16[2,48,4096]{2,1,0:T(8,128)(2,1)S(1)} %collective-permute-done.10.refs_10_), channel_id=1, source_target_pairs={{0,1},{1,0},{2,3},{3,2},{4,5},{5,4},{6,7},{7,6},{8,9},{9,8},{10,11... | collective-permute-start | bytes 2359304 | tf_op jit(solution)/shard_map/ppermute | solution.py:31
  79.8 3.0 %collective-permute-start.18 = (bf16[2,48,4096]{2,1,0:T(8,128)(2,1)S(1)}, bf16[2,48,4096]{2,1,0:T(8,128)(2,1)S(1)}, u32[]{:S(2)}, u32[]{:S(2)}) collective-permute-start(bf16[2,48,4096]{2,1,0:T(8,128)(2,1)S(1)} %collective-permute-done.11.refs_14_), channel_id=1, source_target_pairs={{0,1},{1,0},{2,3},{3,2},{4,5},{5,4},{6,7},{7,6},{8,9},{9,8},{10,11... | collective-permute-start | bytes 2359304 | tf_op jit(solution)/shard_map/ppermute | solution.py:31
  79.9 13.8 %collective-permute-start.14 = (bf16[48,4096]{1,0:T(8,128)(2,1)S(1)}, bf16[48,4096]{1,0:T(8,128)(2,1)S(1)}, u32[]{:S(2)}, u32[]{:S(2)}) collective-permute-start(bf16[48,4096]{1,0:T(8,128)(2,1)S(1)} %collective-permute-done.3.refs_0_), channel_id=1, source_target_pairs={{0,4},{1,5},{2,6},{3,7},{4,8},{5,9},{6,10},{7,11},{8,12},{9,13},{1... | collective-permute-start | bytes 1179656 | tf_op jit(solution)/shard_map/ppermute | solution.py:31
  79.9 29.7 %collective-permute-start.28 = (bf16[48,4096]{1,0:T(8,128)(2,1)S(1)}, bf16[48,4096]{1,0:T(8,128)(2,1)S(1)}, u32[]{:S(2)}, u32[]{:S(2)}) collective-permute-start(bf16[48,4096]{1,0:T(8,128)(2,1)S(1)} %collective-permute-done.3.refs_0_), channel_id=1, source_target_pairs={{0,12},{1,13},{2,14},{3,15},{4,0},{5,1},{6,2},{7,3},{8,4},{9,5},{1... | collective-permute-start | bytes 1179656 | tf_op jit(solution)/shard_map/ppermute | solution.py:31
  82.9 1.1 copy-start
  84.0 2.2 %copy-start.2 = (bf16[1,2,256,4096]{3,2,1,0:T(8,128)(2,1)S(1)}, bf16[1,2,256,4096]{3,2,1,0:T(8,128)(2,1)}, u32[]{:S(2)}) copy-start(bf16[1,2,256,4096]{3,2,1,0:T(8,128)(2,1)} %param.3) | copy-start | bytes 12582916
  86.2 7.6 %copy-start.1 = (bf16[1,2,48,4096]{3,2,1,0:T(8,128)(2,1)S(1)}, bf16[1,2,48,4096]{3,2,1,0:T(8,128)(2,1)}, u32[]{:S(2)}) copy-start(bf16[1,2,48,4096]{3,2,1,0:T(8,128)(2,1)} %param.5) | copy-start | bytes 2359300
  91.0 23.0 %collective-permute-start.31 = (bf16[48,4096]{1,0:T(8,128)(2,1)S(1)}, bf16[48,4096]{1,0:T(8,128)(2,1)S(1)}, u32[]{:S(2)}, u32[]{:S(2)}) collective-permute-start(bf16[48,4096]{1,0:T(8,128)(2,1)S(1)} %collective-permute-done.12.refs_6_), channel_id=1, source_target_pairs={{0,4},{1,5},{2,6},{3,7},{4,8},{5,9},{6,10},{7,11},{8,12},{9,13},{1... | collective-permute-start | bytes 1179656 | tf_op jit(solution)/shard_map/ppermute | solution.py:31
  91.1 11.4 %collective-permute-start.21 = (bf16[48,4096]{1,0:T(8,128)(2,1)S(1)}, bf16[48,4096]{1,0:T(8,128)(2,1)S(1)}, u32[]{:S(2)}, u32[]{:S(2)}) collective-permute-start(bf16[48,4096]{1,0:T(8,128)(2,1)S(1)} %collective-permute-done.12.refs_6_), channel_id=1, source_target_pairs={{0,12},{1,13},{2,14},{3,15},{4,0},{5,1},{6,2},{7,3},{8,4},{9,5},{1... | collective-permute-start | bytes 1179656 | tf_op jit(solution)/shard_map/ppermute | solution.py:31
  93.8 17.2 %collective-permute-start.19 = (bf16[48,4096]{1,0:T(8,128)(2,1)S(1)}, bf16[48,4096]{1,0:T(8,128)(2,1)S(1)}, u32[]{:S(2)}, u32[]{:S(2)}) collective-permute-start(bf16[48,4096]{1,0:T(8,128)(2,1)S(1)} %collective-permute-done.14.refs_2_), channel_id=1, source_target_pairs={{0,4},{1,5},{2,6},{3,7},{4,8},{5,9},{6,10},{7,11},{8,12},{9,13},{1... | collective-permute-start | bytes 1179656 | tf_op jit(solution)/shard_map/ppermute | solution.py:31
  101.1 14.5 %collective-permute-start.26 = (bf16[48,4096]{1,0:T(8,128)(2,1)S(1)}, bf16[48,4096]{1,0:T(8,128)(2,1)S(1)}, u32[]{:S(2)}, u32[]{:S(2)}) collective-permute-start(bf16[48,4096]{1,0:T(8,128)(2,1)S(1)} %collective-permute-done.3.refs_0_), channel_id=1, source_target_pairs={{0,1},{1,0},{2,3},{3,2},{4,5},{5,4},{6,7},{7,6},{8,9},{9,8},{10,11... | collective-permute-start | bytes 1179656 | tf_op jit(solution)/shard_map/ppermute | solution.py:31
  102.5 20.0 %collective-permute-start.24 = (bf16[768,256]{1,0:T(8,128)(2,1)S(1)}, bf16[768,256]{1,0:T(8,128)(2,1)S(1)}, u32[]{:S(2)}, u32[]{:S(2)}) collective-permute-start(bf16[768,256]{1,0:T(8,128)(2,1)S(1)} %get-tuple-element.42), channel_id=1, source_target_pairs={{0,16},{16,32},{32,48},{48,64},{64,80},{80,96},{96,112},{112,128},... | collective-permute-start | bytes 1179656 | tf_op jit(solution)/shard_map/ppermute | solution.py:58
  109.7 20.7 %collective-permute-start.23 = (bf16[768,256]{1,0:T(8,128)(2,1)S(1)}, bf16[768,256]{1,0:T(8,128)(2,1)S(1)}, u32[]{:S(2)}, u32[]{:S(2)}) collective-permute-start(bf16[768,256]{1,0:T(8,128)(2,1)S(1)} %get-tuple-element.39), channel_id=1, source_target_pairs={{16,0},{32,16},{48,32},{64,48},{80,64},{96,80},{112,96},{128,112},... | collective-permute-start | bytes 1179656 | tf_op jit(solution)/shard_map/ppermute | solution.py:58
  111.0 20.1 %collective-permute-start.22 = (bf16[48,4096]{1,0:T(8,128)(2,1)S(1)}, bf16[48,4096]{1,0:T(8,128)(2,1)S(1)}, u32[]{:S(2)}, u32[]{:S(2)}) collective-permute-start(bf16[48,4096]{1,0:T(8,128)(2,1)S(1)} %collective-permute-done.21.refs_10_), channel_id=1, source_target_pairs={{0,12},{1,13},{2,14},{3,15},{4,0},{5,1},{6,2},{7,3},{8,4},{9,5},{1... | collective-permute-start | bytes 1179656 | tf_op jit(solution)/shard_map/ppermute | solution.py:31
  114.0 17.1 %collective-permute-start.27 = (bf16[48,4096]{1,0:T(8,128)(2,1)S(1)}, bf16[48,4096]{1,0:T(8,128)(2,1)S(1)}, u32[]{:S(2)}, u32[]{:S(2)}) collective-permute-start(bf16[48,4096]{1,0:T(8,128)(2,1)S(1)} %collective-permute-done.14.refs_2_), channel_id=1, source_target_pairs={{0,1},{1,0},{2,3},{3,2},{4,5},{5,4},{6,7},{7,6},{8,9},{9,8},{10,11... | collective-permute-start | bytes 1179656 | tf_op jit(solution)/shard_map/ppermute | solution.py:31
  115.6 16.0 %collective-permute-start.29 = (bf16[48,4096]{1,0:T(8,128)(2,1)S(1)}, bf16[48,4096]{1,0:T(8,128)(2,1)S(1)}, u32[]{:S(2)}, u32[]{:S(2)}) collective-permute-start(bf16[48,4096]{1,0:T(8,128)(2,1)S(1)} %collective-permute-done.28.refs_4_), channel_id=1, source_target_pairs={{0,1},{1,0},{2,3},{3,2},{4,5},{5,4},{6,7},{7,6},{8,9},{9,8},{10,11... | collective-permute-start | bytes 1179656 | tf_op jit(solution)/shard_map/ppermute | solution.py:31
  122.5 10.2 %collective-permute-start.30 = (bf16[48,4096]{1,0:T(8,128)(2,1)S(1)}, bf16[48,4096]{1,0:T(8,128)(2,1)S(1)}, u32[]{:S(2)}, u32[]{:S(2)}) collective-permute-start(bf16[48,4096]{1,0:T(8,128)(2,1)S(1)} %collective-permute-done.12.refs_6_), channel_id=1, source_target_pairs={{0,1},{1,0},{2,3},{3,2},{4,5},{5,4},{6,7},{7,6},{8,9},{9,8},{10,11... | collective-permute-start | bytes 1179656 | tf_op jit(solution)/shard_map/ppermute | solution.py:31
  130.4 2.3 %collective-permute-start.32 = (bf16[48,4096]{1,0:T(8,128)(2,1)S(1)}, bf16[48,4096]{1,0:T(8,128)(2,1)S(1)}, u32[]{:S(2)}, u32[]{:S(2)}) collective-permute-start(bf16[48,4096]{1,0:T(8,128)(2,1)S(1)} %collective-permute-done.31.refs_8_), channel_id=1, source_target_pairs={{0,1},{1,0},{2,3},{3,2},{4,5},{5,4},{6,7},{7,6},{8,9},{9,8},{10,11... | collective-permute-start | bytes 1179656 | tf_op jit(solution)/shard_map/ppermute | solution.py:31
  131.1 1.9 %collective-permute-start.33 = (bf16[48,4096]{1,0:T(8,128)(2,1)S(1)}, bf16[48,4096]{1,0:T(8,128)(2,1)S(1)}, u32[]{:S(2)}, u32[]{:S(2)}) collective-permute-start(bf16[48,4096]{1,0:T(8,128)(2,1)S(1)} %collective-permute-done.21.refs_10_), channel_id=1, source_target_pairs={{0,1},{1,0},{2,3},{3,2},{4,5},{5,4},{6,7},{7,6},{8,9},{9,8},{10,11... | collective-permute-start | bytes 1179656 | tf_op jit(solution)/shard_map/ppermute | solution.py:31
  131.1 8.3 %collective-permute-start.20 = (bf16[48,4096]{1,0:T(8,128)(2,1)S(1)}, bf16[48,4096]{1,0:T(8,128)(2,1)S(1)}, u32[]{:S(2)}, u32[]{:S(2)}) collective-permute-start(bf16[48,4096]{1,0:T(8,128)(2,1)S(1)} %collective-permute-done.19.refs_0_), channel_id=1, source_target_pairs={{0,1},{1,0},{2,3},{3,2},{4,5},{5,4},{6,7},{7,6},{8,9},{9,8},{10,11... | collective-permute-start | bytes 1179656 | tf_op jit(solution)/shard_map/ppermute | solution.py:31
  131.6 7.8 %collective-permute-start.25 = (bf16[48,4096]{1,0:T(8,128)(2,1)S(1)}, bf16[48,4096]{1,0:T(8,128)(2,1)S(1)}, u32[]{:S(2)}, u32[]{:S(2)}) collective-permute-start(bf16[48,4096]{1,0:T(8,128)(2,1)S(1)} %collective-permute-done.22.refs_2_), channel_id=1, source_target_pairs={{0,1},{1,0},{2,3},{3,2},{4,5},{5,4},{6,7},{7,6},{8,9},{9,8},{10,11... | collective-permute-start | bytes 1179656 | tf_op jit(solution)/shard_map/ppermute | solution.py:31

commit v4 on v3

--- a/solution.py
+++ b/solution.py
@@ -177,12 +177,10 @@
         far[0, 0, 0],
         *share(near, (0, 0), (-1, 0), (1, 0), (0, 1)),
     ]
-    far_context = mirrored(after(up_context, *step))
     step = [
         send(near, upward, (0, 1), (-1, 1), *step),
         send(near, downward, (1, 1), (2, 1), *step),
         send(far, across, (0, 0), (0, 1), *step),
-        far_context,
     ]
     for spot in ((2, 0), (1, 1)):
         send(near, to_sibling, spot, spot, far[0, 1, 0])
@@ -190,6 +188,7 @@
         send(near, to_sibling, spot, spot, *step)
     send(far, upward, (0, 0), (-1, 0), *step)
     send(far, downward, (0, 0), (1, 0), *step)
+    far_context = mirrored(after(up_context, *step))
 
     back_shape = jax.ShapeDtypeStruct((tokens, width_in), jnp.bfloat16)
     back = pl.pallas_call(
@@ -203,7 +202,7 @@
             pltpu.SemaphoreType.DMA((len(NEAR),)),
             pltpu.SemaphoreType.DMA((2,)),
         ],
-        compiler_params=pltpu.CompilerParams(vmem_limit_bytes=20 * 2**20),
+        compiler_params=pltpu.CompilerParams(vmem_limit_bytes=40 * 2**20),
         cost_estimate=pl.CostEstimate(
             flops=2 * flops, bytes_accessed=4 * (tokens + width_in) * width_out, transcendentals=0
         ),
@@ -243,13 +242,15 @@
             ),
         )(*blocks, held, *([] if total is None else [total]))
 
-    (total,) = summed(NEAR, [near[key] for key in NEAR], after(context[0, 0], *back), None, ())
-    send(far, downward, (1, 1), (2, 1), total)
+    (total,) = summed(NEAR, [near[key] for key in NEAR], after(context[0, 0], *back, far[1, 1, 0]), None, ())
+    send(far, downward, (1, 1), (2, 1))
     for spot in ((0, 0), (0, 1), (-1, 0), (1, 0)):
-        send(far, to_sibling, spot, spot, total)
+        send(far, to_sibling, spot, spot, total, far_context)
     share(far, (-1, 1), (1, 1), (2, 0))
-    send(far, to_sibling, (2, 1), (2, 1), from_next, from_prior)
-    total, late_context = summed(EARLY, [far[key] for key in EARLY], far_context, total, LATE)
+    total, late_context = summed(
+        EARLY, [far[key] for key in EARLY], after(far_context, from_next, from_prior), total, LATE
+    )
+    send(far, to_sibling, (2, 1), (2, 1), total)
     late = len(LATE) * rows
 
     wide = 1024

time: 143 us -> 139 us (0.972)
  the two profiles are of different devices: /device:TPU:1 before, /device:TPU:58 now
where the time goes in v4:
time: 139 us; the launch traced here: 136 us
  waiting for transfers between devices  69.1 us (50%)
  starting transfers between devices  39.8 us (29%)
  Pallas kernels  22.4 us (16%)
  local copies, waits for them, and re-layouts  3.35 us (2%)
    ppermute x30, waiting for transfers between devices, moved(): return lax.ppermute(value, 'tensor', pairs)  43.6 us
    ppermute x30, starting transfers between devices, moved(): return lax.ppermute(value, 'tensor', pairs)  22.5 us
    pallas_call x2, Pallas kernels, summed(): pl.pallas_call(functools.partial(sum_kernel, keys, late, total is not Non...  13.8 us
    ppermute x2, waiting for transfers between devices, mirrored(): lax.ppermute(value, 'pipe', [(i, count - 1 - i) for i in range(count)])  12.9 us
    ppermute x2, waiting for transfers between devices, from_behind(): return lax.ppermute(value, 'pipe', pairs)  12.6 us
    ppermute x2, starting transfers between devices, from_behind(): return lax.ppermute(value, 'pipe', pairs)  10.3 us
    ppermute x2, starting transfers between devices, mirrored(): lax.ppermute(value, 'pipe', [(i, count - 1 - i) for i in range(count)])  6.97 us
    pallas_call x1, Pallas kernels, shards(): pl.pallas_call(back_kernel, out_shape=(back_shape,) * 2, in_specs=[HBM] +...  5.85 us
  transfers between devices with their start and end apart: 34, of which 16 were waited for; matrix products, arithmetic and copies ran while one was open for 2% of the time, Pallas kernels for 14%

profile of v4, /device:TPU:58, one launch (start us, length us, event | category | flops | bytes accessed | tf_op | source)
XLA Modules:
  0.0 136.3 jit_solution(1758191242352089348)
XLA Ops:
  0.6 0.2 collective-permute-start.2
  0.8 0.2 collective-permute-start
  1.0 1.8 %collective-permute-start.1 = (bf16[2,48,4096]{2,1,0:T(8,128)(2,1)}, bf16[2,48,4096]{2,1,0:T(8,128)(2,1)S(1)}, u32[]{:S(2)}, u32[]{:S(2)}) collective-permute-start(bf16[2,48,4096]{2,1,0:T(8,128)(2,1)} %bitcast.15), channel_id=1, source_target_pairs={{0,12},{1,13},{2,14},{3,15},{4,0},{5,1},{6,2},{7,3},{8,4},{9,5},{1... | collective-permute-start | bytes 2359304 | tf_op jit(solution)/shard_map/ppermute | solution.py:31
  2.9 0.0 collective-permute-start.6
  2.9 1.1 slice_bitcast_fusion.2
  3.9 16.3 %collective-permute-done.2.refs_8_ = bf16[2,48,4096]{2,1,0:T(8,128)(2,1)S(1)} collective-permute-done((bf16[2,48,4096]{2,1,0:T(8,128)(2,1)}, bf16[2,48,4096]{2,1,0:T(8,128)(2,1)S(1)}, u32[]{:S(2)}, u32[]{:S(2)}) %collective-permute-start.2) | collective-permute-done | bytes 786464 | tf_op jit(solution)/shard_map/ppermute | solution.py:31
  20.2 0.1 collective-permute-done.refs_2_
  20.3 1.3 collective-permute-done.1.refs_4_
  21.6 6.9 %collective-permute-start.3 = (bf16[48,4096]{1,0:T(8,128)(2,1)S(1)}, bf16[48,4096]{1,0:T(8,128)(2,1)S(1)}, u32[]{:S(2)}, u32[]{:S(2)}) collective-permute-start(bf16[48,4096]{1,0:T(8,128)(2,1)S(1)} %slice_bitcast_fusion.2), channel_id=1, source_target_pairs={{0,240},{16,224},{32,208},{48,192},{64,176},{80,160},{96,144},{112... | collective-permute-start | bytes 1179656 | tf_op jit(solution)/shard_map/ppermute | solution.py:52
  28.5 1.2 slice_bitcast_fusion
  29.6 0.4 collective-permute-start.4
  30.0 1.7 %collective-permute-start.5 = (bf16[2,48,4096]{2,1,0:T(8,128)(2,1)S(1)}, bf16[2,48,4096]{2,1,0:T(8,128)(2,1)S(1)}, u32[]{:S(2)}, u32[]{:S(2)}) collective-permute-start(bf16[2,48,4096]{2,1,0:T(8,128)(2,1)S(1)} %collective-permute-done.2.refs_8_), channel_id=1, source_target_pairs={{0,12},{1,13},{2,14},{3,15},{4,0},{5,1},{6,2},{7,3},{8,4},{9,5},{1... | collective-permute-start | bytes 2359304 | tf_op jit(solution)/shard_map/ppermute | solution.py:31
  31.8 0.0 collective-permute-start.9
  31.8 0.0 collective-permute-done.6.refs_1_
  31.8 0.5 collective-permute-start.7
  32.3 12.3 %collective-permute-done.3.refs_0_ = bf16[48,4096]{1,0:T(8,128)(2,1)S(1)} collective-permute-done((bf16[48,4096]{1,0:T(8,128)(2,1)S(1)}, bf16[48,4096]{1,0:T(8,128)(2,1)S(1)}, u32[]{:S(2)}, u32[]{:S(2)}) %collective-permute-start.3) | collective-permute-done | bytes 393248 | tf_op jit(solution)/shard_map/ppermute | solution.py:52
  44.6 0.0 collective-permute-start.8
  44.6 2.7 %collective-permute-done.4.refs_6_ = bf16[2,48,4096]{2,1,0:T(8,128)(2,1)S(1)} collective-permute-done((bf16[2,48,4096]{2,1,0:T(8,128)(2,1)S(1)}, bf16[2,48,4096]{2,1,0:T(8,128)(2,1)S(1)}, u32[]{:S(2)}, u32[]{:S(2)}) %collective-permute-start.4) | collective-permute-done | bytes 786464 | tf_op jit(solution)/shard_map/ppermute | solution.py:31
  47.3 1.6 %collective-permute-done.5.refs_12_ = bf16[2,48,4096]{2,1,0:T(8,128)(2,1)S(1)} collective-permute-done((bf16[2,48,4096]{2,1,0:T(8,128)(2,1)S(1)}, bf16[2,48,4096]{2,1,0:T(8,128)(2,1)S(1)}, u32[]{:S(2)}, u32[]{:S(2)}) %collective-permute-start.5) | collective-permute-done | bytes 786464 | tf_op jit(solution)/shard_map/ppermute | solution.py:31
  48.9 0.2 collective-permute-start.11
  49.1 3.1 %collective-permute-start.10 = (bf16[2,48,4096]{2,1,0:T(8,128)(2,1)S(1)}, bf16[2,48,4096]{2,1,0:T(8,128)(2,1)S(1)}, u32[]{:S(2)}, u32[]{:S(2)}) collective-permute-start(bf16[2,48,4096]{2,1,0:T(8,128)(2,1)S(1)} %collective-permute-done.2.refs_8_), channel_id=1, source_target_pairs={{0,4},{1,5},{2,6},{3,7},{4,8},{5,9},{6,10},{7,11},{8,12},{9,13},{1... | collective-permute-start | bytes 2359304 | tf_op jit(solution)/shard_map/ppermute | solution.py:31
  52.2 1.0 collective-permute-start.12
  53.2 7.5 %collective-permute-done.12.refs_6_ = bf16[48,4096]{1,0:T(8,128)(2,1)S(1)} collective-permute-done((bf16[48,4096]{1,0:T(8,128)(2,1)S(1)}, bf16[48,4096]{1,0:T(8,128)(2,1)S(1)}, u32[]{:S(2)}, u32[]{:S(2)}) %collective-permute-start.12) | collective-permute-done | bytes 393248 | tf_op jit(solution)/shard_map/ppermute | solution.py:31
  60.7 0.5 collective-permute-start.14
  61.2 6.4 %collective-permute-done.11.refs_14_ = bf16[2,48,4096]{2,1,0:T(8,128)(2,1)S(1)} collective-permute-done((bf16[2,48,4096]{2,1,0:T(8,128)(2,1)S(1)}, bf16[2,48,4096]{2,1,0:T(8,128)(2,1)S(1)}, u32[]{:S(2)}, u32[]{:S(2)}) %collective-permute-start.11) | collective-permute-done | bytes 786464 | tf_op jit(solution)/shard_map/ppermute | solution.py:31
  67.7 0.0 collective-permute-start.17
  67.7 0.5 collective-permute-start.15
  68.2 3.0 %collective-permute-start.13 = (bf16[48,4096]{1,0:T(8,128)(2,1)S(1)}, bf16[48,4096]{1,0:T(8,128)(2,1)S(1)}, u32[]{:S(2)}, u32[]{:S(2)}) collective-permute-start(bf16[48,4096]{1,0:T(8,128)(2,1)S(1)} %collective-permute-done.3.refs_0_), channel_id=1, source_target_pairs={{0,4},{1,5},{2,6},{3,7},{4,8},{5,9},{6,10},{7,11},{8,12},{9,13},{1... | collective-permute-start | bytes 1179656 | tf_op jit(solution)/shard_map/ppermute | solution.py:31
  71.1 0.0 collective-permute-done.16.refs_13_
  71.2 0.0 collective-permute-done.15.refs_11_
  71.2 0.0 copy-start
  71.2 1.1 copy-done
  72.3 5.9 %shard_map.50 = (bf16[768,256]{1,0:T(8,128)(2,1)S(1)}, bf16[768,256]{1,0:T(8,128)(2,1)S(1)}) custom-call(bf16[2,48,4096]{2,1,0:T(8,128)(2,1)S(1)} %bitcast.17, bf16[2,48,4096]{2,1,0:T(8,128)(2,1)S(1)} %collective-permute-done.6.refs_1_, bf16[2,48,4096]{2,1,0:T(8,128)(2,1)S(1)} %collective-permute-done.refs_2_, ...), custom_call_target="tpu_custom_call" | custom-call | flops 3221225472 | bytes 16777216 | tf_op jit(solution)/shard_map/pallas_call | solution.py:194
  78.2 0.1 collective-permute-start.20
  78.3 0.1 collective-permute-start.22
  78.4 1.2 collective-permute-start.25
  79.6 7.7 %collective-permute-start.31 = (bf16[768,256]{1,0:T(8,128)(2,1)S(1)}, bf16[768,256]{1,0:T(8,128)(2,1)S(1)}, u32[]{:S(2)}, u32[]{:S(2)}) collective-permute-start(bf16[768,256]{1,0:T(8,128)(2,1)S(1)} %get-tuple-element.38), channel_id=1, source_target_pairs={{16,0},{32,16},{48,32},{64,48},{80,64},{96,80},{112,96},{128,112},... | collective-permute-start | bytes 1179656 | tf_op jit(solution)/shard_map/ppermute | solution.py:58
  87.3 2.1 %collective-permute-start.28 = (bf16[48,4096]{1,0:T(8,128)(2,1)S(1)}, bf16[48,4096]{1,0:T(8,128)(2,1)S(1)}, u32[]{:S(2)}, u32[]{:S(2)}) collective-permute-start(bf16[48,4096]{1,0:T(8,128)(2,1)S(1)} %collective-permute-done.12.refs_6_), channel_id=1, source_target_pairs={{0,4},{1,5},{2,6},{3,7},{4,8},{5,9},{6,10},{7,11},{8,12},{9,13},{1... | collective-permute-start | bytes 1179656 | tf_op jit(solution)/shard_map/ppermute | solution.py:31
  89.3 2.1 %collective-permute-done.20.refs_10_ = bf16[48,4096]{1,0:T(8,128)(2,1)S(1)} collective-permute-done((bf16[48,4096]{1,0:T(8,128)(2,1)S(1)}, bf16[48,4096]{1,0:T(8,128)(2,1)S(1)}, u32[]{:S(2)}, u32[]{:S(2)}) %collective-permute-start.20) | collective-permute-done | bytes 393248 | tf_op jit(solution)/shard_map/ppermute | solution.py:31
  91.4 2.6 %collective-permute-start.32 = (bf16[768,256]{1,0:T(8,128)(2,1)S(1)}, bf16[768,256]{1,0:T(8,128)(2,1)S(1)}, u32[]{:S(2)}, u32[]{:S(2)}) collective-permute-start(bf16[768,256]{1,0:T(8,128)(2,1)S(1)} %get-tuple-element.41), channel_id=1, source_target_pairs={{0,16},{16,32},{32,48},{48,64},{64,80},{80,96},{96,112},{112,128},... | collective-permute-start | bytes 1179656 | tf_op jit(solution)/shard_map/ppermute | solution.py:58
  94.0 7.4 %shard_map.51.refs_13_ = f32[256,4096]{1,0:T(8,128)S(1)} custom-call(bf16[2,48,4096]{2,1,0:T(8,128)(2,1)S(1)} %bitcast.18, bf16[2,48,4096]{2,1,0:T(8,128)(2,1)S(1)} %collective-permute-done.6.refs_1_, bf16[2,48,4096]{2,1,0:T(8,128)(2,1)S(1)} %collective-permute-done.refs_2_, bf16[2,48,4096]{2,1,0:T(8,128)(2,1)S(1)} %collective-permute-done.7.refs_3_, ...), custom_call_target="tpu_custom_call" | custom-call | flops 1610612736 | bytes 12582912 | tf_op jit(solution)/shard_map/pallas_call | solution.py:225
  101.4 0.6 collective-permute-done.22.refs_12_
  102.0 3.4 %collective-permute-start.18 = (bf16[48,4096]{1,0:T(8,128)(2,1)S(1)}, bf16[48,4096]{1,0:T(8,128)(2,1)S(1)}, u32[]{:S(2)}, u32[]{:S(2)}) collective-permute-start(bf16[48,4096]{1,0:T(8,128)(2,1)S(1)} %collective-permute-done.13.refs_2_), channel_id=1, source_target_pairs={{0,4},{1,5},{2,6},{3,7},{4,8},{5,9},{6,10},{7,11},{8,12},{9,13},{1... | collective-permute-start | bytes 1179656 | tf_op jit(solution)/shard_map/ppermute | solution.py:31
  105.3 0.0 collective-permute-done.25.refs_4_
  105.3 0.0 collective-permute-start.27
  105.3 0.5 collective-permute-start.26
  105.8 12.6 %collective-permute-done.32 = bf16[768,256]{1,0:T(8,128)(2,1)S(1)} collective-permute-done((bf16[768,256]{1,0:T(8,128)(2,1)S(1)}, bf16[768,256]{1,0:T(8,128)(2,1)S(1)}, u32[]{:S(2)}, u32[]{:S(2)}) %collective-permute-start.32) | collective-permute-done | bytes 393248 | tf_op jit(solution)/shard_map/ppermute | solution.py:58
  118.4 0.0 collective-permute-start.24
  118.5 0.5 collective-permute-start.23
  119.0 0.1 collective-permute-start.29
  119.0 0.0 collective-permute-done.27.refs_7_
  119.0 0.4 collective-permute-start.30
  119.5 1.1 collective-permute-start.21
  120.6 0.0 collective-permute-done.24.refs_3_
  120.6 0.0 collective-permute-start.19
  120.6 0.1 collective-permute-done.23.refs_1_
  120.7 0.6 collective-permute-done.29.refs_9_
  121.3 0.6 collective-permute-done.30.refs_11_
  121.8 6.4 %shard_map.52 = (f32[256,4096]{1,0:T(8,128)S(1)}, bf16[256,192]{1,0:T(8,128)(2,1)S(1)}) custom-call(bf16[48,4096]{1,0:T(8,128)(2,1)S(1)} %collective-permute-done.3.refs_0_, bf16[48,4096]{1,0:T(8,128)(2,1)S(1)} %collective-permute-done.23.refs_1_, bf16[48,4096]{1,0:T(8,128)(2,1)S(1)} %collective-permute-done.13.refs_2_, ...), custom_call_target="tpu_custom_call" | custom-call | flops 1207959552 | bytes 11010048 | tf_op jit(solution)/shard_map/pallas_call | solution.py:225
  128.3 3.5 %collective-permute-done.21.refs_2_ = bf16[48,4096]{1,0:T(8,128)(2,1)S(1)} collective-permute-done((bf16[48,4096]{1,0:T(8,128)(2,1)S(1)}, bf16[48,4096]{1,0:T(8,128)(2,1)S(1)}, u32[]{:S(2)}, u32[]{:S(2)}) %collective-permute-start.21) | collective-permute-done | bytes 393248 | tf_op jit(solution)/shard_map/ppermute | solution.py:31
  131.8 0.0 collective-permute-start.33
  131.8 0.9 maximum_bitcast_fusion
  132.7 0.8 collective-permute-done.33.refs_3_
  133.5 2.8 %shard_map.53 = bf16[256,4096]{1,0:T(8,128)(2,1)} custom-call(bf16[48,4096]{1,0:T(8,128)(2,1)S(1)} %collective-permute-done.18.refs_0_, bf16[48,4096]{1,0:T(8,128)(2,1)S(1)} %collective-permute-done.19.refs_1_, bf16[48,4096]{1,0:T(8,128)(2,1)S(1)} %collective-permute-done.21.refs_2_, bf16[48,4096]{1,0:T(8,128)(2,1)S(1)} %collective-permute-done.33.refs_3_, ...), custom_call_target="tpu_custom_call" | custom-call | flops 402653184 | bytes 7864320 | tf_op jit(solution)/shard_map/pallas_call | solution.py:258
  (13 shorter events, 0.0 us)
Async XLA Ops:
  0.6 19.6 %collective-permute-start.2 = (bf16[2,48,4096]{2,1,0:T(8,128)(2,1)}, bf16[2,48,4096]{2,1,0:T(8,128)(2,1)S(1)}, u32[]{:S(2)}, u32[]{:S(2)}) collective-permute-start(bf16[2,48,4096]{2,1,0:T(8,128)(2,1)} %bitcast.13), channel_id=1, source_target_pairs={{0,2},{1,3},{2,0},{3,1},{4,6},{5,7},{6,4},{7,5},{8,10},{9,11},{10,... | collective-permute-start | bytes 2359304 | tf_op jit(solution)/shard_map/ppermute | solution.py:31
  0.8 19.5 %collective-permute-start = (bf16[2,48,4096]{2,1,0:T(8,128)(2,1)}, bf16[2,48,4096]{2,1,0:T(8,128)(2,1)S(1)}, u32[]{:S(2)}, u32[]{:S(2)}) collective-permute-start(bf16[2,48,4096]{2,1,0:T(8,128)(2,1)} %bitcast.14), channel_id=1, source_target_pairs={{0,4},{1,5},{2,6},{3,7},{4,8},{5,9},{6,10},{7,11},{8,12},{9,13},{1... | collective-permute-start | bytes 2359304 | tf_op jit(solution)/shard_map/ppermute | solution.py:31
  1.0 20.6 %collective-permute-start.1 = (bf16[2,48,4096]{2,1,0:T(8,128)(2,1)}, bf16[2,48,4096]{2,1,0:T(8,128)(2,1)S(1)}, u32[]{:S(2)}, u32[]{:S(2)}) collective-permute-start(bf16[2,48,4096]{2,1,0:T(8,128)(2,1)} %bitcast.15), channel_id=1, source_target_pairs={{0,12},{1,13},{2,14},{3,15},{4,0},{5,1},{6,2},{7,3},{8,4},{9,5},{1... | collective-permute-start | bytes 2359304 | tf_op jit(solution)/shard_map/ppermute | solution.py:31
  2.9 28.9 %collective-permute-start.6 = (bf16[2,48,4096]{2,1,0:T(8,128)(2,1)}, bf16[2,48,4096]{2,1,0:T(8,128)(2,1)S(1)}, u32[]{:S(2)}, u32[]{:S(2)}) collective-permute-start(bf16[2,48,4096]{2,1,0:T(8,128)(2,1)} %bitcast.16), channel_id=1, source_target_pairs={{0,1},{1,0},{2,3},{3,2},{4,5},{5,4},{6,7},{7,6},{8,9},{9,8},{10,11... | collective-permute-start | bytes 2359304 | tf_op jit(solution)/shard_map/ppermute | solution.py:31
  21.6 23.0 %collective-permute-start.3 = (bf16[48,4096]{1,0:T(8,128)(2,1)S(1)}, bf16[48,4096]{1,0:T(8,128)(2,1)S(1)}, u32[]{:S(2)}, u32[]{:S(2)}) collective-permute-start(bf16[48,4096]{1,0:T(8,128)(2,1)S(1)} %slice_bitcast_fusion.2), channel_id=1, source_target_pairs={{0,240},{16,224},{32,208},{48,192},{64,176},{80,160},{96,144},{112... | collective-permute-start | bytes 1179656 | tf_op jit(solution)/shard_map/ppermute | solution.py:52
  29.6 17.7 %collective-permute-start.4 = (bf16[2,48,4096]{2,1,0:T(8,128)(2,1)S(1)}, bf16[2,48,4096]{2,1,0:T(8,128)(2,1)S(1)}, u32[]{:S(2)}, u32[]{:S(2)}) collective-permute-start(bf16[2,48,4096]{2,1,0:T(8,128)(2,1)S(1)} %collective-permute-done.refs_2_), channel_id=1, source_target_pairs={{0,4},{1,5},{2,6},{3,7},{4,8},{5,9},{6,10},{7,11},{8,12},{9,13},{1... | collective-permute-start | bytes 2359304 | tf_op jit(solution)/shard_map/ppermute | solution.py:31
  30.0 18.8 %collective-permute-start.5 = (bf16[2,48,4096]{2,1,0:T(8,128)(2,1)S(1)}, bf16[2,48,4096]{2,1,0:T(8,128)(2,1)S(1)}, u32[]{:S(2)}, u32[]{:S(2)}) collective-permute-start(bf16[2,48,4096]{2,1,0:T(8,128)(2,1)S(1)} %collective-permute-done.2.refs_8_), channel_id=1, source_target_pairs={{0,12},{1,13},{2,14},{3,15},{4,0},{5,1},{6,2},{7,3},{8,4},{9,5},{1... | collective-permute-start | bytes 2359304 | tf_op jit(solution)/shard_map/ppermute | solution.py:31
  31.8 17.1 %collective-permute-start.9 = (bf16[2,48,4096]{2,1,0:T(8,128)(2,1)S(1)}, bf16[2,48,4096]{2,1,0:T(8,128)(2,1)S(1)}, u32[]{:S(2)}, u32[]{:S(2)}) collective-permute-start(bf16[2,48,4096]{2,1,0:T(8,128)(2,1)S(1)} %collective-permute-done.2.refs_8_), channel_id=1, source_target_pairs={{0,1},{1,0},{2,3},{3,2},{4,5},{5,4},{6,7},{7,6},{8,9},{9,8},{10,11... | collective-permute-start | bytes 2359304 | tf_op jit(solution)/shard_map/ppermute | solution.py:31
  31.8 17.1 %collective-permute-start.7 = (bf16[2,48,4096]{2,1,0:T(8,128)(2,1)S(1)}, bf16[2,48,4096]{2,1,0:T(8,128)(2,1)S(1)}, u32[]{:S(2)}, u32[]{:S(2)}) collective-permute-start(bf16[2,48,4096]{2,1,0:T(8,128)(2,1)S(1)} %collective-permute-done.refs_2_), channel_id=1, source_target_pairs={{0,1},{1,0},{2,3},{3,2},{4,5},{5,4},{6,7},{7,6},{8,9},{9,8},{10,11... | collective-permute-start | bytes 2359304 | tf_op jit(solution)/shard_map/ppermute | solution.py:31
  44.6 4.3 %collective-permute-start.8 = (bf16[2,48,4096]{2,1,0:T(8,128)(2,1)S(1)}, bf16[2,48,4096]{2,1,0:T(8,128)(2,1)S(1)}, u32[]{:S(2)}, u32[]{:S(2)}) collective-permute-start(bf16[2,48,4096]{2,1,0:T(8,128)(2,1)S(1)} %collective-permute-done.1.refs_4_), channel_id=1, source_target_pairs={{0,1},{1,0},{2,3},{3,2},{4,5},{5,4},{6,7},{7,6},{8,9},{9,8},{10,11... | collective-permute-start | bytes 2359304 | tf_op jit(solution)/shard_map/ppermute | solution.py:31
  48.9 18.8 %collective-permute-start.11 = (bf16[2,48,4096]{2,1,0:T(8,128)(2,1)S(1)}, bf16[2,48,4096]{2,1,0:T(8,128)(2,1)S(1)}, u32[]{:S(2)}, u32[]{:S(2)}) collective-permute-start(bf16[2,48,4096]{2,1,0:T(8,128)(2,1)S(1)} %collective-permute-done.5.refs_12_), channel_id=1, source_target_pairs={{0,12},{1,13},{2,14},{3,15},{4,0},{5,1},{6,2},{7,3},{8,4},{9,5},{1... | collective-permute-start | bytes 2359304 | tf_op jit(solution)/shard_map/ppermute | solution.py:31
  49.1 18.5 %collective-permute-start.10 = (bf16[2,48,4096]{2,1,0:T(8,128)(2,1)S(1)}, bf16[2,48,4096]{2,1,0:T(8,128)(2,1)S(1)}, u32[]{:S(2)}, u32[]{:S(2)}) collective-permute-start(bf16[2,48,4096]{2,1,0:T(8,128)(2,1)S(1)} %collective-permute-done.2.refs_8_), channel_id=1, source_target_pairs={{0,4},{1,5},{2,6},{3,7},{4,8},{5,9},{6,10},{7,11},{8,12},{9,13},{1... | collective-permute-start | bytes 2359304 | tf_op jit(solution)/shard_map/ppermute | solution.py:31
  52.2 8.5 %collective-permute-start.12 = (bf16[48,4096]{1,0:T(8,128)(2,1)S(1)}, bf16[48,4096]{1,0:T(8,128)(2,1)S(1)}, u32[]{:S(2)}, u32[]{:S(2)}) collective-permute-start(bf16[48,4096]{1,0:T(8,128)(2,1)S(1)} %collective-permute-done.3.refs_0_), channel_id=1, source_target_pairs={{0,2},{1,3},{2,0},{3,1},{4,6},{5,7},{6,4},{7,5},{8,10},{9,11},{10,... | collective-permute-start | bytes 1179656 | tf_op jit(solution)/shard_map/ppermute | solution.py:31
  60.7 10.4 %collective-permute-start.16 = (bf16[2,48,4096]{2,1,0:T(8,128)(2,1)S(1)}, bf16[2,48,4096]{2,1,0:T(8,128)(2,1)S(1)}, u32[]{:S(2)}, u32[]{:S(2)}) collective-permute-start(bf16[2,48,4096]{2,1,0:T(8,128)(2,1)S(1)} %collective-permute-done.5.refs_12_), channel_id=1, source_target_pairs={{0,1},{1,0},{2,3},{3,2},{4,5},{5,4},{6,7},{7,6},{8,9},{9,8},{10,11... | collective-permute-start | bytes 2359304 | tf_op jit(solution)/shard_map/ppermute | solution.py:31
  60.7 10.4 %collective-permute-start.14 = (bf16[2,48,4096]{2,1,0:T(8,128)(2,1)S(1)}, bf16[2,48,4096]{2,1,0:T(8,128)(2,1)S(1)}, u32[]{:S(2)}, u32[]{:S(2)}) collective-permute-start(bf16[2,48,4096]{2,1,0:T(8,128)(2,1)S(1)} %collective-permute-done.4.refs_6_), channel_id=1, source_target_pairs={{0,1},{1,0},{2,3},{3,2},{4,5},{5,4},{6,7},{7,6},{8,9},{9,8},{10,11... | collective-permute-start | bytes 2359304 | tf_op jit(solution)/shard_map/ppermute | solution.py:31
  67.7 3.5 %collective-permute-start.17 = (bf16[2,48,4096]{2,1,0:T(8,128)(2,1)S(1)}, bf16[2,48,4096]{2,1,0:T(8,128)(2,1)S(1)}, u32[]{:S(2)}, u32[]{:S(2)}) collective-permute-start(bf16[2,48,4096]{2,1,0:T(8,128)(2,1)S(1)} %collective-permute-done.11.refs_14_), channel_id=1, source_target_pairs={{0,1},{1,0},{2,3},{3,2},{4,5},{5,4},{6,7},{7,6},{8,9},{9,8},{10,11... | collective-permute-start | bytes 2359304 | tf_op jit(solution)/shard_map/ppermute | solution.py:31
  67.7 3.5 %collective-permute-start.15 = (bf16[2,48,4096]{2,1,0:T(8,128)(2,1)S(1)}, bf16[2,48,4096]{2,1,0:T(8,128)(2,1)S(1)}, u32[]{:S(2)}, u32[]{:S(2)}) collective-permute-start(bf16[2,48,4096]{2,1,0:T(8,128)(2,1)S(1)} %collective-permute-done.10.refs_10_), channel_id=1, source_target_pairs={{0,1},{1,0},{2,3},{3,2},{4,5},{5,4},{6,7},{7,6},{8,9},{9,8},{10,11... | collective-permute-start | bytes 2359304 | tf_op jit(solution)/shard_map/ppermute | solution.py:31
  68.2 19.1 %collective-permute-start.13 = (bf16[48,4096]{1,0:T(8,128)(2,1)S(1)}, bf16[48,4096]{1,0:T(8,128)(2,1)S(1)}, u32[]{:S(2)}, u32[]{:S(2)}) collective-permute-start(bf16[48,4096]{1,0:T(8,128)(2,1)S(1)} %collective-permute-done.3.refs_0_), channel_id=1, source_target_pairs={{0,4},{1,5},{2,6},{3,7},{4,8},{5,9},{6,10},{7,11},{8,12},{9,13},{1... | collective-permute-start | bytes 1179656 | tf_op jit(solution)/shard_map/ppermute | solution.py:31
  71.2 1.1 copy-start
  78.2 13.3 %collective-permute-start.20 = (bf16[48,4096]{1,0:T(8,128)(2,1)S(1)}, bf16[48,4096]{1,0:T(8,128)(2,1)S(1)}, u32[]{:S(2)}, u32[]{:S(2)}) collective-permute-start(bf16[48,4096]{1,0:T(8,128)(2,1)S(1)} %collective-permute-done.12.refs_6_), channel_id=1, source_target_pairs={{0,12},{1,13},{2,14},{3,15},{4,0},{5,1},{6,2},{7,3},{8,4},{9,5},{1... | collective-permute-start | bytes 1179656 | tf_op jit(solution)/shard_map/ppermute | solution.py:31
  78.3 23.7 %collective-permute-start.22 = (bf16[768,256]{1,0:T(8,128)(2,1)S(1)}, bf16[768,256]{1,0:T(8,128)(2,1)S(1)}, u32[]{:S(2)}, u32[]{:S(2)}) collective-permute-start(bf16[768,256]{1,0:T(8,128)(2,1)S(1)} %get-tuple-element.43), channel_id=1, source_target_pairs={{0,240},{16,224},{32,208},{48,192},{64,176},{80,160},{96,144},{112... | collective-permute-start | bytes 1179656 | tf_op jit(solution)/shard_map/ppermute | solution.py:52
  78.4 27.0 %collective-permute-start.25 = (bf16[48,4096]{1,0:T(8,128)(2,1)S(1)}, bf16[48,4096]{1,0:T(8,128)(2,1)S(1)}, u32[]{:S(2)}, u32[]{:S(2)}) collective-permute-start(bf16[48,4096]{1,0:T(8,128)(2,1)S(1)} %collective-permute-done.3.refs_0_), channel_id=1, source_target_pairs={{0,12},{1,13},{2,14},{3,15},{4,0},{5,1},{6,2},{7,3},{8,4},{9,5},{1... | collective-permute-start | bytes 1179656 | tf_op jit(solution)/shard_map/ppermute | solution.py:31
  79.6 25.8 %collective-permute-start.31 = (bf16[768,256]{1,0:T(8,128)(2,1)S(1)}, bf16[768,256]{1,0:T(8,128)(2,1)S(1)}, u32[]{:S(2)}, u32[]{:S(2)}) collective-permute-start(bf16[768,256]{1,0:T(8,128)(2,1)S(1)} %get-tuple-element.38), channel_id=1, source_target_pairs={{16,0},{32,16},{48,32},{64,48},{80,64},{96,80},{112,96},{128,112},... | collective-permute-start | bytes 1179656 | tf_op jit(solution)/shard_map/ppermute | solution.py:58
  87.3 31.2 %collective-permute-start.28 = (bf16[48,4096]{1,0:T(8,128)(2,1)S(1)}, bf16[48,4096]{1,0:T(8,128)(2,1)S(1)}, u32[]{:S(2)}, u32[]{:S(2)}) collective-permute-start(bf16[48,4096]{1,0:T(8,128)(2,1)S(1)} %collective-permute-done.12.refs_6_), channel_id=1, source_target_pairs={{0,4},{1,5},{2,6},{3,7},{4,8},{5,9},{6,10},{7,11},{8,12},{9,13},{1... | collective-permute-start | bytes 1179656 | tf_op jit(solution)/shard_map/ppermute | solution.py:31
  91.4 27.0 %collective-permute-start.32 = (bf16[768,256]{1,0:T(8,128)(2,1)S(1)}, bf16[768,256]{1,0:T(8,128)(2,1)S(1)}, u32[]{:S(2)}, u32[]{:S(2)}) collective-permute-start(bf16[768,256]{1,0:T(8,128)(2,1)S(1)} %get-tuple-element.41), channel_id=1, source_target_pairs={{0,16},{16,32},{32,48},{48,64},{64,80},{80,96},{96,112},{112,128},... | collective-permute-start | bytes 1179656 | tf_op jit(solution)/shard_map/ppermute | solution.py:58
  102.0 17.0 %collective-permute-start.18 = (bf16[48,4096]{1,0:T(8,128)(2,1)S(1)}, bf16[48,4096]{1,0:T(8,128)(2,1)S(1)}, u32[]{:S(2)}, u32[]{:S(2)}) collective-permute-start(bf16[48,4096]{1,0:T(8,128)(2,1)S(1)} %collective-permute-done.13.refs_2_), channel_id=1, source_target_pairs={{0,4},{1,5},{2,6},{3,7},{4,8},{5,9},{6,10},{7,11},{8,12},{9,13},{1... | collective-permute-start | bytes 1179656 | tf_op jit(solution)/shard_map/ppermute | solution.py:31
  105.3 13.7 %collective-permute-start.27 = (bf16[48,4096]{1,0:T(8,128)(2,1)S(1)}, bf16[48,4096]{1,0:T(8,128)(2,1)S(1)}, u32[]{:S(2)}, u32[]{:S(2)}) collective-permute-start(bf16[48,4096]{1,0:T(8,128)(2,1)S(1)} %collective-permute-done.12.refs_6_), channel_id=1, source_target_pairs={{0,1},{1,0},{2,3},{3,2},{4,5},{5,4},{6,7},{7,6},{8,9},{9,8},{10,11... | collective-permute-start | bytes 1179656 | tf_op jit(solution)/shard_map/ppermute | solution.py:31
  105.3 14.1 %collective-permute-start.26 = (bf16[48,4096]{1,0:T(8,128)(2,1)S(1)}, bf16[48,4096]{1,0:T(8,128)(2,1)S(1)}, u32[]{:S(2)}, u32[]{:S(2)}) collective-permute-start(bf16[48,4096]{1,0:T(8,128)(2,1)S(1)} %collective-permute-done.25.refs_4_), channel_id=1, source_target_pairs={{0,1},{1,0},{2,3},{3,2},{4,5},{5,4},{6,7},{7,6},{8,9},{9,8},{10,11... | collective-permute-start | bytes 1179656 | tf_op jit(solution)/shard_map/ppermute | solution.py:31
  118.4 2.2 %collective-permute-start.24 = (bf16[48,4096]{1,0:T(8,128)(2,1)S(1)}, bf16[48,4096]{1,0:T(8,128)(2,1)S(1)}, u32[]{:S(2)}, u32[]{:S(2)}) collective-permute-start(bf16[48,4096]{1,0:T(8,128)(2,1)S(1)} %collective-permute-done.13.refs_2_), channel_id=1, source_target_pairs={{0,1},{1,0},{2,3},{3,2},{4,5},{5,4},{6,7},{7,6},{8,9},{9,8},{10,11... | collective-permute-start | bytes 1179656 | tf_op jit(solution)/shard_map/ppermute | solution.py:31
  118.5 2.3 %collective-permute-start.23 = (bf16[48,4096]{1,0:T(8,128)(2,1)S(1)}, bf16[48,4096]{1,0:T(8,128)(2,1)S(1)}, u32[]{:S(2)}, u32[]{:S(2)}) collective-permute-start(bf16[48,4096]{1,0:T(8,128)(2,1)S(1)} %collective-permute-done.3.refs_0_), channel_id=1, source_target_pairs={{0,1},{1,0},{2,3},{3,2},{4,5},{5,4},{6,7},{7,6},{8,9},{9,8},{10,11... | collective-permute-start | bytes 1179656 | tf_op jit(solution)/shard_map/ppermute | solution.py:31
  119.0 2.3 %collective-permute-start.29 = (bf16[48,4096]{1,0:T(8,128)(2,1)S(1)}, bf16[48,4096]{1,0:T(8,128)(2,1)S(1)}, u32[]{:S(2)}, u32[]{:S(2)}) collective-permute-start(bf16[48,4096]{1,0:T(8,128)(2,1)S(1)} %collective-permute-done.28.refs_8_), channel_id=1, source_target_pairs={{0,1},{1,0},{2,3},{3,2},{4,5},{5,4},{6,7},{7,6},{8,9},{9,8},{10,11... | collective-permute-start | bytes 1179656 | tf_op jit(solution)/shard_map/ppermute | solution.py:31
  119.0 2.8 %collective-permute-start.30 = (bf16[48,4096]{1,0:T(8,128)(2,1)S(1)}, bf16[48,4096]{1,0:T(8,128)(2,1)S(1)}, u32[]{:S(2)}, u32[]{:S(2)}) collective-permute-start(bf16[48,4096]{1,0:T(8,128)(2,1)S(1)} %collective-permute-done.20.refs_10_), channel_id=1, source_target_pairs={{0,1},{1,0},{2,3},{3,2},{4,5},{5,4},{6,7},{7,6},{8,9},{9,8},{10,11... | collective-permute-start | bytes 1179656 | tf_op jit(solution)/shard_map/ppermute | solution.py:31
  119.5 12.3 %collective-permute-start.21 = (bf16[48,4096]{1,0:T(8,128)(2,1)S(1)}, bf16[48,4096]{1,0:T(8,128)(2,1)S(1)}, u32[]{:S(2)}, u32[]{:S(2)}) collective-permute-start(bf16[48,4096]{1,0:T(8,128)(2,1)S(1)} %collective-permute-done.20.refs_10_), channel_id=1, source_target_pairs={{0,12},{1,13},{2,14},{3,15},{4,0},{5,1},{6,2},{7,3},{8,4},{9,5},{1... | collective-permute-start | bytes 1179656 | tf_op jit(solution)/shard_map/ppermute | solution.py:31
  120.6 12.2 %collective-permute-start.19 = (bf16[48,4096]{1,0:T(8,128)(2,1)S(1)}, bf16[48,4096]{1,0:T(8,128)(2,1)S(1)}, u32[]{:S(2)}, u32[]{:S(2)}) collective-permute-start(bf16[48,4096]{1,0:T(8,128)(2,1)S(1)} %collective-permute-done.18.refs_0_), channel_id=1, source_target_pairs={{0,1},{1,0},{2,3},{3,2},{4,5},{5,4},{6,7},{7,6},{8,9},{9,8},{10,11... | collective-permute-start | bytes 1179656 | tf_op jit(solution)/shard_map/ppermute | solution.py:31
  131.8 1.7 %collective-permute-start.33 = (bf16[48,4096]{1,0:T(8,128)(2,1)S(1)}, bf16[48,4096]{1,0:T(8,128)(2,1)S(1)}, u32[]{:S(2)}, u32[]{:S(2)}) collective-permute-start(bf16[48,4096]{1,0:T(8,128)(2,1)S(1)} %collective-permute-done.21.refs_2_), channel_id=1, source_target_pairs={{0,1},{1,0},{2,3},{3,2},{4,5},{5,4},{6,7},{7,6},{8,9},{9,8},{10,11... | collective-permute-start | bytes 1179656 | tf_op jit(solution)/shard_map/ppermute | solution.py:31

commit v5 on v4

--- a/solution.py
+++ b/solution.py
@@ -110,7 +110,7 @@
         total, *rest = rest
     whole, upright, flat, bsems, csems = rest
     rows = whole.shape[0] // n
-    copies = []
+    copies, turned = [], []
     for i, block in enumerate(blocks):
         source = block.at[0] if len(block.shape) == 3 else block
         copies.append(
@@ -119,12 +119,17 @@
     for i, key in enumerate(keys + late_keys):
         source = context.at[pl.ds(first_row(key, rows), rows), :]
         target = upright.at[pl.ds(i * rows, rows), :]
-        copies.append(pltpu.make_async_copy(source, target, csems.at[i]))
-    run(copies)
+        turned.append(pltpu.make_async_copy(source, target, csems.at[i]))
+    for copy in turned + copies:
+        copy.start()
+    for copy in turned:
+        copy.wait()
     count = n * rows
     flat[...] = upright[pl.ds(0, count), :].T
     if late_keys:
         late[...] = upright[pl.ds(count, len(late_keys) * rows), :].T
+    for copy in copies:
+        copy.wait()
     wide = 512
 
     @pl.loop(0, total.shape[1] // wide)

time: 139 us -> 139 us (level)
  transfers between devices with their start and end apart: 34 -> 34, of which waited for: 16 -> 16; matrix products, arithmetic and copies ran while one was open for 2% -> 2% of each run, Pallas kernels for 14% -> 15%
where the time goes in v5:
time: 139 us; the launch traced here: 136 us
  waiting for transfers between devices  68.7 us (49%)
  starting transfers between devices  39.8 us (29%)
  Pallas kernels  22.9 us (16%)
  local copies, waits for them, and re-layouts  3.35 us (2%)
    ppermute x30, waiting for transfers between devices, moved(): return lax.ppermute(value, 'tensor', pairs)  43.4 us
    ppermute x30, starting transfers between devices, moved(): return lax.ppermute(value, 'tensor', pairs)  22.5 us
    pallas_call x2, Pallas kernels, summed(): pl.pallas_call(functools.partial(sum_kernel, keys, late, total is not Non...  14.2 us
    ppermute x2, waiting for transfers between devices, mirrored(): lax.ppermute(value, 'pipe', [(i, count - 1 - i) for i in range(count)])  12.7 us
    ppermute x2, waiting for transfers between devices, from_behind(): return lax.ppermute(value, 'pipe', pairs)  12.6 us
    ppermute x2, starting transfers between devices, from_behind(): return lax.ppermute(value, 'pipe', pairs)  10.3 us
    ppermute x2, starting transfers between devices, mirrored(): lax.ppermute(value, 'pipe', [(i, count - 1 - i) for i in range(count)])  6.97 us
    pallas_call x1, Pallas kernels, shards(): pl.pallas_call(back_kernel, out_shape=(back_shape,) * 2, in_specs=[HBM] +...  5.85 us
  transfers between devices with their start and end apart: 34, of which 16 were waited for; matrix products, arithmetic and copies ran while one was open for 2% of the time, Pallas kernels for 15%

profile of v5, /device:TPU:58, one launch (start us, length us, event | category | flops | bytes accessed | tf_op | source)
XLA Modules:
  0.0 136.3 jit_solution(3507777506554434169)
XLA Ops:
  0.6 0.2 collective-permute-start.2
  0.8 0.2 collective-permute-start
  1.0 1.8 %collective-permute-start.1 = (bf16[2,48,4096]{2,1,0:T(8,128)(2,1)}, bf16[2,48,4096]{2,1,0:T(8,128)(2,1)S(1)}, u32[]{:S(2)}, u32[]{:S(2)}) collective-permute-start(bf16[2,48,4096]{2,1,0:T(8,128)(2,1)} %bitcast.15), channel_id=1, source_target_pairs={{0,12},{1,13},{2,14},{3,15},{4,0},{5,1},{6,2},{7,3},{8,4},{9,5},{1... | collective-permute-start | bytes 2359304 | tf_op jit(solution)/shard_map/ppermute | solution.py:31
  2.9 0.0 collective-permute-start.6
  2.9 1.1 slice_bitcast_fusion.2
  3.9 16.3 %collective-permute-done.2.refs_8_ = bf16[2,48,4096]{2,1,0:T(8,128)(2,1)S(1)} collective-permute-done((bf16[2,48,4096]{2,1,0:T(8,128)(2,1)}, bf16[2,48,4096]{2,1,0:T(8,128)(2,1)S(1)}, u32[]{:S(2)}, u32[]{:S(2)}) %collective-permute-start.2) | collective-permute-done | bytes 786464 | tf_op jit(solution)/shard_map/ppermute | solution.py:31
  20.2 0.1 collective-permute-done.refs_2_
  20.3 1.3 collective-permute-done.1.refs_4_
  21.6 6.9 %collective-permute-start.3 = (bf16[48,4096]{1,0:T(8,128)(2,1)S(1)}, bf16[48,4096]{1,0:T(8,128)(2,1)S(1)}, u32[]{:S(2)}, u32[]{:S(2)}) collective-permute-start(bf16[48,4096]{1,0:T(8,128)(2,1)S(1)} %slice_bitcast_fusion.2), channel_id=1, source_target_pairs={{0,240},{16,224},{32,208},{48,192},{64,176},{80,160},{96,144},{112... | collective-permute-start | bytes 1179656 | tf_op jit(solution)/shard_map/ppermute | solution.py:52
  28.5 1.2 slice_bitcast_fusion
  29.6 0.4 collective-permute-start.4
  30.0 1.7 %collective-permute-start.5 = (bf16[2,48,4096]{2,1,0:T(8,128)(2,1)S(1)}, bf16[2,48,4096]{2,1,0:T(8,128)(2,1)S(1)}, u32[]{:S(2)}, u32[]{:S(2)}) collective-permute-start(bf16[2,48,4096]{2,1,0:T(8,128)(2,1)S(1)} %collective-permute-done.2.refs_8_), channel_id=1, source_target_pairs={{0,12},{1,13},{2,14},{3,15},{4,0},{5,1},{6,2},{7,3},{8,4},{9,5},{1... | collective-permute-start | bytes 2359304 | tf_op jit(solution)/shard_map/ppermute | solution.py:31
  31.8 0.0 collective-permute-start.9
  31.8 0.0 collective-permute-done.6.refs_1_
  31.8 0.5 collective-permute-start.7
  32.3 12.3 %collective-permute-done.3.refs_0_ = bf16[48,4096]{1,0:T(8,128)(2,1)S(1)} collective-permute-done((bf16[48,4096]{1,0:T(8,128)(2,1)S(1)}, bf16[48,4096]{1,0:T(8,128)(2,1)S(1)}, u32[]{:S(2)}, u32[]{:S(2)}) %collective-permute-start.3) | collective-permute-done | bytes 393248 | tf_op jit(solution)/shard_map/ppermute | solution.py:52
  44.6 0.0 collective-permute-start.8
  44.6 2.7 %collective-permute-done.4.refs_6_ = bf16[2,48,4096]{2,1,0:T(8,128)(2,1)S(1)} collective-permute-done((bf16[2,48,4096]{2,1,0:T(8,128)(2,1)S(1)}, bf16[2,48,4096]{2,1,0:T(8,128)(2,1)S(1)}, u32[]{:S(2)}, u32[]{:S(2)}) %collective-permute-start.4) | collective-permute-done | bytes 786464 | tf_op jit(solution)/shard_map/ppermute | solution.py:31
  47.3 1.6 %collective-permute-done.5.refs_12_ = bf16[2,48,4096]{2,1,0:T(8,128)(2,1)S(1)} collective-permute-done((bf16[2,48,4096]{2,1,0:T(8,128)(2,1)S(1)}, bf16[2,48,4096]{2,1,0:T(8,128)(2,1)S(1)}, u32[]{:S(2)}, u32[]{:S(2)}) %collective-permute-start.5) | collective-permute-done | bytes 786464 | tf_op jit(solution)/shard_map/ppermute | solution.py:31
  48.9 0.2 collective-permute-start.11
  49.1 3.1 %collective-permute-start.10 = (bf16[2,48,4096]{2,1,0:T(8,128)(2,1)S(1)}, bf16[2,48,4096]{2,1,0:T(8,128)(2,1)S(1)}, u32[]{:S(2)}, u32[]{:S(2)}) collective-permute-start(bf16[2,48,4096]{2,1,0:T(8,128)(2,1)S(1)} %collective-permute-done.2.refs_8_), channel_id=1, source_target_pairs={{0,4},{1,5},{2,6},{3,7},{4,8},{5,9},{6,10},{7,11},{8,12},{9,13},{1... | collective-permute-start | bytes 2359304 | tf_op jit(solution)/shard_map/ppermute | solution.py:31
  52.2 1.0 collective-permute-start.12
  53.2 7.5 %collective-permute-done.12.refs_6_ = bf16[48,4096]{1,0:T(8,128)(2,1)S(1)} collective-permute-done((bf16[48,4096]{1,0:T(8,128)(2,1)S(1)}, bf16[48,4096]{1,0:T(8,128)(2,1)S(1)}, u32[]{:S(2)}, u32[]{:S(2)}) %collective-permute-start.12) | collective-permute-done | bytes 393248 | tf_op jit(solution)/shard_map/ppermute | solution.py:31
  60.7 0.5 collective-permute-start.14
  61.2 6.4 %collective-permute-done.11.refs_14_ = bf16[2,48,4096]{2,1,0:T(8,128)(2,1)S(1)} collective-permute-done((bf16[2,48,4096]{2,1,0:T(8,128)(2,1)S(1)}, bf16[2,48,4096]{2,1,0:T(8,128)(2,1)S(1)}, u32[]{:S(2)}, u32[]{:S(2)}) %collective-permute-start.11) | collective-permute-done | bytes 786464 | tf_op jit(solution)/shard_map/ppermute | solution.py:31
  67.7 0.0 collective-permute-start.17
  67.7 0.5 collective-permute-start.15
  68.2 3.0 %collective-permute-start.13 = (bf16[48,4096]{1,0:T(8,128)(2,1)S(1)}, bf16[48,4096]{1,0:T(8,128)(2,1)S(1)}, u32[]{:S(2)}, u32[]{:S(2)}) collective-permute-start(bf16[48,4096]{1,0:T(8,128)(2,1)S(1)} %collective-permute-done.3.refs_0_), channel_id=1, source_target_pairs={{0,4},{1,5},{2,6},{3,7},{4,8},{5,9},{6,10},{7,11},{8,12},{9,13},{1... | collective-permute-start | bytes 1179656 | tf_op jit(solution)/shard_map/ppermute | solution.py:31
  71.1 0.0 collective-permute-done.16.refs_13_
  71.2 0.0 collective-permute-done.15.refs_11_
  71.2 0.0 copy-start
  71.2 1.1 copy-done
  72.3 5.9 %shard_map.50 = (bf16[768,256]{1,0:T(8,128)(2,1)S(1)}, bf16[768,256]{1,0:T(8,128)(2,1)S(1)}) custom-call(bf16[2,48,4096]{2,1,0:T(8,128)(2,1)S(1)} %bitcast.17, bf16[2,48,4096]{2,1,0:T(8,128)(2,1)S(1)} %collective-permute-done.6.refs_1_, bf16[2,48,4096]{2,1,0:T(8,128)(2,1)S(1)} %collective-permute-done.refs_2_, ...), custom_call_target="tpu_custom_call" | custom-call | flops 3221225472 | bytes 16777216 | tf_op jit(solution)/shard_map/pallas_call | solution.py:199
  78.2 0.1 collective-permute-start.20
  78.3 0.1 collective-permute-start.22
  78.4 1.2 collective-permute-start.25
  79.6 7.7 %collective-permute-start.31 = (bf16[768,256]{1,0:T(8,128)(2,1)S(1)}, bf16[768,256]{1,0:T(8,128)(2,1)S(1)}, u32[]{:S(2)}, u32[]{:S(2)}) collective-permute-start(bf16[768,256]{1,0:T(8,128)(2,1)S(1)} %get-tuple-element.38), channel_id=1, source_target_pairs={{16,0},{32,16},{48,32},{64,48},{80,64},{96,80},{112,96},{128,112},... | collective-permute-start | bytes 1179656 | tf_op jit(solution)/shard_map/ppermute | solution.py:58
  87.3 2.1 %collective-permute-start.28 = (bf16[48,4096]{1,0:T(8,128)(2,1)S(1)}, bf16[48,4096]{1,0:T(8,128)(2,1)S(1)}, u32[]{:S(2)}, u32[]{:S(2)}) collective-permute-start(bf16[48,4096]{1,0:T(8,128)(2,1)S(1)} %collective-permute-done.12.refs_6_), channel_id=1, source_target_pairs={{0,4},{1,5},{2,6},{3,7},{4,8},{5,9},{6,10},{7,11},{8,12},{9,13},{1... | collective-permute-start | bytes 1179656 | tf_op jit(solution)/shard_map/ppermute | solution.py:31
  89.3 2.1 %collective-permute-done.20.refs_10_ = bf16[48,4096]{1,0:T(8,128)(2,1)S(1)} collective-permute-done((bf16[48,4096]{1,0:T(8,128)(2,1)S(1)}, bf16[48,4096]{1,0:T(8,128)(2,1)S(1)}, u32[]{:S(2)}, u32[]{:S(2)}) %collective-permute-start.20) | collective-permute-done | bytes 393248 | tf_op jit(solution)/shard_map/ppermute | solution.py:31
  91.4 2.6 %collective-permute-start.32 = (bf16[768,256]{1,0:T(8,128)(2,1)S(1)}, bf16[768,256]{1,0:T(8,128)(2,1)S(1)}, u32[]{:S(2)}, u32[]{:S(2)}) collective-permute-start(bf16[768,256]{1,0:T(8,128)(2,1)S(1)} %get-tuple-element.41), channel_id=1, source_target_pairs={{0,16},{16,32},{32,48},{48,64},{64,80},{80,96},{96,112},{112,128},... | collective-permute-start | bytes 1179656 | tf_op jit(solution)/shard_map/ppermute | solution.py:58
  94.0 7.6 %shard_map.51.refs_13_ = f32[256,4096]{1,0:T(8,128)S(1)} custom-call(bf16[2,48,4096]{2,1,0:T(8,128)(2,1)S(1)} %bitcast.18, bf16[2,48,4096]{2,1,0:T(8,128)(2,1)S(1)} %collective-permute-done.6.refs_1_, bf16[2,48,4096]{2,1,0:T(8,128)(2,1)S(1)} %collective-permute-done.refs_2_, bf16[2,48,4096]{2,1,0:T(8,128)(2,1)S(1)} %collective-permute-done.7.refs_3_, ...), custom_call_target="tpu_custom_call" | custom-call | flops 1610612736 | bytes 12582912 | tf_op jit(solution)/shard_map/pallas_call | solution.py:230
  101.6 0.3 collective-permute-done.22.refs_12_
  102.0 3.4 %collective-permute-start.18 = (bf16[48,4096]{1,0:T(8,128)(2,1)S(1)}, bf16[48,4096]{1,0:T(8,128)(2,1)S(1)}, u32[]{:S(2)}, u32[]{:S(2)}) collective-permute-start(bf16[48,4096]{1,0:T(8,128)(2,1)S(1)} %collective-permute-done.13.refs_2_), channel_id=1, source_target_pairs={{0,4},{1,5},{2,6},{3,7},{4,8},{5,9},{6,10},{7,11},{8,12},{9,13},{1... | collective-permute-start | bytes 1179656 | tf_op jit(solution)/shard_map/ppermute | solution.py:31
  105.3 0.0 collective-permute-done.25.refs_4_
  105.3 0.0 collective-permute-start.27
  105.3 0.5 collective-permute-start.26
  105.8 12.6 %collective-permute-done.32 = bf16[768,256]{1,0:T(8,128)(2,1)S(1)} collective-permute-done((bf16[768,256]{1,0:T(8,128)(2,1)S(1)}, bf16[768,256]{1,0:T(8,128)(2,1)S(1)}, u32[]{:S(2)}, u32[]{:S(2)}) %collective-permute-start.32) | collective-permute-done | bytes 393248 | tf_op jit(solution)/shard_map/ppermute | solution.py:58
  118.4 0.0 collective-permute-start.24
  118.5 0.5 collective-permute-start.23
  119.0 0.1 collective-permute-start.29
  119.0 0.0 collective-permute-done.27.refs_7_
  119.0 0.4 collective-permute-start.30
  119.5 1.1 collective-permute-start.21
  120.6 0.0 collective-permute-done.24.refs_3_
  120.6 0.0 collective-permute-start.19
  120.6 0.1 collective-permute-done.23.refs_1_
  120.7 0.6 collective-permute-done.29.refs_9_
  121.3 0.6 collective-permute-done.30.refs_11_
  121.8 6.6 %shard_map.52 = (f32[256,4096]{1,0:T(8,128)S(1)}, bf16[256,192]{1,0:T(8,128)(2,1)S(1)}) custom-call(bf16[48,4096]{1,0:T(8,128)(2,1)S(1)} %collective-permute-done.3.refs_0_, bf16[48,4096]{1,0:T(8,128)(2,1)S(1)} %collective-permute-done.23.refs_1_, bf16[48,4096]{1,0:T(8,128)(2,1)S(1)} %collective-permute-done.13.refs_2_, ...), custom_call_target="tpu_custom_call" | custom-call | flops 1207959552 | bytes 11010048 | tf_op jit(solution)/shard_map/pallas_call | solution.py:230
  128.5 3.3 %collective-permute-done.21.refs_2_ = bf16[48,4096]{1,0:T(8,128)(2,1)S(1)} collective-permute-done((bf16[48,4096]{1,0:T(8,128)(2,1)S(1)}, bf16[48,4096]{1,0:T(8,128)(2,1)S(1)}, u32[]{:S(2)}, u32[]{:S(2)}) %collective-permute-start.21) | collective-permute-done | bytes 393248 | tf_op jit(solution)/shard_map/ppermute | solution.py:31
  131.8 0.0 collective-permute-start.33
  131.8 0.9 maximum_bitcast_fusion
  132.7 0.8 collective-permute-done.33.refs_3_
  133.5 2.8 %shard_map.53 = bf16[256,4096]{1,0:T(8,128)(2,1)} custom-call(bf16[48,4096]{1,0:T(8,128)(2,1)S(1)} %collective-permute-done.18.refs_0_, bf16[48,4096]{1,0:T(8,128)(2,1)S(1)} %collective-permute-done.19.refs_1_, bf16[48,4096]{1,0:T(8,128)(2,1)S(1)} %collective-permute-done.21.refs_2_, bf16[48,4096]{1,0:T(8,128)(2,1)S(1)} %collective-permute-done.33.refs_3_, ...), custom_call_target="tpu_custom_call" | custom-call | flops 402653184 | bytes 7864320 | tf_op jit(solution)/shard_map/pallas_call | solution.py:263
  (13 shorter events, 0.0 us)
Async XLA Ops:
  0.6 19.6 %collective-permute-start.2 = (bf16[2,48,4096]{2,1,0:T(8,128)(2,1)}, bf16[2,48,4096]{2,1,0:T(8,128)(2,1)S(1)}, u32[]{:S(2)}, u32[]{:S(2)}) collective-permute-start(bf16[2,48,4096]{2,1,0:T(8,128)(2,1)} %bitcast.13), channel_id=1, source_target_pairs={{0,2},{1,3},{2,0},{3,1},{4,6},{5,7},{6,4},{7,5},{8,10},{9,11},{10,... | collective-permute-start | bytes 2359304 | tf_op jit(solution)/shard_map/ppermute | solution.py:31
  0.8 19.5 %collective-permute-start = (bf16[2,48,4096]{2,1,0:T(8,128)(2,1)}, bf16[2,48,4096]{2,1,0:T(8,128)(2,1)S(1)}, u32[]{:S(2)}, u32[]{:S(2)}) collective-permute-start(bf16[2,48,4096]{2,1,0:T(8,128)(2,1)} %bitcast.14), channel_id=1, source_target_pairs={{0,4},{1,5},{2,6},{3,7},{4,8},{5,9},{6,10},{7,11},{8,12},{9,13},{1... | collective-permute-start | bytes 2359304 | tf_op jit(solution)/shard_map/ppermute | solution.py:31
  1.0 20.6 %collective-permute-start.1 = (bf16[2,48,4096]{2,1,0:T(8,128)(2,1)}, bf16[2,48,4096]{2,1,0:T(8,128)(2,1)S(1)}, u32[]{:S(2)}, u32[]{:S(2)}) collective-permute-start(bf16[2,48,4096]{2,1,0:T(8,128)(2,1)} %bitcast.15), channel_id=1, source_target_pairs={{0,12},{1,13},{2,14},{3,15},{4,0},{5,1},{6,2},{7,3},{8,4},{9,5},{1... | collective-permute-start | bytes 2359304 | tf_op jit(solution)/shard_map/ppermute | solution.py:31
  2.9 28.9 %collective-permute-start.6 = (bf16[2,48,4096]{2,1,0:T(8,128)(2,1)}, bf16[2,48,4096]{2,1,0:T(8,128)(2,1)S(1)}, u32[]{:S(2)}, u32[]{:S(2)}) collective-permute-start(bf16[2,48,4096]{2,1,0:T(8,128)(2,1)} %bitcast.16), channel_id=1, source_target_pairs={{0,1},{1,0},{2,3},{3,2},{4,5},{5,4},{6,7},{7,6},{8,9},{9,8},{10,11... | collective-permute-start | bytes 2359304 | tf_op jit(solution)/shard_map/ppermute | solution.py:31
  21.6 23.0 %collective-permute-start.3 = (bf16[48,4096]{1,0:T(8,128)(2,1)S(1)}, bf16[48,4096]{1,0:T(8,128)(2,1)S(1)}, u32[]{:S(2)}, u32[]{:S(2)}) collective-permute-start(bf16[48,4096]{1,0:T(8,128)(2,1)S(1)} %slice_bitcast_fusion.2), channel_id=1, source_target_pairs={{0,240},{16,224},{32,208},{48,192},{64,176},{80,160},{96,144},{112... | collective-permute-start | bytes 1179656 | tf_op jit(solution)/shard_map/ppermute | solution.py:52
  29.6 17.7 %collective-permute-start.4 = (bf16[2,48,4096]{2,1,0:T(8,128)(2,1)S(1)}, bf16[2,48,4096]{2,1,0:T(8,128)(2,1)S(1)}, u32[]{:S(2)}, u32[]{:S(2)}) collective-permute-start(bf16[2,48,4096]{2,1,0:T(8,128)(2,1)S(1)} %collective-permute-done.refs_2_), channel_id=1, source_target_pairs={{0,4},{1,5},{2,6},{3,7},{4,8},{5,9},{6,10},{7,11},{8,12},{9,13},{1... | collective-permute-start | bytes 2359304 | tf_op jit(solution)/shard_map/ppermute | solution.py:31
  30.0 18.8 %collective-permute-start.5 = (bf16[2,48,4096]{2,1,0:T(8,128)(2,1)S(1)}, bf16[2,48,4096]{2,1,0:T(8,128)(2,1)S(1)}, u32[]{:S(2)}, u32[]{:S(2)}) collective-permute-start(bf16[2,48,4096]{2,1,0:T(8,128)(2,1)S(1)} %collective-permute-done.2.refs_8_), channel_id=1, source_target_pairs={{0,12},{1,13},{2,14},{3,15},{4,0},{5,1},{6,2},{7,3},{8,4},{9,5},{1... | collective-permute-start | bytes 2359304 | tf_op jit(solution)/shard_map/ppermute | solution.py:31
  31.8 17.1 %collective-permute-start.9 = (bf16[2,48,4096]{2,1,0:T(8,128)(2,1)S(1)}, bf16[2,48,4096]{2,1,0:T(8,128)(2,1)S(1)}, u32[]{:S(2)}, u32[]{:S(2)}) collective-permute-start(bf16[2,48,4096]{2,1,0:T(8,128)(2,1)S(1)} %collective-permute-done.2.refs_8_), channel_id=1, source_target_pairs={{0,1},{1,0},{2,3},{3,2},{4,5},{5,4},{6,7},{7,6},{8,9},{9,8},{10,11... | collective-permute-start | bytes 2359304 | tf_op jit(solution)/shard_map/ppermute | solution.py:31
  31.8 17.1 %collective-permute-start.7 = (bf16[2,48,4096]{2,1,0:T(8,128)(2,1)S(1)}, bf16[2,48,4096]{2,1,0:T(8,128)(2,1)S(1)}, u32[]{:S(2)}, u32[]{:S(2)}) collective-permute-start(bf16[2,48,4096]{2,1,0:T(8,128)(2,1)S(1)} %collective-permute-done.refs_2_), channel_id=1, source_target_pairs={{0,1},{1,0},{2,3},{3,2},{4,5},{5,4},{6,7},{7,6},{8,9},{9,8},{10,11... | collective-permute-start | bytes 2359304 | tf_op jit(solution)/shard_map/ppermute | solution.py:31
  44.6 4.3 %collective-permute-start.8 = (bf16[2,48,4096]{2,1,0:T(8,128)(2,1)S(1)}, bf16[2,48,4096]{2,1,0:T(8,128)(2,1)S(1)}, u32[]{:S(2)}, u32[]{:S(2)}) collective-permute-start(bf16[2,48,4096]{2,1,0:T(8,128)(2,1)S(1)} %collective-permute-done.1.refs_4_), channel_id=1, source_target_pairs={{0,1},{1,0},{2,3},{3,2},{4,5},{5,4},{6,7},{7,6},{8,9},{9,8},{10,11... | collective-permute-start | bytes 2359304 | tf_op jit(solution)/shard_map/ppermute | solution.py:31
  48.9 18.8 %collective-permute-start.11 = (bf16[2,48,4096]{2,1,0:T(8,128)(2,1)S(1)}, bf16[2,48,4096]{2,1,0:T(8,128)(2,1)S(1)}, u32[]{:S(2)}, u32[]{:S(2)}) collective-permute-start(bf16[2,48,4096]{2,1,0:T(8,128)(2,1)S(1)} %collective-permute-done.5.refs_12_), channel_id=1, source_target_pairs={{0,12},{1,13},{2,14},{3,15},{4,0},{5,1},{6,2},{7,3},{8,4},{9,5},{1... | collective-permute-start | bytes 2359304 | tf_op jit(solution)/shard_map/ppermute | solution.py:31
  49.1 18.5 %collective-permute-start.10 = (bf16[2,48,4096]{2,1,0:T(8,128)(2,1)S(1)}, bf16[2,48,4096]{2,1,0:T(8,128)(2,1)S(1)}, u32[]{:S(2)}, u32[]{:S(2)}) collective-permute-start(bf16[2,48,4096]{2,1,0:T(8,128)(2,1)S(1)} %collective-permute-done.2.refs_8_), channel_id=1, source_target_pairs={{0,4},{1,5},{2,6},{3,7},{4,8},{5,9},{6,10},{7,11},{8,12},{9,13},{1... | collective-permute-start | bytes 2359304 | tf_op jit(solution)/shard_map/ppermute | solution.py:31
  52.2 8.5 %collective-permute-start.12 = (bf16[48,4096]{1,0:T(8,128)(2,1)S(1)}, bf16[48,4096]{1,0:T(8,128)(2,1)S(1)}, u32[]{:S(2)}, u32[]{:S(2)}) collective-permute-start(bf16[48,4096]{1,0:T(8,128)(2,1)S(1)} %collective-permute-done.3.refs_0_), channel_id=1, source_target_pairs={{0,2},{1,3},{2,0},{3,1},{4,6},{5,7},{6,4},{7,5},{8,10},{9,11},{10,... | collective-permute-start | bytes 1179656 | tf_op jit(solution)/shard_map/ppermute | solution.py:31
  60.7 10.4 %collective-permute-start.16 = (bf16[2,48,4096]{2,1,0:T(8,128)(2,1)S(1)}, bf16[2,48,4096]{2,1,0:T(8,128)(2,1)S(1)}, u32[]{:S(2)}, u32[]{:S(2)}) collective-permute-start(bf16[2,48,4096]{2,1,0:T(8,128)(2,1)S(1)} %collective-permute-done.5.refs_12_), channel_id=1, source_target_pairs={{0,1},{1,0},{2,3},{3,2},{4,5},{5,4},{6,7},{7,6},{8,9},{9,8},{10,11... | collective-permute-start | bytes 2359304 | tf_op jit(solution)/shard_map/ppermute | solution.py:31
  60.7 10.4 %collective-permute-start.14 = (bf16[2,48,4096]{2,1,0:T(8,128)(2,1)S(1)}, bf16[2,48,4096]{2,1,0:T(8,128)(2,1)S(1)}, u32[]{:S(2)}, u32[]{:S(2)}) collective-permute-start(bf16[2,48,4096]{2,1,0:T(8,128)(2,1)S(1)} %collective-permute-done.4.refs_6_), channel_id=1, source_target_pairs={{0,1},{1,0},{2,3},{3,2},{4,5},{5,4},{6,7},{7,6},{8,9},{9,8},{10,11... | collective-permute-start | bytes 2359304 | tf_op jit(solution)/shard_map/ppermute | solution.py:31
  67.7 3.5 %collective-permute-start.17 = (bf16[2,48,4096]{2,1,0:T(8,128)(2,1)S(1)}, bf16[2,48,4096]{2,1,0:T(8,128)(2,1)S(1)}, u32[]{:S(2)}, u32[]{:S(2)}) collective-permute-start(bf16[2,48,4096]{2,1,0:T(8,128)(2,1)S(1)} %collective-permute-done.11.refs_14_), channel_id=1, source_target_pairs={{0,1},{1,0},{2,3},{3,2},{4,5},{5,4},{6,7},{7,6},{8,9},{9,8},{10,11... | collective-permute-start | bytes 2359304 | tf_op jit(solution)/shard_map/ppermute | solution.py:31
  67.7 3.5 %collective-permute-start.15 = (bf16[2,48,4096]{2,1,0:T(8,128)(2,1)S(1)}, bf16[2,48,4096]{2,1,0:T(8,128)(2,1)S(1)}, u32[]{:S(2)}, u32[]{:S(2)}) collective-permute-start(bf16[2,48,4096]{2,1,0:T(8,128)(2,1)S(1)} %collective-permute-done.10.refs_10_), channel_id=1, source_target_pairs={{0,1},{1,0},{2,3},{3,2},{4,5},{5,4},{6,7},{7,6},{8,9},{9,8},{10,11... | collective-permute-start | bytes 2359304 | tf_op jit(solution)/shard_map/ppermute | solution.py:31
  68.2 19.1 %collective-permute-start.13 = (bf16[48,4096]{1,0:T(8,128)(2,1)S(1)}, bf16[48,4096]{1,0:T(8,128)(2,1)S(1)}, u32[]{:S(2)}, u32[]{:S(2)}) collective-permute-start(bf16[48,4096]{1,0:T(8,128)(2,1)S(1)} %collective-permute-done.3.refs_0_), channel_id=1, source_target_pairs={{0,4},{1,5},{2,6},{3,7},{4,8},{5,9},{6,10},{7,11},{8,12},{9,13},{1... | collective-permute-start | bytes 1179656 | tf_op jit(solution)/shard_map/ppermute | solution.py:31
  71.2 1.1 copy-start
  78.2 13.3 %collective-permute-start.20 = (bf16[48,4096]{1,0:T(8,128)(2,1)S(1)}, bf16[48,4096]{1,0:T(8,128)(2,1)S(1)}, u32[]{:S(2)}, u32[]{:S(2)}) collective-permute-start(bf16[48,4096]{1,0:T(8,128)(2,1)S(1)} %collective-permute-done.12.refs_6_), channel_id=1, source_target_pairs={{0,12},{1,13},{2,14},{3,15},{4,0},{5,1},{6,2},{7,3},{8,4},{9,5},{1... | collective-permute-start | bytes 1179656 | tf_op jit(solution)/shard_map/ppermute | solution.py:31
  78.3 23.7 %collective-permute-start.22 = (bf16[768,256]{1,0:T(8,128)(2,1)S(1)}, bf16[768,256]{1,0:T(8,128)(2,1)S(1)}, u32[]{:S(2)}, u32[]{:S(2)}) collective-permute-start(bf16[768,256]{1,0:T(8,128)(2,1)S(1)} %get-tuple-element.43), channel_id=1, source_target_pairs={{0,240},{16,224},{32,208},{48,192},{64,176},{80,160},{96,144},{112... | collective-permute-start | bytes 1179656 | tf_op jit(solution)/shard_map/ppermute | solution.py:52
  78.4 27.0 %collective-permute-start.25 = (bf16[48,4096]{1,0:T(8,128)(2,1)S(1)}, bf16[48,4096]{1,0:T(8,128)(2,1)S(1)}, u32[]{:S(2)}, u32[]{:S(2)}) collective-permute-start(bf16[48,4096]{1,0:T(8,128)(2,1)S(1)} %collective-permute-done.3.refs_0_), channel_id=1, source_target_pairs={{0,12},{1,13},{2,14},{3,15},{4,0},{5,1},{6,2},{7,3},{8,4},{9,5},{1... | collective-permute-start | bytes 1179656 | tf_op jit(solution)/shard_map/ppermute | solution.py:31
  79.6 25.8 %collective-permute-start.31 = (bf16[768,256]{1,0:T(8,128)(2,1)S(1)}, bf16[768,256]{1,0:T(8,128)(2,1)S(1)}, u32[]{:S(2)}, u32[]{:S(2)}) collective-permute-start(bf16[768,256]{1,0:T(8,128)(2,1)S(1)} %get-tuple-element.38), channel_id=1, source_target_pairs={{16,0},{32,16},{48,32},{64,48},{80,64},{96,80},{112,96},{128,112},... | collective-permute-start | bytes 1179656 | tf_op jit(solution)/shard_map/ppermute | solution.py:58
  87.3 31.2 %collective-permute-start.28 = (bf16[48,4096]{1,0:T(8,128)(2,1)S(1)}, bf16[48,4096]{1,0:T(8,128)(2,1)S(1)}, u32[]{:S(2)}, u32[]{:S(2)}) collective-permute-start(bf16[48,4096]{1,0:T(8,128)(2,1)S(1)} %collective-permute-done.12.refs_6_), channel_id=1, source_target_pairs={{0,4},{1,5},{2,6},{3,7},{4,8},{5,9},{6,10},{7,11},{8,12},{9,13},{1... | collective-permute-start | bytes 1179656 | tf_op jit(solution)/shard_map/ppermute | solution.py:31
  91.4 27.0 %collective-permute-start.32 = (bf16[768,256]{1,0:T(8,128)(2,1)S(1)}, bf16[768,256]{1,0:T(8,128)(2,1)S(1)}, u32[]{:S(2)}, u32[]{:S(2)}) collective-permute-start(bf16[768,256]{1,0:T(8,128)(2,1)S(1)} %get-tuple-element.41), channel_id=1, source_target_pairs={{0,16},{16,32},{32,48},{48,64},{64,80},{80,96},{96,112},{112,128},... | collective-permute-start | bytes 1179656 | tf_op jit(solution)/shard_map/ppermute | solution.py:58
  102.0 17.0 %collective-permute-start.18 = (bf16[48,4096]{1,0:T(8,128)(2,1)S(1)}, bf16[48,4096]{1,0:T(8,128)(2,1)S(1)}, u32[]{:S(2)}, u32[]{:S(2)}) collective-permute-start(bf16[48,4096]{1,0:T(8,128)(2,1)S(1)} %collective-permute-done.13.refs_2_), channel_id=1, source_target_pairs={{0,4},{1,5},{2,6},{3,7},{4,8},{5,9},{6,10},{7,11},{8,12},{9,13},{1... | collective-permute-start | bytes 1179656 | tf_op jit(solution)/shard_map/ppermute | solution.py:31
  105.3 13.7 %collective-permute-start.27 = (bf16[48,4096]{1,0:T(8,128)(2,1)S(1)}, bf16[48,4096]{1,0:T(8,128)(2,1)S(1)}, u32[]{:S(2)}, u32[]{:S(2)}) collective-permute-start(bf16[48,4096]{1,0:T(8,128)(2,1)S(1)} %collective-permute-done.12.refs_6_), channel_id=1, source_target_pairs={{0,1},{1,0},{2,3},{3,2},{4,5},{5,4},{6,7},{7,6},{8,9},{9,8},{10,11... | collective-permute-start | bytes 1179656 | tf_op jit(solution)/shard_map/ppermute | solution.py:31
  105.3 14.1 %collective-permute-start.26 = (bf16[48,4096]{1,0:T(8,128)(2,1)S(1)}, bf16[48,4096]{1,0:T(8,128)(2,1)S(1)}, u32[]{:S(2)}, u32[]{:S(2)}) collective-permute-start(bf16[48,4096]{1,0:T(8,128)(2,1)S(1)} %collective-permute-done.25.refs_4_), channel_id=1, source_target_pairs={{0,1},{1,0},{2,3},{3,2},{4,5},{5,4},{6,7},{7,6},{8,9},{9,8},{10,11... | collective-permute-start | bytes 1179656 | tf_op jit(solution)/shard_map/ppermute | solution.py:31
  118.4 2.2 %collective-permute-start.24 = (bf16[48,4096]{1,0:T(8,128)(2,1)S(1)}, bf16[48,4096]{1,0:T(8,128)(2,1)S(1)}, u32[]{:S(2)}, u32[]{:S(2)}) collective-permute-start(bf16[48,4096]{1,0:T(8,128)(2,1)S(1)} %collective-permute-done.13.refs_2_), channel_id=1, source_target_pairs={{0,1},{1,0},{2,3},{3,2},{4,5},{5,4},{6,7},{7,6},{8,9},{9,8},{10,11... | collective-permute-start | bytes 1179656 | tf_op jit(solution)/shard_map/ppermute | solution.py:31
  118.5 2.3 %collective-permute-start.23 = (bf16[48,4096]{1,0:T(8,128)(2,1)S(1)}, bf16[48,4096]{1,0:T(8,128)(2,1)S(1)}, u32[]{:S(2)}, u32[]{:S(2)}) collective-permute-start(bf16[48,4096]{1,0:T(8,128)(2,1)S(1)} %collective-permute-done.3.refs_0_), channel_id=1, source_target_pairs={{0,1},{1,0},{2,3},{3,2},{4,5},{5,4},{6,7},{7,6},{8,9},{9,8},{10,11... | collective-permute-start | bytes 1179656 | tf_op jit(solution)/shard_map/ppermute | solution.py:31
  119.0 2.3 %collective-permute-start.29 = (bf16[48,4096]{1,0:T(8,128)(2,1)S(1)}, bf16[48,4096]{1,0:T(8,128)(2,1)S(1)}, u32[]{:S(2)}, u32[]{:S(2)}) collective-permute-start(bf16[48,4096]{1,0:T(8,128)(2,1)S(1)} %collective-permute-done.28.refs_8_), channel_id=1, source_target_pairs={{0,1},{1,0},{2,3},{3,2},{4,5},{5,4},{6,7},{7,6},{8,9},{9,8},{10,11... | collective-permute-start | bytes 1179656 | tf_op jit(solution)/shard_map/ppermute | solution.py:31
  119.0 2.8 %collective-permute-start.30 = (bf16[48,4096]{1,0:T(8,128)(2,1)S(1)}, bf16[48,4096]{1,0:T(8,128)(2,1)S(1)}, u32[]{:S(2)}, u32[]{:S(2)}) collective-permute-start(bf16[48,4096]{1,0:T(8,128)(2,1)S(1)} %collective-permute-done.20.refs_10_), channel_id=1, source_target_pairs={{0,1},{1,0},{2,3},{3,2},{4,5},{5,4},{6,7},{7,6},{8,9},{9,8},{10,11... | collective-permute-start | bytes 1179656 | tf_op jit(solution)/shard_map/ppermute | solution.py:31
  119.5 12.3 %collective-permute-start.21 = (bf16[48,4096]{1,0:T(8,128)(2,1)S(1)}, bf16[48,4096]{1,0:T(8,128)(2,1)S(1)}, u32[]{:S(2)}, u32[]{:S(2)}) collective-permute-start(bf16[48,4096]{1,0:T(8,128)(2,1)S(1)} %collective-permute-done.20.refs_10_), channel_id=1, source_target_pairs={{0,12},{1,13},{2,14},{3,15},{4,0},{5,1},{6,2},{7,3},{8,4},{9,5},{1... | collective-permute-start | bytes 1179656 | tf_op jit(solution)/shard_map/ppermute | solution.py:31
  120.6 12.2 %collective-permute-start.19 = (bf16[48,4096]{1,0:T(8,128)(2,1)S(1)}, bf16[48,4096]{1,0:T(8,128)(2,1)S(1)}, u32[]{:S(2)}, u32[]{:S(2)}) collective-permute-start(bf16[48,4096]{1,0:T(8,128)(2,1)S(1)} %collective-permute-done.18.refs_0_), channel_id=1, source_target_pairs={{0,1},{1,0},{2,3},{3,2},{4,5},{5,4},{6,7},{7,6},{8,9},{9,8},{10,11... | collective-permute-start | bytes 1179656 | tf_op jit(solution)/shard_map/ppermute | solution.py:31
  131.8 1.7 %collective-permute-start.33 = (bf16[48,4096]{1,0:T(8,128)(2,1)S(1)}, bf16[48,4096]{1,0:T(8,128)(2,1)S(1)}, u32[]{:S(2)}, u32[]{:S(2)}) collective-permute-start(bf16[48,4096]{1,0:T(8,128)(2,1)S(1)} %collective-permute-done.21.refs_2_), channel_id=1, source_target_pairs={{0,1},{1,0},{2,3},{3,2},{4,5},{5,4},{6,7},{7,6},{8,9},{9,8},{10,11... | collective-permute-start | bytes 1179656 | tf_op jit(solution)/shard_map/ppermute | solution.py:31
